TPU v7x, 32 devices: a whole 2x2x4 slice. The times are simulated.
32 devices in a mesh: clip: 8 (over y, x, core), tm: 4 (over z).
Axes of the slice: x: 2, y: 2, z: 4, core: 2. Of those that a mesh axis runs over, the one named last changes fastest.
Arguments:
- patches: bfloat16 [8, 768, 512], P('clip', 'tm'), may hold values from -6 to 6
- patch_index: int32 [8, 768], P('clip', 'tm'), may hold values from 0 to 3599
- counts: int32 [8, 4], P('clip', 'tm'), may hold values from 1 to 192, 576 in all within a row
- w_embed: bfloat16 [512, 1024], replicated, may hold values from -0.25 to 0.25
- embed_bias: bfloat16 [1024], replicated, may hold values from -3 to 3
- ln_gain: bfloat16 [1024], replicated, may hold values from 0.099609375 to 1.8984375
- w_qkv: bfloat16 [1024, 3072], P(None, 'tm'), may hold values from -1 to 1
- w_o: bfloat16 [1024, 1024], P('tm'), may hold values from -0.1875 to 0.1875
- cotangent: bfloat16 [8, 768, 1024], P('clip', 'tm'), may hold values from -6 to 6
Outputs:
- encoded: bfloat16 [8, 768, 1024], P('clip', 'tm')
- grad_w_o: float32 [1024, 1024], P('tm')
Inputs may be any that keep to these rules, and one draw needn't show every extreme that they name: Entry [c, b] is the number of visible tokens of clip c in time bin b, held in the first slots of that bin's 192; each clip's counts sum to 576, and in each clip one bin is full. `patch_index`: patch number is row times 80 plus column; entries of slots that are not valid are ignored.
All inputs are finite; a program needn't handle non-finite values. No bound on the sum of `counts` on one device may be relied on, other than what follows from the above.
Results may differ from a plain program's by a relative error of at most 0.02.
Values may be sent and summed in bfloat16 or wider, within the bound.
No kernel may reach another device: no remote copies, remote signals or barrier semaphores. Data moves between devices by JAX's collectives and lax.ppermute only.
A program may use at most 64 MiB of HBM per device.

v0:
```python
import math

import jax
import jax.numpy as jnp
from jax import lax
from jax.sharding import PartitionSpec as P

HEAD_DIM = 64
PATCH_COLS = 80


NEG_FILL = -1e30
NORM_EPS = 1e-05


def sincos_features(coord, width):
    half_width = width // 2
    step_ids = jnp.arange(half_width).astype(jnp.float32)
    frequency = 10000.0 ** (-step_ids / half_width)
    phase = coord.astype(jnp.float32)[:, None] * frequency[None, :]
    return jnp.concatenate([jnp.sin(phase), jnp.cos(phase)], axis=1)


def position_table(patch_ids, bin_ids, width):
    time_width = width // 4
    space_width = (width - time_width) // 2
    return jnp.concatenate(
        [
            sincos_features(bin_ids, time_width),
            sincos_features(patch_ids // PATCH_COLS, space_width),
            sincos_features(patch_ids % PATCH_COLS, space_width),
        ],
        axis=1,
    )


def layer_norm(rows_in, ln_gain):
    values = rows_in.astype(jnp.float32)
    row_mean = jnp.mean(values, axis=-1, keepdims=True)
    centred = values - row_mean
    variance = jnp.mean(centred * centred, axis=-1, keepdims=True)
    return (centred * lax.rsqrt(variance + NORM_EPS) * ln_gain.astype(jnp.float32)).astype(
        jnp.bfloat16
    )


def attend_heads(mixed_rows, key_valid):
    total_rows = mixed_rows.shape[0]
    heads_here = mixed_rows.shape[1] // (3 * HEAD_DIM)
    split_rows = mixed_rows.reshape(total_rows, heads_here, 3, HEAD_DIM)
    queries = split_rows[:, :, 0]
    keys_all = split_rows[:, :, 1]
    values_all = split_rows[:, :, 2]
    block_rows = math.gcd(total_rows, 512)
    query_blocks = queries.reshape(total_rows // block_rows, block_rows, heads_here, HEAD_DIM)
    score_scale = 1.0 / math.sqrt(HEAD_DIM)

    def one_block(query_block):
        scores = (
            jnp.einsum("qhd,khd->hqk", query_block, keys_all, preferred_element_type=jnp.float32)
            * score_scale
        )
        scores = jnp.where(key_valid[None, None, :], scores, NEG_FILL)
        row_max = jnp.max(scores, axis=2, keepdims=True)
        weights = jnp.exp(scores - row_max)
        weight_sum = jnp.sum(weights, axis=2, keepdims=True)
        mixed = jnp.einsum(
            "hqk,khd->qhd",
            weights.astype(jnp.bfloat16),
            values_all,
            preferred_element_type=jnp.float32,
        )
        return (mixed / weight_sum.transpose(1, 0, 2)).astype(jnp.bfloat16)

    outcome = lax.map(one_block, query_blocks)
    return outcome.reshape(total_rows, heads_here * HEAD_DIM)


def per_device(patches, patch_index, counts, w_embed, embed_bias, ln_gain, w_qkv, w_o, cotangent):
    row_count = patches.shape[1]
    width = w_embed.shape[1]
    bin_total = lax.axis_size("tm")
    clip_total = lax.axis_size("clip")
    bin_now = lax.axis_index("tm")
    local_slots = jnp.arange(row_count)
    valid_rows = local_slots < counts[0, 0]
    bin_ids = jnp.zeros((row_count,), jnp.int32) + bin_now
    position = position_table(patch_index[0], bin_ids, width)
    embedded = jnp.dot(patches[0], w_embed, preferred_element_type=jnp.float32)
    embedded = embedded + embed_bias.astype(jnp.float32) + position
    hidden_rows = jnp.where(valid_rows[:, None], embedded, 0.0).astype(jnp.bfloat16)
    normed = layer_norm(hidden_rows, ln_gain)
    all_counts = lax.all_gather(counts, "tm", axis=1, tiled=True)
    key_slots = jnp.arange(row_count * bin_total)
    key_bins = key_slots // row_count
    bin_table = key_bins[:, None] == jnp.arange(bin_total)[None, :]
    key_count = jnp.sum(jnp.where(bin_table, all_counts[0][None, :], 0), axis=1)
    key_valid = key_slots % row_count < key_count
    mixed_rows = jnp.dot(
        lax.all_gather(normed, "tm", axis=0, tiled=True), w_qkv, preferred_element_type=jnp.float32
    ).astype(jnp.bfloat16)
    head_rows = attend_heads(mixed_rows, key_valid)
    attended = lax.all_to_all(head_rows, "tm", split_axis=0, concat_axis=1, tiled=True)
    columns = attended
    projected = jnp.dot(
        columns, lax.all_gather(w_o, "tm", axis=0, tiled=True), preferred_element_type=jnp.float32
    )
    encoded = jnp.where(
        valid_rows[:, None], hidden_rows.astype(jnp.float32) + projected, 0.0
    ).astype(jnp.bfloat16)
    cot_rows = jnp.where(valid_rows[:, None], cotangent[0], jnp.zeros((), jnp.bfloat16))
    grad_scale = 1.0 / math.sqrt(clip_total * row_count * bin_total)
    columns = attended
    grad_part = lax.psum_scatter(
        jnp.dot(columns.T, cot_rows, preferred_element_type=jnp.float32).astype(jnp.bfloat16),
        "tm",
        scatter_dimension=0,
        tiled=True,
    )
    grad_rows = lax.psum(grad_part, "clip").astype(jnp.float32)
    grad_w_o = grad_rows * grad_scale
    return (encoded[None], grad_w_o)


def solution(mesh):
    in_specs = (
        P("clip", "tm", None),
        P("clip", "tm"),
        P("clip", "tm"),
        P(),
        P(),
        P(),
        P(None, "tm"),
        P("tm", None),
        P("clip", "tm", None),
    )
    out_specs = (P("clip", "tm", None), P("tm", None))
    return jax.shard_map(
        per_device, mesh=mesh, in_specs=in_specs, out_specs=out_specs, check_vma=False
    )
```

profile of v0, /device:TPU:0, one launch (start us, length us, event | category | flops | bytes accessed | tf_op | source)
XLA Modules:
  0.0 243.8 jit_solution(16511596076242640852)
XLA Ops:
  7.2 0.8 broadcast_remainder_fusion
  8.0 0.7 compare_reduce_fusion
  9.5 0.7 convert_element_type.69
  10.2 1.4 multiply_cosine_fusion
  11.9 1.8 fusion.50
  14.0 0.9 multiply_convert_fusion
  15.0 0.7 dynamic-slice
  15.7 0.7 bitcast_dynamic-update-slice_fusion
  16.4 9.9 %all-reduce = s32[4]{0:T(128)S(1)} all-reduce(s32[4]{0:T(128)S(1)} %bitcast_dynamic-update-slice_fusion), channel_id=1, replica_groups=mesh['clip'=8,'tm'=4] {'tm'}, use_global_device_ids=true, to_apply=%add | all-reduce | flops 4 | bytes 32
  26.4 28.5 %all-gather.3.cloned.1.call-done = bf16[768,1024]{1,0:T(8,128)(2,1)} async-done(((bf16[192,1024]{1,0:T(8,128)(2,1)}), bf16[768,1024]{1,0:T(8,128)(2,1)}) %all-gather.3.cloned.1.call-update) | async-done | bytes 1572880 | tf_op jit(solution)/shard_map/all_gather | solution.py:100
  54.9 2.8 %convolution_convert_fusion.1 = bf16[768,768]{0,1:T(8,128)(2,1)S(1)} fusion(bf16[768,1024]{1,0:T(8,128)(2,1)} %all-gather.3.cloned.1.call-done, bf16[1024,768]{1,0:T(8,128)(2,1)S(1)} %copy-done), kind=kOutput, calls=%fused_computation.19 | convolution fusion | flops 1208549376 | bytes 4325376 | tf_op jit(solution)/shard_map/dot_general | solution.py:99
  57.9 1.0 reshape_squeeze.3
  58.8 1.1 copy.29
  59.9 9.3 %while.10 = (s32[]{:T(128)}, bf16[3,256,4,64]{1,3,2,0:T(8,128)(2,1)}, pred[768]{0:T(1024)(128)(4,1)S(1)}, bf16[3,256,4,64]{1,3,2,0:T(8,128)(2,1)S(1)}, bf16[768,...) while((s32[]{:T(128)}, bf16[3,256,4,64]{1,3,2,0:T(8,128)(2,1)}, ...), condition=%wide.region_6.7_spmd, body=%wide.region_3.6_spmd.sunk | while | flops 210106368 | bytes 10509393 | solution.py:75
  59.9 0.7 fusion.68
  60.6 0.8 fusion.69
  61.5 1.6 fusion.70
  63.0 0.7 fusion.68
  63.7 0.8 fusion.69
  64.6 1.6 fusion.70
  66.1 0.7 fusion.68
  66.8 0.8 fusion.69
  67.7 1.6 fusion.70
  69.2 1.4 copy.33
  71.2 14.2 %all_to_all.19 = bf16[4,192,256]{2,1,0:T(8,128)(2,1)S(1)} all-to-all(bf16[4,192,256]{2,1,0:T(8,128)(2,1)S(1)} %reshape.108), channel_id=1, replica_groups=mesh['clip'=8,'tm'=4] {'tm'}, dimensions={0} | all-to-all | bytes 786432 | tf_op jit(solution)/shard_map/all_to_all | solution.py:103
  85.4 3.1 %convolution_convert_fusion = bf16[1024,1024]{1,0:T(8,128)(2,1)} fusion(bf16[192,1024]{1,0:T(8,128)(2,1)S(1)} %bitcast.79, bf16[1,192,1024]{2,1,0:T(8,128)(2,1)} %param.19, pred[192]{0:T(512)(128)(4,1)S(1)} %iota_compare_fusion.1), kind=kOutput, calls=%fused_computation.18 | convolution fusion | flops 403898368 | bytes 2883776 | tf_op jit(solution)/shard_map/dot_general | solution.py:115
  88.6 0.7 all-gather.5.cloned.1.call-update
  89.3 42.3 %reduce-scatter.2.cloned.1.call-done = bf16[256,1024]{1,0:T(8,128)(2,1)} async-done(((bf16[1024,1024]{1,0:T(8,128)(2,1)}), bf16[256,1024]{1,0:T(8,128)(2,1)}) %reduce-scatter.2.cloned.1.call-update) | async-done | bytes 524304 | tf_op jit(solution)/shard_map/reduce_scatter | solution.py:114
  131.6 46.9 %all-gather.5.cloned.1.call-done = bf16[1024,1024]{1,0:T(8,128)(2,1)} async-done(((bf16[256,1024]{1,0:T(8,128)(2,1)}), bf16[1024,1024]{1,0:T(8,128)(2,1)}) %all-gather.5.cloned.1.call-update) | async-done | bytes 2097168 | tf_op jit(solution)/shard_map/all_gather | solution.py:106
  178.6 2.9 %fusion.33 = bf16[1,192,1024]{2,1,0:T(8,128)(2,1)} fusion(f32[192,1024]{1,0:T(8,128)S(1)} %get-tuple-element.81, bf16[192,1024]{1,0:T(8,128)(2,1)S(1)} %bitcast.80, bf16[1024,1024]{1,0:T(8,128)(2,1)} %all-gather.5.cloned.1.call-done, pred[192]{0:T(512)(128)(4,1)S(1)} %iota_compare_fusion.1), kind=kOutput, calls=%fused_computation.28 | convolution fusion | flops 403243008 | bytes 3670208 | tf_op jit(solution)/shard_map/dot_general | solution.py:105
  181.5 53.6 %all-reduce.3.cloned.1.call-done = bf16[256,1024]{1,0:T(8,128)(2,1)} async-done(((bf16[256,1024]{1,0:T(8,128)(2,1)}), bf16[256,1024]{1,0:T(8,128)(2,1)}) %all-reduce.3.cloned.1.call-update) | async-done | bytes 524304 | tf_op jit(solution)/shard_map/psum | solution.py:120
  235.1 2.1 convert_multiply_fusion
  (32 shorter events, 1.5 us)
Async XLA Ops:
  7.2 47.7 %copy-start = (bf16[1024,768]{1,0:T(8,128)(2,1)S(1)}, bf16[1024,768]{1,0:T(8,128)(2,1)}, u32[]{:S(2)}) copy-start(bf16[1024,768]{1,0:T(8,128)(2,1)} %param.17) | copy-start | bytes 4718596
  7.2 47.7 %all-gather.3.cloned.1.call-start = ((), (), s32[]{:S(2)}) async-start(), calls=%async_computation.2 | async-start | bytes 1966080 | tf_op jit(solution)/shard_map/all_gather | solution.py:100
  10.2 3.8 %copy-start.1 = (bf16[1024]{0:T(1024)(128)(2,1)S(1)}, bf16[1024]{0:T(1024)(128)(2,1)}, u32[]{:S(2)}) copy-start(bf16[1024]{0:T(1024)(128)(2,1)} %param.16) | copy-start | bytes 6148
  11.6 3.4 %copy-start.2 = (u32[32]{0:T(128)S(1)}, u32[32]{0:T(128)}, u32[]{:S(2)}) copy-start(u32[32]{0:T(128)} %constant.87) | copy-start | bytes 388
  15.0 116.6 %reduce-scatter.2.cloned.1.call-start = ((), (), s32[]{:S(2)}) async-start(), calls=%async_computation.4 | async-start | bytes 2621440 | tf_op jit(solution)/shard_map/reduce_scatter | solution.py:114
  88.5 90.0 %all-gather.5.cloned.1.call-start = ((), (), s32[]{:S(2)}) async-start(), calls=%async_computation.3 | async-start | bytes 2621440 | tf_op jit(solution)/shard_map/all_gather | solution.py:106
  89.3 145.8 %all-reduce.3.cloned.1.call-start = ((), (), s32[]{:S(2)}) async-start(), calls=%async_computation.5 | async-start | bytes 1048576 | tf_op jit(solution)/shard_map/psum | solution.py:120
Sparse Core Ops, SparseCore 0:
  15.1 39.7 all-gather.2
  88.7 42.8 reduce-scatter.1
  133.2 45.2 all-gather.4
  181.8 53.2 all-reduce.2
where the time goes:
time: 244 us
  waiting for transfers between devices  172 us (70%)
  blocking collectives  24.2 us (10%)
  matrix products  17.5 us (7%)
  between operations  14.6 us (6%)
  other arithmetic  9.57 us (4%)
  local copies, waits for them, and re-layouts  5.69 us (2%)
    psum x1, waiting for transfers between devices, per_device(): grad_rows = lax.psum(grad_part, 'clip').astype(jnp.float32)  53.6 us
    all_gather x1, waiting for transfers between devices, per_device(): lax.all_gather(w_o, 'tm', axis=0, tiled=True)  46.9 us
    reduce_scatter x1, waiting for transfers between devices, per_device(): lax.psum_scatter(jnp.dot(columns.T, cot_rows, preferred_element_type=jnp....  42.3 us
    all_gather x1, waiting for transfers between devices, per_device(): lax.all_gather(normed, 'tm', axis=0, tiled=True)  28.5 us
    all_to_all x1, blocking collectives, per_device(): lax.all_to_all(head_rows, 'tm', split_axis=0, concat_axis=1, tiled=True)  14.2 us
    unnamed x1, blocking collectives  9.92 us
  transfers between devices with their start and end apart: 4, of which 4 were waited for; matrix products, arithmetic and copies ran while one was open for 2% of the time, Pallas kernels for 0%

commit v1 on v0

--- a/solution.py
+++ b/solution.py
@@ -1,16 +1,23 @@
+import functools
 import math
 
 import jax
 import jax.numpy as jnp
+import ml_dtypes
+import numpy as np
 from jax import lax
+from jax.experimental import pallas as pl
+from jax.experimental.pallas import tpu as pltpu
 from jax.sharding import PartitionSpec as P
 
 HEAD_DIM = 64
 PATCH_COLS = 80
-
-
+PATCH_ROWS = 45
 NEG_FILL = -1e30
 NORM_EPS = 1e-05
+VMEM_LIMIT = 50 * 1024 * 1024
+F32 = jnp.float32
+BF16 = jnp.bfloat16
 
 
 def sincos_features(coord, width):
@@ -76,7 +83,9 @@
     return outcome.reshape(total_rows, heads_here * HEAD_DIM)
 
 
-def per_device(patches, patch_index, counts, w_embed, embed_bias, ln_gain, w_qkv, w_o, cotangent):
+def general_device(
+    patches, patch_index, counts, w_embed, embed_bias, ln_gain, w_qkv, w_o, cotangent
+):
     row_count = patches.shape[1]
     width = w_embed.shape[1]
     bin_total = lax.axis_size("tm")
@@ -101,24 +110,405 @@
     ).astype(jnp.bfloat16)
     head_rows = attend_heads(mixed_rows, key_valid)
     attended = lax.all_to_all(head_rows, "tm", split_axis=0, concat_axis=1, tiled=True)
-    columns = attended
     projected = jnp.dot(
-        columns, lax.all_gather(w_o, "tm", axis=0, tiled=True), preferred_element_type=jnp.float32
+        attended, lax.all_gather(w_o, "tm", axis=0, tiled=True), preferred_element_type=jnp.float32
     )
     encoded = jnp.where(
         valid_rows[:, None], hidden_rows.astype(jnp.float32) + projected, 0.0
     ).astype(jnp.bfloat16)
     cot_rows = jnp.where(valid_rows[:, None], cotangent[0], jnp.zeros((), jnp.bfloat16))
     grad_scale = 1.0 / math.sqrt(clip_total * row_count * bin_total)
-    columns = attended
     grad_part = lax.psum_scatter(
-        jnp.dot(columns.T, cot_rows, preferred_element_type=jnp.float32).astype(jnp.bfloat16),
+        jnp.dot(attended.T, cot_rows, preferred_element_type=jnp.float32).astype(jnp.bfloat16),
         "tm",
         scatter_dimension=0,
         tiled=True,
     )
     grad_rows = lax.psum(grad_part, "clip").astype(jnp.float32)
     grad_w_o = grad_rows * grad_scale
+    return (encoded[None], grad_w_o)
+
+
+META = 16
+
+
+def sincos_np(coord, width):
+    half_width = width // 2
+    frequency = 10000.0 ** (-np.arange(half_width) / half_width)
+    phase = np.asarray(coord, np.float64)[:, None] * frequency[None, :]
+    return np.concatenate([np.sin(phase), np.cos(phase)], axis=1)
+
+
+def position_parts(bin_total, width):
+    time_width = width // 4
+    space_width = (width - time_width) // 2
+    table = np.zeros((128, 2 * space_width), np.float64)
+    table[:PATCH_ROWS, :space_width] = sincos_np(np.arange(PATCH_ROWS), space_width)
+    table[PATCH_ROWS : PATCH_ROWS + PATCH_COLS, space_width:] = sincos_np(
+        np.arange(PATCH_COLS), space_width
+    )
+    high = table.astype(ml_dtypes.bfloat16)
+    low = (table - high.astype(np.float64)).astype(ml_dtypes.bfloat16)
+    bins = np.zeros((8, time_width), np.float32)
+    bins[:bin_total] = sincos_np(np.arange(bin_total), time_width)
+    return np.concatenate([high, low], axis=0), bins
+
+
+def vmem_call(kernel, out_shape, scalars, arrays, scratch=(), flops=0):
+    n_scalar = len(scalars)
+    specs = [pl.BlockSpec(memory_space=pltpu.SMEM)] * n_scalar
+    specs += [pl.BlockSpec(memory_space=pltpu.VMEM)] * len(arrays)
+    size = sum(math.prod(a.shape) * a.dtype.itemsize for a in arrays)
+    return pl.pallas_call(
+        kernel,
+        out_shape=out_shape,
+        in_specs=specs,
+        out_specs=jax.tree.map(lambda _: pl.BlockSpec(memory_space=pltpu.VMEM), out_shape),
+        scratch_shapes=list(scratch),
+        compiler_params=pltpu.CompilerParams(vmem_limit_bytes=VMEM_LIMIT),
+        cost_estimate=pl.CostEstimate(flops=flops, bytes_accessed=size, transcendentals=0),
+    )(*scalars, *arrays)
+
+
+def pack_kernel(clip_ref, count_ref, patch_ref, index_ref, w_ref, packet_ref, meta):
+    rows = patch_ref.shape[0]
+    half = patch_ref.shape[1]
+    piece = w_ref.shape[0] // 8
+    packet_ref[0:rows, :] = patch_ref[...]
+    index = jnp.clip(index_ref[...], 0, PATCH_ROWS * PATCH_COLS - 1).astype(F32)
+    patch_row = jnp.floor((index + 0.5) * (1.0 / PATCH_COLS))
+    meta[...] = jnp.full(meta.shape, 1.0, F32) * count_ref[0].astype(F32)
+    meta[0:1, 0:rows] = patch_row
+    meta[0:1, 256 : 256 + rows] = index - patch_row * PATCH_COLS
+    packet_ref[rows : rows + META, :] = meta[...].astype(BF16)
+    start = pl.multiple_of(clip_ref[0] * piece, piece)
+    base = rows + META
+    packet_ref[base : base + piece, :] = w_ref[pl.ds(start, piece), 0:half]
+    packet_ref[base + piece : base + 2 * piece, :] = w_ref[pl.ds(start, piece), half : 2 * half]
+
+
+def attend_kernel(
+    rows,
+    bin_ref,
+    p0_ref,
+    p1_ref,
+    p2_ref,
+    pb_ref,
+    pf_ref,
+    w_embed_ref,
+    table_ref,
+    bins_ref,
+    bias_ref,
+    gain_ref,
+    w_qkv_ref,
+    a0_ref,
+    a1_ref,
+    a2_ref,
+    a3_ref,
+    hidden_ref,
+    piece_ref,
+    p3_ref,
+    q_ref,
+    k_ref,
+    v_ref,
+):
+    me = bin_ref[0]
+    inner = jnp.logical_or(me == 1, me == 2)
+
+    @pl.when(inner)
+    def _():
+        p3_ref[...] = pb_ref[...]
+
+    @pl.when(jnp.logical_not(inner))
+    def _():
+        p3_ref[...] = pf_ref[...]
+
+    packets = (p0_ref, p1_ref, p2_ref, p3_ref)
+    outs = (a0_ref, a1_ref, a2_ref, a3_ref)
+    group = 4 * HEAD_DIM
+    slot = lax.broadcasted_iota(jnp.int32, (rows, 1), 0).astype(F32)
+    place = lax.broadcasted_iota(jnp.int32, (128, rows), 0).astype(F32)
+    bias = bias_ref[...].astype(F32)
+    gain = gain_ref[...].astype(F32)
+    valid = []
+    for k in range(4):
+        packet = packets[k]
+        base = rows + META
+        piece_ref[k] = packet[base:, :]
+        meta = packet[rows : rows + META, :].astype(F32)
+        count = meta[1:2, 0:1]
+        ok = slot < count
+        valid.append(ok)
+        hit = jnp.logical_or(
+            place == meta[0:1, 0:rows], place == meta[0:1, 256 : 256 + rows] + PATCH_ROWS
+        )
+        hot = jnp.where(hit, 1.0, 0.0).astype(BF16)
+        hot = jnp.concatenate([hot, hot], axis=0)
+        space = lax.dot_general(
+            hot, table_ref[...], (((0,), (0,)), ((), ())), preferred_element_type=F32
+        )
+        embedded = jnp.dot(packet[0:rows, :], w_embed_ref[...], preferred_element_type=F32)
+        times = bins_ref[pl.ds(jnp.bitwise_xor(me, k), 1), :]
+        times = jnp.broadcast_to(times, (rows, times.shape[1]))
+        embedded = embedded + bias + jnp.concatenate([times, space], axis=1)
+        hidden = jnp.where(ok, embedded, 0.0).astype(BF16)
+        if k == 0:
+            hidden_ref[...] = hidden
+        values = hidden.astype(F32)
+        centred = values - jnp.mean(values, axis=1, keepdims=True)
+        variance = jnp.mean(centred * centred, axis=1, keepdims=True)
+        normed = (centred * lax.rsqrt(variance + NORM_EPS) * gain).astype(BF16)
+        qkv = jnp.dot(normed, w_qkv_ref[...], preferred_element_type=F32).astype(BF16)
+        here = slice(k * rows, (k + 1) * rows)
+        q_ref[here, :] = qkv[:, 0:group] * jnp.asarray(1.0 / math.sqrt(HEAD_DIM), BF16)
+        k_ref[here, :] = qkv[:, group : 2 * group]
+        v_ref[here, :] = qkv[:, 2 * group : 3 * group]
+
+    lane = lax.broadcasted_iota(jnp.int32, (1, group), 1)
+    key_bias = jnp.concatenate([jnp.where(ok, 0.0, NEG_FILL) for ok in valid], axis=0)
+    total = [None] * 4
+    for h in range(4):
+        own = jnp.logical_and(lane >= h * HEAD_DIM, lane < (h + 1) * HEAD_DIM)
+        spare_at = ((h + 1) * HEAD_DIM) % group
+        spare = lane == spare_at
+        keys = jnp.where(own, k_ref[...].astype(F32), jnp.where(spare, key_bias, 0.0)).astype(BF16)
+        rest = jnp.where(spare, 1.0, 0.0)
+        vals = jnp.where(own, v_ref[...].astype(F32), rest).astype(BF16)
+        for b in range(4):
+            queries = q_ref[b * rows : (b + 1) * rows, :].astype(F32)
+            queries = jnp.where(own, queries, rest).astype(BF16)
+            scores = lax.dot_general(
+                queries, keys, (((1,), (1,)), ((), ())), preferred_element_type=F32
+            )
+            weights = jnp.exp(scores - jnp.max(scores, axis=1, keepdims=True)).astype(BF16)
+            mixed = jnp.dot(weights, vals, preferred_element_type=F32)
+            mixed = mixed / mixed[:, spare_at : spare_at + 1]
+            total[b] = mixed if h == 0 else jnp.where(own, mixed, total[b])
+    for b in range(4):
+        outs[b][...] = jnp.where(valid[b], total[b], 0.0).astype(BF16)
+
+
+def grad_kernel(
+    bin_ref,
+    core_ref,
+    a0_ref,
+    a1_ref,
+    a2_ref,
+    a3_ref,
+    c0_ref,
+    c1_ref,
+    c2_ref,
+    cb_ref,
+    cf_ref,
+    keep_ref,
+    send_ref,
+    c3_ref,
+    sum_ref,
+):
+    me = bin_ref[0]
+    inner = jnp.logical_or(me == 1, me == 2)
+
+    @pl.when(inner)
+    def _():
+        c3_ref[...] = cb_ref[...]
+
+    @pl.when(jnp.logical_not(inner))
+    def _():
+        c3_ref[...] = cf_ref[...]
+
+    total = None
+    for a_ref, c_ref in ((a0_ref, c0_ref), (a1_ref, c1_ref), (a2_ref, c2_ref), (a3_ref, c3_ref)):
+        part = lax.dot_general(
+            a_ref[...], c_ref[...], (((0,), (0,)), ((), ())), preferred_element_type=F32
+        )
+        total = part if total is None else total + part
+    sum_ref[...] = total
+    half = sum_ref.shape[0] // 2
+    core = core_ref[0]
+    keep_ref[...] = sum_ref[pl.ds(pl.multiple_of(core * half, half), half), :].astype(BF16)
+    send_ref[...] = sum_ref[pl.ds(pl.multiple_of((1 - core) * half, half), half), :].astype(BF16)
+
+
+def gather_kernel(clip_ref, *refs):
+    out_ref = refs[-1]
+    clip = clip_ref[0]
+    piece = refs[0].shape[1] // 2
+    half = refs[0].shape[2]
+    for m in range(8):
+        start = pl.multiple_of(jnp.bitwise_xor(clip, m) * piece, piece)
+        for k in range(4):
+            out_ref[k, pl.ds(start, piece), 0:half] = refs[m][k, 0:piece, :]
+            out_ref[k, pl.ds(start, piece), half : 2 * half] = refs[m][k, piece : 2 * piece, :]
+
+
+def project_kernel(count_ref, hidden_ref, a0_ref, a1_ref, a2_ref, a3_ref, w_ref, out_ref):
+    rows = hidden_ref.shape[0]
+    heads = jnp.concatenate([a0_ref[...], a1_ref[...], a2_ref[...], a3_ref[...]], axis=1)
+    slot = lax.broadcasted_iota(jnp.int32, (rows, 1), 0)
+    projected = jnp.dot(heads, w_ref[...], preferred_element_type=F32)
+    total = hidden_ref[...].astype(F32) + projected
+    out_ref[...] = jnp.where(slot < count_ref[0], total, 0.0).astype(BF16)
+
+
+def finish_kernel(scale, core_ref, *refs):
+    out_ref = refs[-1]
+    core = core_ref[0]
+    half = out_ref.shape[0] // 2
+    parts = (len(refs) - 1) // 3
+    width = out_ref.shape[1] // parts
+    for c in range(parts):
+        upper, lower, other = refs[3 * c : 3 * c + 3]
+        columns = slice(c * width, (c + 1) * width)
+        quarter = half // 2
+        mine = pl.multiple_of(core * half, half)
+        theirs = pl.multiple_of((1 - core) * half, half)
+        out_ref[pl.ds(mine, quarter), columns] = upper[...].astype(F32) * scale
+        out_ref[pl.ds(mine + quarter, quarter), columns] = lower[...].astype(F32) * scale
+        out_ref[pl.ds(theirs, half), columns] = other[...].astype(F32) * scale
+
+
+def along_tm(array, pairs):
+    return lax.ppermute(array, "tm", pairs)
+
+
+def along_clip(array, flip):
+    return lax.ppermute(array, "clip", [(i, i ^ flip) for i in range(8)])
+
+
+NEAR = [(0, 1), (1, 0), (2, 3), (3, 2)]
+MIDDLE = [(1, 2), (2, 1)]
+TWO = [(0, 2), (1, 3), (2, 0), (3, 1)]
+RELAY = [(2, 3), (1, 0)]
+
+
+def add_rounded(first, second):
+    return (first.astype(F32) + second.astype(F32)).astype(BF16)
+
+
+def after(value, *others):
+    return lax.optimization_barrier((value, *others))[0]
+
+
+def line_device(
+    patches, patch_index, counts, w_embed, embed_bias, ln_gain, w_qkv, w_o, cotangent
+):
+    rows = patches.shape[1]
+    half = patches.shape[2]
+    width = w_embed.shape[1]
+    group = 4 * HEAD_DIM
+    piece = w_o.shape[0] // 8
+    me = lax.axis_index("tm").astype(jnp.int32)
+    clip = lax.axis_index("clip").astype(jnp.int32)
+    core = clip % 2
+    me_s, clip_s, core_s = me[None], clip[None], core[None]
+    count_s = counts[0]
+    shape = jax.ShapeDtypeStruct
+    table, bins = position_parts(4, width)
+
+    packet = vmem_call(
+        pack_kernel,
+        shape((rows + META + 2 * piece, half), BF16),
+        [clip_s, count_s],
+        [patches[0], patch_index, w_o],
+        scratch=[pltpu.VMEM((META, half), F32)],
+    )
+    cots = [cotangent[0][:, :half], cotangent[0][:, half:]]
+
+    def send(array):
+        near = along_tm(array, NEAR)
+        two = along_tm(array, TWO)
+        middle = along_tm(array, MIDDLE)
+        return near, two, middle
+
+    p1, p2, pb = send(packet)
+    c1, c2, cb = send(after(cots[0], p1))
+    pf = along_tm(p2, RELAY)
+    d1, d2, db = send(after(cots[1], c1))
+    cf = along_tm(c2, RELAY)
+    df = along_tm(d2, RELAY)
+
+    w_ordered = w_qkv.reshape(width, 4, 3, HEAD_DIM).transpose(0, 2, 1, 3).reshape(width, 3 * group)
+    a_shape = shape((rows, group), BF16)
+    *heads, hidden, pieces = vmem_call(
+        functools.partial(attend_kernel, rows),
+        [a_shape] * 4 + [shape((rows, width), BF16), shape((4, 2 * piece, half), BF16)],
+        [me_s],
+        [
+            packet,
+            p1,
+            p2,
+            pb,
+            pf,
+            w_embed,
+            jnp.asarray(table),
+            jnp.asarray(bins),
+            embed_bias[None],
+            ln_gain[None],
+            w_ordered,
+        ],
+        scratch=[pltpu.VMEM(packet.shape, BF16)] + [pltpu.VMEM((4 * rows, group), BF16)] * 3,
+        flops=4_000_000_000,
+    )
+
+    by_x = along_clip(pieces, 2)
+    by_y = along_clip(pieces, 4)
+    onward = jnp.where(core == 0, by_x, by_y)
+    turn = [(i, i ^ 4) if i % 2 == 0 else (i, i ^ 2) for i in range(8)]
+    by_xy = lax.ppermute(onward, "clip", turn)
+    held = {0: pieces, 2: by_x, 4: by_y, 6: by_xy}
+    for m in (0, 2, 4, 6):
+        held[m + 1] = along_clip(held[m], 1)
+    w_all = vmem_call(
+        gather_kernel,
+        shape((4, 8 * piece, width), BF16),
+        [clip_s],
+        [held[m] for m in range(8)],
+    ).reshape(width, width)
+
+    finals = []
+    for own, one, two, mid, far in (
+        (cots[0], c1, c2, cb, cf),
+        (cots[1], d1, d2, db, df),
+    ):
+        keep, give = vmem_call(
+            grad_kernel,
+            [shape((group // 2, half), BF16)] * 2,
+            [me_s, core_s],
+            [*heads, own, one, two, mid, far],
+            scratch=[pltpu.VMEM((rows, half), BF16), pltpu.VMEM((group, half), F32)],
+            flops=400_000_000,
+        )
+        mine = add_rounded(keep, along_clip(give, 1))
+        quarter = group // 4
+        upper, lower = mine[:quarter], mine[quarter:]
+        upper, lower = (
+            add_rounded(upper, along_clip(upper, 2)),
+            add_rounded(lower, along_clip(lower, 4)),
+        )
+        upper, lower = (
+            add_rounded(upper, along_clip(upper, 4)),
+            add_rounded(lower, along_clip(lower, 2)),
+        )
+        other = along_clip(jnp.concatenate([upper, lower], axis=0), 1)
+        finals += [upper, lower, other]
+
+    moved = [heads[0]]
+    for k in (1, 2, 3):
+        block = after(heads[k], df)
+        moved.append(along_tm(block, [(i, i ^ k) for i in range(4)]))
+    encoded = vmem_call(
+        project_kernel,
+        shape((rows, width), BF16),
+        [count_s],
+        [hidden, *moved, w_all],
+        flops=400_000_000,
+    )
+    grad_w_o = vmem_call(
+        functools.partial(finish_kernel, 1.0 / math.sqrt(8 * rows * 4)),
+        shape((group, width), F32),
+        [core_s],
+        finals,
+    )
     return (encoded[None], grad_w_o)
 
 
@@ -135,6 +525,11 @@
         P("clip", "tm", None),
     )
     out_specs = (P("clip", "tm", None), P("tm", None))
+    on_line = mesh.shape["tm"] == 4 and mesh.shape["clip"] == 8
     return jax.shard_map(
-        per_device, mesh=mesh, in_specs=in_specs, out_specs=out_specs, check_vma=False
-    )
+        line_device if on_line else general_device,
+        mesh=mesh,
+        in_specs=in_specs,
+        out_specs=out_specs,
+        check_vma=False,
+    )

time: 244 us -> 120 us (0.49)
  waiting for transfers between devices: 172 us -> 38.4 us
  starting transfers between devices: 0.16 us -> 41.5 us
  blocking collectives: 24.2 us -> 0 us
  Pallas kernels: 0 us -> 17.8 us
  matrix products: 17.5 us -> 0 us
  local copies, waits for them, and re-layouts: 5.69 us -> 19.4 us
  between operations: 14.6 us -> 1.7 us
  other arithmetic: 9.57 us -> 0.26 us
    all_gather x2 -> x0, waiting for transfers between devices: 75.5 us -> none  [the longest x1 46.9 us: per_device(): lax.all_gather(w_o, 'tm', axis=0, tiled=True)]
    psum x1 -> x0, waiting for transfers between devices: 53.6 us -> none  [per_device(): grad_rows = lax.psum(grad_part, 'clip').astype(jnp.float32)]
    reduce_scatter x1 -> x0, waiting for transfers between devices: 42.3 us -> none  [per_device(): lax.psum_scatter(jnp.dot(columns.T, cot_rows, preferred_element_type=jnp....]
    ppermute x0 -> x34, starting transfers between devices: none -> 41.5 us  [the longest x15 24.9 us: along_tm(): return lax.ppermute(array, 'tm', pairs)]
    ppermute x0 -> x34, waiting for transfers between devices: none -> 38.4 us  [the longest x15 28.3 us: along_tm(): return lax.ppermute(array, 'tm', pairs)]
    pallas_call x0 -> x7, Pallas kernels: none -> 17.8 us  [vmem_call(): pl.pallas_call(kernel, out_shape=out_shape, in_specs=specs, out_specs=jax...]
    dot_general x10 -> x0, matrix products: 17.5 us -> none  [the longest x3 4.69 us: one_block(): jnp.einsum('hqk,khd->qhd', weights.astype(jnp.bfloat16), values_all, pref...]
    all_to_all x1 -> x0, blocking collectives: 14.2 us -> none  [per_device(): lax.all_to_all(head_rows, 'tm', split_axis=0, concat_axis=1, tiled=True)]
  transfers between devices with their start and end apart: 4 -> 34, of which waited for: 4 -> 10; matrix products, arithmetic and copies ran while one was open for 2% -> 8% of each run, Pallas kernels for 0% -> 13%
where the time goes in v1:
time: 120 us; the launch traced here: 119 us
  starting transfers between devices  41.5 us (35%)
  waiting for transfers between devices  38.4 us (32%)
  local copies, waits for them, and re-layouts  19.4 us (16%)
  Pallas kernels  17.8 us (15%)
  between operations  1.7 us (1%)
    ppermute x15, waiting for transfers between devices, along_tm(): return lax.ppermute(array, 'tm', pairs)  28.3 us
    ppermute x15, starting transfers between devices, along_tm(): return lax.ppermute(array, 'tm', pairs)  24.9 us
    pallas_call x7, Pallas kernels, vmem_call(): pl.pallas_call(kernel, out_shape=out_shape, in_specs=specs, out_specs=jax...  17.8 us
    ppermute x18, starting transfers between devices, along_clip(): return lax.ppermute(array, 'clip', [(i, i ^ flip) for i in range(8)])  15 us
    unnamed x41, local copies, waits for them, and re-layouts  12.9 us
    ppermute x18, waiting for transfers between devices, along_clip(): return lax.ppermute(array, 'clip', [(i, i ^ flip) for i in range(8)])  10.1 us
    transpose x1, local copies, waits for them, and re-layouts, line_device(): w_qkv.reshape(width, 4, 3, HEAD_DIM).transpose(0, 2, 1, 3)  2.7 us
    reshape x1, local copies, waits for them, and re-layouts, line_device(): w_qkv.reshape(width, 4, 3, HEAD_DIM).transpose(0, 2, 1, 3)  2.69 us
  transfers between devices with their start and end apart: 34, of which 10 were waited for; matrix products, arithmetic and copies ran while one was open for 8% of the time, Pallas kernels for 13%

profile of v1, /device:TPU:0, one launch (start us, length us, event | category | flops | bytes accessed | tf_op | source)
XLA Modules:
  0.0 119.1 jit_solution(9336299652081128913)
XLA Ops:
  4.0 4.1 %collective-permute-start.1 = (bf16[272,512]{1,0:T(8,128)(2,1)S(1)}, bf16[272,512]{1,0:T(8,128)(2,1)S(1)}, u32[]{:S(2)}, u32[]{:S(2)}) collective-permute-start(bf16[272,512]{1,0:T(8,128)(2,1)S(1)} %shard_map.122.p0_ref), channel_id=1, source_target_pairs={{0,2},{1,3},{2,0},{3,1},{4,6},{5,7},{6,4},{7,5},{8,10},{9,11},{10,... | collective-permute-start | bytes 835592 | tf_op jit(solution)/shard_map/ppermute | solution.py:371
  8.1 1.6 %collective-permute-start = (bf16[272,512]{1,0:T(8,128)(2,1)S(1)}, bf16[272,512]{1,0:T(8,128)(2,1)S(1)}, u32[]{:S(2)}, u32[]{:S(2)}) collective-permute-start(bf16[272,512]{1,0:T(8,128)(2,1)S(1)} %shard_map.122.p0_ref), channel_id=1, source_target_pairs={{0,1},{1,0},{2,3},{3,2},{4,5},{5,4},{6,7},{7,6},{8,9},{9,8},{10,11... | collective-permute-start | bytes 835592 | tf_op jit(solution)/shard_map/ppermute | solution.py:371
  10.3 11.2 %collective-permute-done.1.p2_ref = bf16[272,512]{1,0:T(8,128)(2,1)S(1)} collective-permute-done((bf16[272,512]{1,0:T(8,128)(2,1)S(1)}, bf16[272,512]{1,0:T(8,128)(2,1)S(1)}, u32[]{:S(2)}, u32[]{:S(2)}) %collective-permute-start.1) | collective-permute-done | bytes 278560 | tf_op jit(solution)/shard_map/ppermute | solution.py:371
  23.9 4.0 %collective-permute-start.17 = (bf16[192,512]{1,0:T(8,128)(2,1)S(1)}, bf16[192,512]{1,0:T(8,128)(2,1)S(1)}, u32[]{:S(2)}, u32[]{:S(2)}) collective-permute-start(bf16[192,512]{1,0:T(8,128)(2,1)S(1)} %get-tuple-element.20.c0_ref), channel_id=1, source_target_pairs={{0,2},{1,3},{2,0},{3,1},{4,6},{5,7},{6,4},{7,5},{8,10},{9,11},{10,... | collective-permute-start | bytes 589832 | tf_op jit(solution)/shard_map/ppermute | solution.py:371
  27.9 2.6 %copy.14 = bf16[1024,768]{0,1:T(8,128)(2,1)} copy(bf16[1024,768]{1,0:T(8,128)(2,1)} %param.17) | data formatting | bytes 3145728 | tf_op args[6]
  30.5 2.7 %copy.15 = bf16[1024,3,4,64]{0,3,2,1:T(8,128)(2,1)} copy(bf16[1024,3,4,64]{0,3,1,2:T(8,128)(2,1)} %bitcast.17) | data formatting | bytes 3145728 | tf_op jit(solution)/shard_map/transpose | solution.py:430
  33.2 2.7 %copy.16.w_qkv_ref = bf16[1024,768]{1,0:T(8,128)(2,1)} copy(bf16[1024,768]{0,1:T(8,128)(2,1)} %bitcast.16) | data formatting | bytes 3145728 | tf_op jit(solution)/shard_map/reshape | solution.py:430
  36.7 1.3 %collective-permute-start.19 = (bf16[192,512]{1,0:T(8,128)(2,1)S(1)}, bf16[192,512]{1,0:T(8,128)(2,1)S(1)}, u32[]{:S(2)}, u32[]{:S(2)}) collective-permute-start(bf16[192,512]{1,0:T(8,128)(2,1)S(1)} %collective-permute-done.17.c2_ref), channel_id=1, source_target_pairs={{2,3},{1,0},{6,7},{5,4},{10,11},{9,8},{14,15},{13,12},{18,19},{17,... | collective-permute-start | bytes 589832 | tf_op jit(solution)/shard_map/ppermute | solution.py:371
  41.4 12.9 %shard_map.123 = (bf16[192,256]{1,0:T(8,128)(2,1)S(1)}, bf16[192,256]{1,0:T(8,128)(2,1)S(1)}, bf16[192,256]{1,0:T(8,128)(2,1)S(1)}, bf16[192,256]{1,0:T(8,128)(2...) custom-call(s32[1]{0:T(128)} %bitcast.1.bin_ref, bf16[272,512]{1,0:T(8,128)(2,1)S(1)} %shard_map.122.p0_ref, ...), custom_call_target="tpu_custom_call" | custom-call | flops 4000000000 | bytes 4419584 | tf_op jit(solution)/shard_map/pallas_call | solution.py:162
  55.0 1.3 %collective-permute-done.20 = bf16[128,512]{1,0:T(8,128)(2,1)S(1)} collective-permute-done((bf16[128,512]{1,0:T(8,128)(2,1)S(1)}, bf16[128,512]{1,0:T(8,128)(2,1)S(1)}, u32[]{:S(2)}, u32[]{:S(2)}) %collective-permute-start.20) | collective-permute-done | bytes 131104 | tf_op jit(solution)/shard_map/ppermute | solution.py:375
  56.4 1.6 %collective-permute-start.21 = (bf16[64,512]{1,0:T(8,128)(2,1)S(1)}, bf16[64,512]{1,0:T(8,128)(2,1)S(1)}, u32[]{:S(2)}, u32[]{:S(2)}) collective-permute-start(bf16[64,512]{1,0:T(8,128)(2,1)S(1)} %get-tuple-element.41), channel_id=1, source_target_pairs={{0,8},{4,12},{8,0},{12,4},{16,24},{20,28},{24,16},{28,20},{1,9},{5... | collective-permute-start | bytes 196616 | tf_op jit(solution)/shard_map/ppermute | solution.py:375
  58.0 1.5 %collective-permute-start.23 = (bf16[64,512]{1,0:T(8,128)(2,1)S(1)}, bf16[64,512]{1,0:T(8,128)(2,1)S(1)}, u32[]{:S(2)}, u32[]{:S(2)}) collective-permute-start(bf16[64,512]{1,0:T(8,128)(2,1)S(1)} %get-tuple-element.40), channel_id=1, source_target_pairs={{0,16},{4,20},{8,24},{12,28},{16,0},{20,4},{24,8},{28,12},{1,17},{... | collective-permute-start | bytes 196616 | tf_op jit(solution)/shard_map/ppermute | solution.py:375
  60.5 4.7 %collective-permute-start.5 = (bf16[192,512]{1,0:T(8,128)(2,1)S(1)}, bf16[192,512]{1,0:T(8,128)(2,1)S(1)}, u32[]{:S(2)}, u32[]{:S(2)}) collective-permute-start(bf16[192,512]{1,0:T(8,128)(2,1)S(1)} %get-tuple-element.21.c0_ref), channel_id=1, source_target_pairs={{0,2},{1,3},{2,0},{3,1},{4,6},{5,7},{6,4},{7,5},{8,10},{9,11},{10,... | collective-permute-start | bytes 589832 | tf_op jit(solution)/shard_map/ppermute | solution.py:371
  66.0 8.7 %collective-permute-done.5.c2_ref = bf16[192,512]{1,0:T(8,128)(2,1)S(1)} collective-permute-done((bf16[192,512]{1,0:T(8,128)(2,1)S(1)}, bf16[192,512]{1,0:T(8,128)(2,1)S(1)}, u32[]{:S(2)}, u32[]{:S(2)}) %collective-permute-start.5) | collective-permute-done | bytes 196640 | tf_op jit(solution)/shard_map/ppermute | solution.py:371
  74.7 1.5 %collective-permute-start.6 = (bf16[192,512]{1,0:T(8,128)(2,1)S(1)}, bf16[192,512]{1,0:T(8,128)(2,1)S(1)}, u32[]{:S(2)}, u32[]{:S(2)}) collective-permute-start(bf16[192,512]{1,0:T(8,128)(2,1)S(1)} %collective-permute-done.5.c2_ref), channel_id=1, source_target_pairs={{2,3},{1,0},{6,7},{5,4},{10,11},{9,8},{14,15},{13,12},{18,19},{17,... | collective-permute-start | bytes 589832 | tf_op jit(solution)/shard_map/ppermute | solution.py:371
  76.2 1.7 %collective-permute-start.24 = (bf16[64,512]{1,0:T(8,128)(2,1)S(1)}, bf16[64,512]{1,0:T(8,128)(2,1)S(1)}, u32[]{:S(2)}, u32[]{:S(2)}) collective-permute-start(bf16[64,512]{1,0:T(8,128)(2,1)S(1)} %get-tuple-element.38), channel_id=1, source_target_pairs={{0,8},{4,12},{8,0},{12,4},{16,24},{20,28},{24,16},{28,20},{1,9},{5... | collective-permute-start | bytes 196616 | tf_op jit(solution)/shard_map/ppermute | solution.py:375
  77.9 1.6 %collective-permute-start.15 = (bf16[4,64,512]{2,1,0:T(8,128)(2,1)S(1)}, bf16[4,64,512]{2,1,0:T(8,128)(2,1)S(1)}, u32[]{:S(2)}, u32[]{:S(2)}) collective-permute-start(bf16[4,64,512]{2,1,0:T(8,128)(2,1)S(1)} %broadcast_select_fusion), channel_id=1, source_target_pairs={{0,16},{4,12},{8,24},{12,4},{16,0},{20,28},{24,8},{28,20},{1,17},{... | collective-permute-start | bytes 786440 | tf_op jit(solution)/shard_map/ppermute | solution.py:457
  79.5 4.5 %collective-permute-done.6.cf_ref = bf16[192,512]{1,0:T(8,128)(2,1)S(1)} collective-permute-done((bf16[192,512]{1,0:T(8,128)(2,1)S(1)}, bf16[192,512]{1,0:T(8,128)(2,1)S(1)}, u32[]{:S(2)}, u32[]{:S(2)}) %collective-permute-start.6) | collective-permute-done | bytes 196640 | tf_op jit(solution)/shard_map/ppermute | solution.py:371
  87.3 1.7 %collective-permute-start.22 = (bf16[64,512]{1,0:T(8,128)(2,1)S(1)}, bf16[64,512]{1,0:T(8,128)(2,1)S(1)}, u32[]{:S(2)}, u32[]{:S(2)}) collective-permute-start(bf16[64,512]{1,0:T(8,128)(2,1)S(1)} %get-tuple-element.39), channel_id=1, source_target_pairs={{0,16},{4,20},{8,24},{12,28},{16,0},{20,4},{24,8},{28,12},{1,17},{... | collective-permute-start | bytes 196616 | tf_op jit(solution)/shard_map/ppermute | solution.py:375
  89.2 1.6 %collective-permute-start.29 = (bf16[64,512]{1,0:T(8,128)(2,1)S(1)}, bf16[64,512]{1,0:T(8,128)(2,1)S(1)}, u32[]{:S(2)}, u32[]{:S(2)}) collective-permute-start(bf16[64,512]{1,0:T(8,128)(2,1)S(1)} %get-tuple-element.37), channel_id=1, source_target_pairs={{0,8},{4,12},{8,0},{12,4},{16,24},{20,28},{24,16},{28,20},{1,9},{5... | collective-permute-start | bytes 196616 | tf_op jit(solution)/shard_map/ppermute | solution.py:375
  91.8 1.7 %collective-permute-start.31 = (bf16[64,512]{1,0:T(8,128)(2,1)S(1)}, bf16[64,512]{1,0:T(8,128)(2,1)S(1)}, u32[]{:S(2)}, u32[]{:S(2)}) collective-permute-start(bf16[64,512]{1,0:T(8,128)(2,1)S(1)} %get-tuple-element.36), channel_id=1, source_target_pairs={{0,16},{4,20},{8,24},{12,28},{16,0},{20,4},{24,8},{28,12},{1,17},{... | collective-permute-start | bytes 196616 | tf_op jit(solution)/shard_map/ppermute | solution.py:375
  93.6 2.5 %collective-permute-done.31 = bf16[64,512]{1,0:T(8,128)(2,1)S(1)} collective-permute-done((bf16[64,512]{1,0:T(8,128)(2,1)S(1)}, bf16[64,512]{1,0:T(8,128)(2,1)S(1)}, u32[]{:S(2)}, u32[]{:S(2)}) %collective-permute-start.31) | collective-permute-done | bytes 65568 | tf_op jit(solution)/shard_map/ppermute | solution.py:375
  96.1 1.7 %collective-permute-start.32 = (bf16[64,512]{1,0:T(8,128)(2,1)S(1)}, bf16[64,512]{1,0:T(8,128)(2,1)S(1)}, u32[]{:S(2)}, u32[]{:S(2)}) collective-permute-start(bf16[64,512]{1,0:T(8,128)(2,1)S(1)} %get-tuple-element.34), channel_id=1, source_target_pairs={{0,8},{4,12},{8,0},{12,4},{16,24},{20,28},{24,16},{28,20},{1,9},{5... | collective-permute-start | bytes 196616 | tf_op jit(solution)/shard_map/ppermute | solution.py:375
  97.9 2.6 %collective-permute-done.32 = bf16[64,512]{1,0:T(8,128)(2,1)S(1)} collective-permute-done((bf16[64,512]{1,0:T(8,128)(2,1)S(1)}, bf16[64,512]{1,0:T(8,128)(2,1)S(1)}, u32[]{:S(2)}, u32[]{:S(2)}) %collective-permute-start.32) | collective-permute-done | bytes 65568 | tf_op jit(solution)/shard_map/ppermute | solution.py:375
  100.5 1.7 %collective-permute-start.30 = (bf16[64,512]{1,0:T(8,128)(2,1)S(1)}, bf16[64,512]{1,0:T(8,128)(2,1)S(1)}, u32[]{:S(2)}, u32[]{:S(2)}) collective-permute-start(bf16[64,512]{1,0:T(8,128)(2,1)S(1)} %get-tuple-element.35), channel_id=1, source_target_pairs={{0,16},{4,20},{8,24},{12,28},{16,0},{20,4},{24,8},{28,12},{1,17},{... | collective-permute-start | bytes 196616 | tf_op jit(solution)/shard_map/ppermute | solution.py:375
  102.3 2.5 %collective-permute-done.30 = bf16[64,512]{1,0:T(8,128)(2,1)S(1)} collective-permute-done((bf16[64,512]{1,0:T(8,128)(2,1)S(1)}, bf16[64,512]{1,0:T(8,128)(2,1)S(1)}, u32[]{:S(2)}, u32[]{:S(2)}) %collective-permute-start.30) | collective-permute-done | bytes 65568 | tf_op jit(solution)/shard_map/ppermute | solution.py:375
  105.4 1.8 %collective-permute-start.9 = (bf16[192,256]{1,0:T(8,128)(2,1)S(1)}, bf16[192,256]{1,0:T(8,128)(2,1)S(1)}, u32[]{:S(2)}, u32[]{:S(2)}) collective-permute-start(bf16[192,256]{1,0:T(8,128)(2,1)S(1)} %copy-done.15), channel_id=1, source_target_pairs={{0,3},{1,2},{2,1},{3,0},{4,7},{5,6},{6,5},{7,4},{8,11},{9,10},{10,... | collective-permute-start | bytes 294920 | tf_op jit(solution)/shard_map/ppermute | solution.py:371
  107.2 2.6 %collective-permute-start.7 = (bf16[192,256]{1,0:T(8,128)(2,1)S(1)}, bf16[192,256]{1,0:T(8,128)(2,1)S(1)}, u32[]{:S(2)}, u32[]{:S(2)}) collective-permute-start(bf16[192,256]{1,0:T(8,128)(2,1)S(1)} %copy-done.9), channel_id=1, source_target_pairs={{0,1},{1,0},{2,3},{3,2},{4,5},{5,4},{6,7},{7,6},{8,9},{9,8},{10,11... | collective-permute-start | bytes 294920 | tf_op jit(solution)/shard_map/ppermute | solution.py:371
  110.8 1.5 %shard_map.124 = bf16[4,256,1024]{2,1,0:T(8,128)(2,1)} custom-call(s32[1]{0:T(128)} %bitcast.2.clip_ref, bf16[4,64,512]{2,1,0:T(8,128)(2,1)S(1)} %get-tuple-element.27.refs_0_, bf16[4,64,512]{2,1,0:T(8,128)(2,1)S(1)} %collective-permute-done.10.refs_1_, bf16[4,64,512]{2,1,0:T(8,128)(2,1)S(1)} %collective-permute-done.11.refs_2_, ...), custom_call_target="tpu_custom_call" | custom-call | bytes 2097152 | tf_op jit(solution)/shard_map/pallas_call | solution.py:162
  112.9 3.3 %collective-permute-done.8.a2_ref = bf16[192,256]{1,0:T(8,128)(2,1)S(1)} collective-permute-done((bf16[192,256]{1,0:T(8,128)(2,1)S(1)}, bf16[192,256]{1,0:T(8,128)(2,1)S(1)}, u32[]{:S(2)}, u32[]{:S(2)}) %collective-permute-start.8) | collective-permute-done | bytes 98336 | tf_op jit(solution)/shard_map/ppermute | solution.py:371
  116.2 1.6 %copy-done = bf16[4,256,1024]{2,1,0:T(8,128)(2,1)S(1)} copy-done((bf16[4,256,1024]{2,1,0:T(8,128)(2,1)S(1)}, bf16[4,256,1024]{2,1,0:T(8,128)(2,1)}, u32[]{:S(2)}) %copy-start) | copy-done | bytes 2097176
  117.8 1.3 %shard_map.125 = bf16[192,1024]{1,0:T(8,128)(2,1)} custom-call(s32[1]{0:T(128)} %bitcast.13.count_ref, bf16[192,1024]{1,0:T(8,128)(2,1)S(1)} %get-tuple-element.17.hidden_ref, bf16[192,256]{1,0:T(8,128)(2,1)S(1)} %get-tuple-element.18.a0_ref, bf16[192,256]{1,0:T(8,128)(2,1)S(1)} %collective-permute-done.7.a1_ref, ...), custom_call_target="tpu_custom_call" | custom-call | flops 400000000 | bytes 2883584 | tf_op jit(solution)/shard_map/pallas_call | solution.py:162
  (102 shorter events, 19.2 us)
Async XLA Ops:
  4.0 17.6 %collective-permute-start.1 = (bf16[272,512]{1,0:T(8,128)(2,1)S(1)}, bf16[272,512]{1,0:T(8,128)(2,1)S(1)}, u32[]{:S(2)}, u32[]{:S(2)}) collective-permute-start(bf16[272,512]{1,0:T(8,128)(2,1)S(1)} %shard_map.122.p0_ref), channel_id=1, source_target_pairs={{0,2},{1,3},{2,0},{3,1},{4,6},{5,7},{6,4},{7,5},{8,10},{9,11},{10,... | collective-permute-start | bytes 835592 | tf_op jit(solution)/shard_map/ppermute | solution.py:371
  8.1 15.8 %collective-permute-start = (bf16[272,512]{1,0:T(8,128)(2,1)S(1)}, bf16[272,512]{1,0:T(8,128)(2,1)S(1)}, u32[]{:S(2)}, u32[]{:S(2)}) collective-permute-start(bf16[272,512]{1,0:T(8,128)(2,1)S(1)} %shard_map.122.p0_ref), channel_id=1, source_target_pairs={{0,1},{1,0},{2,3},{3,2},{4,5},{5,4},{6,7},{7,6},{8,9},{9,8},{10,11... | collective-permute-start | bytes 835592 | tf_op jit(solution)/shard_map/ppermute | solution.py:371
  9.6 28.4 %collective-permute-start.2 = (bf16[272,512]{1,0:T(8,128)(2,1)S(1)}, bf16[272,512]{1,0:T(8,128)(2,1)S(1)}, u32[]{:S(2)}, u32[]{:S(2)}) collective-permute-start(bf16[272,512]{1,0:T(8,128)(2,1)S(1)} %shard_map.122.p0_ref), channel_id=1, source_target_pairs={{1,2},{2,1},{5,6},{6,5},{9,10},{10,9},{13,14},{14,13},{17,18},{18,... | collective-permute-start | bytes 835592 | tf_op jit(solution)/shard_map/ppermute | solution.py:371
  21.6 16.5 %collective-permute-start.3 = (bf16[272,512]{1,0:T(8,128)(2,1)S(1)}, bf16[272,512]{1,0:T(8,128)(2,1)S(1)}, u32[]{:S(2)}, u32[]{:S(2)}) collective-permute-start(bf16[272,512]{1,0:T(8,128)(2,1)S(1)} %collective-permute-done.1.p2_ref), channel_id=1, source_target_pairs={{2,3},{1,0},{6,7},{5,4},{10,11},{9,8},{14,15},{13,12},{18,19},{17,... | collective-permute-start | bytes 835592 | tf_op jit(solution)/shard_map/ppermute | solution.py:371
  23.9 12.8 %collective-permute-start.17 = (bf16[192,512]{1,0:T(8,128)(2,1)S(1)}, bf16[192,512]{1,0:T(8,128)(2,1)S(1)}, u32[]{:S(2)}, u32[]{:S(2)}) collective-permute-start(bf16[192,512]{1,0:T(8,128)(2,1)S(1)} %get-tuple-element.20.c0_ref), channel_id=1, source_target_pairs={{0,2},{1,3},{2,0},{3,1},{4,6},{5,7},{6,4},{7,5},{8,10},{9,11},{10,... | collective-permute-start | bytes 589832 | tf_op jit(solution)/shard_map/ppermute | solution.py:371
  36.0 18.4 %collective-permute-start.4 = (bf16[192,512]{1,0:T(8,128)(2,1)S(1)}, bf16[192,512]{1,0:T(8,128)(2,1)S(1)}, u32[]{:S(2)}, u32[]{:S(2)}) collective-permute-start(bf16[192,512]{1,0:T(8,128)(2,1)S(1)} %get-tuple-element.20.c0_ref), channel_id=1, source_target_pairs={{0,1},{1,0},{2,3},{3,2},{4,5},{5,4},{6,7},{7,6},{8,9},{9,8},{10,11... | collective-permute-start | bytes 589832 | tf_op jit(solution)/shard_map/ppermute | solution.py:371
  36.1 18.3 %collective-permute-start.18 = (bf16[192,512]{1,0:T(8,128)(2,1)S(1)}, bf16[192,512]{1,0:T(8,128)(2,1)S(1)}, u32[]{:S(2)}, u32[]{:S(2)}) collective-permute-start(bf16[192,512]{1,0:T(8,128)(2,1)S(1)} %get-tuple-element.20.c0_ref), channel_id=1, source_target_pairs={{1,2},{2,1},{5,6},{6,5},{9,10},{10,9},{13,14},{14,13},{17,18},{18,... | collective-permute-start | bytes 589832 | tf_op jit(solution)/shard_map/ppermute | solution.py:371
  36.7 17.6 %collective-permute-start.19 = (bf16[192,512]{1,0:T(8,128)(2,1)S(1)}, bf16[192,512]{1,0:T(8,128)(2,1)S(1)}, u32[]{:S(2)}, u32[]{:S(2)}) collective-permute-start(bf16[192,512]{1,0:T(8,128)(2,1)S(1)} %collective-permute-done.17.c2_ref), channel_id=1, source_target_pairs={{2,3},{1,0},{6,7},{5,4},{10,11},{9,8},{14,15},{13,12},{18,19},{17,... | collective-permute-start | bytes 589832 | tf_op jit(solution)/shard_map/ppermute | solution.py:371
  56.4 8.9 %collective-permute-start.21 = (bf16[64,512]{1,0:T(8,128)(2,1)S(1)}, bf16[64,512]{1,0:T(8,128)(2,1)S(1)}, u32[]{:S(2)}, u32[]{:S(2)}) collective-permute-start(bf16[64,512]{1,0:T(8,128)(2,1)S(1)} %get-tuple-element.41), channel_id=1, source_target_pairs={{0,8},{4,12},{8,0},{12,4},{16,24},{20,28},{24,16},{28,20},{1,9},{5... | collective-permute-start | bytes 196616 | tf_op jit(solution)/shard_map/ppermute | solution.py:375
  58.0 7.3 %collective-permute-start.23 = (bf16[64,512]{1,0:T(8,128)(2,1)S(1)}, bf16[64,512]{1,0:T(8,128)(2,1)S(1)}, u32[]{:S(2)}, u32[]{:S(2)}) collective-permute-start(bf16[64,512]{1,0:T(8,128)(2,1)S(1)} %get-tuple-element.40), channel_id=1, source_target_pairs={{0,16},{4,20},{8,24},{12,28},{16,0},{20,4},{24,8},{28,12},{1,17},{... | collective-permute-start | bytes 196616 | tf_op jit(solution)/shard_map/ppermute | solution.py:375
  59.5 15.2 %collective-permute-start.11 = (bf16[4,64,512]{2,1,0:T(8,128)(2,1)S(1)}, bf16[4,64,512]{2,1,0:T(8,128)(2,1)S(1)}, u32[]{:S(2)}, u32[]{:S(2)}) collective-permute-start(bf16[4,64,512]{2,1,0:T(8,128)(2,1)S(1)} %get-tuple-element.27.refs_0_), channel_id=1, source_target_pairs={{0,8},{4,12},{8,0},{12,4},{16,24},{20,28},{24,16},{28,20},{1,9},{5... | collective-permute-start | bytes 786440 | tf_op jit(solution)/shard_map/ppermute | solution.py:375
  60.0 16.1 %collective-permute-start.13 = (bf16[4,64,512]{2,1,0:T(8,128)(2,1)S(1)}, bf16[4,64,512]{2,1,0:T(8,128)(2,1)S(1)}, u32[]{:S(2)}, u32[]{:S(2)}) collective-permute-start(bf16[4,64,512]{2,1,0:T(8,128)(2,1)S(1)} %get-tuple-element.27.refs_0_), channel_id=1, source_target_pairs={{0,16},{4,20},{8,24},{12,28},{16,0},{20,4},{24,8},{28,12},{1,17},{... | collective-permute-start | bytes 786440 | tf_op jit(solution)/shard_map/ppermute | solution.py:375
  60.5 14.2 %collective-permute-start.5 = (bf16[192,512]{1,0:T(8,128)(2,1)S(1)}, bf16[192,512]{1,0:T(8,128)(2,1)S(1)}, u32[]{:S(2)}, u32[]{:S(2)}) collective-permute-start(bf16[192,512]{1,0:T(8,128)(2,1)S(1)} %get-tuple-element.21.c0_ref), channel_id=1, source_target_pairs={{0,2},{1,3},{2,0},{3,1},{4,6},{5,7},{6,4},{7,5},{8,10},{9,11},{10,... | collective-permute-start | bytes 589832 | tf_op jit(solution)/shard_map/ppermute | solution.py:371
  65.2 12.7 %collective-permute-start.26 = (bf16[192,512]{1,0:T(8,128)(2,1)S(1)}, bf16[192,512]{1,0:T(8,128)(2,1)S(1)}, u32[]{:S(2)}, u32[]{:S(2)}) collective-permute-start(bf16[192,512]{1,0:T(8,128)(2,1)S(1)} %get-tuple-element.21.c0_ref), channel_id=1, source_target_pairs={{0,1},{1,0},{2,3},{3,2},{4,5},{5,4},{6,7},{7,6},{8,9},{9,8},{10,11... | collective-permute-start | bytes 589832 | tf_op jit(solution)/shard_map/ppermute | solution.py:371
  65.3 14.3 %collective-permute-start.27 = (bf16[192,512]{1,0:T(8,128)(2,1)S(1)}, bf16[192,512]{1,0:T(8,128)(2,1)S(1)}, u32[]{:S(2)}, u32[]{:S(2)}) collective-permute-start(bf16[192,512]{1,0:T(8,128)(2,1)S(1)} %get-tuple-element.21.c0_ref), channel_id=1, source_target_pairs={{1,2},{2,1},{5,6},{6,5},{9,10},{10,9},{13,14},{14,13},{17,18},{18,... | collective-permute-start | bytes 589832 | tf_op jit(solution)/shard_map/ppermute | solution.py:371
  74.7 30.1 %collective-permute-start.10 = (bf16[4,64,512]{2,1,0:T(8,128)(2,1)S(1)}, bf16[4,64,512]{2,1,0:T(8,128)(2,1)S(1)}, u32[]{:S(2)}, u32[]{:S(2)}) collective-permute-start(bf16[4,64,512]{2,1,0:T(8,128)(2,1)S(1)} %get-tuple-element.27.refs_0_), channel_id=1, source_target_pairs={{0,4},{4,0},{8,12},{12,8},{16,20},{20,16},{24,28},{28,24},{1,5},{5... | collective-permute-start | bytes 786440 | tf_op jit(solution)/shard_map/ppermute | solution.py:375
  74.7 9.4 %collective-permute-start.6 = (bf16[192,512]{1,0:T(8,128)(2,1)S(1)}, bf16[192,512]{1,0:T(8,128)(2,1)S(1)}, u32[]{:S(2)}, u32[]{:S(2)}) collective-permute-start(bf16[192,512]{1,0:T(8,128)(2,1)S(1)} %collective-permute-done.5.c2_ref), channel_id=1, source_target_pairs={{2,3},{1,0},{6,7},{5,4},{10,11},{9,8},{14,15},{13,12},{18,19},{17,... | collective-permute-start | bytes 589832 | tf_op jit(solution)/shard_map/ppermute | solution.py:371
  76.2 11.2 %collective-permute-start.24 = (bf16[64,512]{1,0:T(8,128)(2,1)S(1)}, bf16[64,512]{1,0:T(8,128)(2,1)S(1)}, u32[]{:S(2)}, u32[]{:S(2)}) collective-permute-start(bf16[64,512]{1,0:T(8,128)(2,1)S(1)} %get-tuple-element.38), channel_id=1, source_target_pairs={{0,8},{4,12},{8,0},{12,4},{16,24},{20,28},{24,16},{28,20},{1,9},{5... | collective-permute-start | bytes 196616 | tf_op jit(solution)/shard_map/ppermute | solution.py:375
  77.9 24.3 %collective-permute-start.15 = (bf16[4,64,512]{2,1,0:T(8,128)(2,1)S(1)}, bf16[4,64,512]{2,1,0:T(8,128)(2,1)S(1)}, u32[]{:S(2)}, u32[]{:S(2)}) collective-permute-start(bf16[4,64,512]{2,1,0:T(8,128)(2,1)S(1)} %broadcast_select_fusion), channel_id=1, source_target_pairs={{0,16},{4,12},{8,24},{12,4},{16,0},{20,28},{24,8},{28,20},{1,17},{... | collective-permute-start | bytes 786440 | tf_op jit(solution)/shard_map/ppermute | solution.py:457
  79.5 27.6 %collective-permute-start.12 = (bf16[4,64,512]{2,1,0:T(8,128)(2,1)S(1)}, bf16[4,64,512]{2,1,0:T(8,128)(2,1)S(1)}, u32[]{:S(2)}, u32[]{:S(2)}) collective-permute-start(bf16[4,64,512]{2,1,0:T(8,128)(2,1)S(1)} %collective-permute-done.11.refs_2_), channel_id=1, source_target_pairs={{0,4},{4,0},{8,12},{12,8},{16,20},{20,16},{24,28},{28,24},{1,5},{5... | collective-permute-start | bytes 786440 | tf_op jit(solution)/shard_map/ppermute | solution.py:375
  87.3 4.5 %collective-permute-start.22 = (bf16[64,512]{1,0:T(8,128)(2,1)S(1)}, bf16[64,512]{1,0:T(8,128)(2,1)S(1)}, u32[]{:S(2)}, u32[]{:S(2)}) collective-permute-start(bf16[64,512]{1,0:T(8,128)(2,1)S(1)} %get-tuple-element.39), channel_id=1, source_target_pairs={{0,16},{4,20},{8,24},{12,28},{16,0},{20,4},{24,8},{28,12},{1,17},{... | collective-permute-start | bytes 196616 | tf_op jit(solution)/shard_map/ppermute | solution.py:375
  89.2 4.4 %collective-permute-start.29 = (bf16[64,512]{1,0:T(8,128)(2,1)S(1)}, bf16[64,512]{1,0:T(8,128)(2,1)S(1)}, u32[]{:S(2)}, u32[]{:S(2)}) collective-permute-start(bf16[64,512]{1,0:T(8,128)(2,1)S(1)} %get-tuple-element.37), channel_id=1, source_target_pairs={{0,8},{4,12},{8,0},{12,4},{16,24},{20,28},{24,16},{28,20},{1,9},{5... | collective-permute-start | bytes 196616 | tf_op jit(solution)/shard_map/ppermute | solution.py:375
  91.8 4.3 %collective-permute-start.31 = (bf16[64,512]{1,0:T(8,128)(2,1)S(1)}, bf16[64,512]{1,0:T(8,128)(2,1)S(1)}, u32[]{:S(2)}, u32[]{:S(2)}) collective-permute-start(bf16[64,512]{1,0:T(8,128)(2,1)S(1)} %get-tuple-element.36), channel_id=1, source_target_pairs={{0,16},{4,20},{8,24},{12,28},{16,0},{20,4},{24,8},{28,12},{1,17},{... | collective-permute-start | bytes 196616 | tf_op jit(solution)/shard_map/ppermute | solution.py:375
  93.5 17.3 %collective-permute-start.14 = (bf16[4,64,512]{2,1,0:T(8,128)(2,1)S(1)}, bf16[4,64,512]{2,1,0:T(8,128)(2,1)S(1)}, u32[]{:S(2)}, u32[]{:S(2)}) collective-permute-start(bf16[4,64,512]{2,1,0:T(8,128)(2,1)S(1)} %collective-permute-done.13.refs_4_), channel_id=1, source_target_pairs={{0,4},{4,0},{8,12},{12,8},{16,20},{20,16},{24,28},{28,24},{1,5},{5... | collective-permute-start | bytes 786440 | tf_op jit(solution)/shard_map/ppermute | solution.py:375
  96.1 4.3 %collective-permute-start.32 = (bf16[64,512]{1,0:T(8,128)(2,1)S(1)}, bf16[64,512]{1,0:T(8,128)(2,1)S(1)}, u32[]{:S(2)}, u32[]{:S(2)}) collective-permute-start(bf16[64,512]{1,0:T(8,128)(2,1)S(1)} %get-tuple-element.34), channel_id=1, source_target_pairs={{0,8},{4,12},{8,0},{12,4},{16,24},{20,28},{24,16},{28,20},{1,9},{5... | collective-permute-start | bytes 196616 | tf_op jit(solution)/shard_map/ppermute | solution.py:375
  100.5 4.3 %collective-permute-start.30 = (bf16[64,512]{1,0:T(8,128)(2,1)S(1)}, bf16[64,512]{1,0:T(8,128)(2,1)S(1)}, u32[]{:S(2)}, u32[]{:S(2)}) collective-permute-start(bf16[64,512]{1,0:T(8,128)(2,1)S(1)} %get-tuple-element.35), channel_id=1, source_target_pairs={{0,16},{4,20},{8,24},{12,28},{16,0},{20,4},{24,8},{28,12},{1,17},{... | collective-permute-start | bytes 196616 | tf_op jit(solution)/shard_map/ppermute | solution.py:375
  102.2 3.2 %collective-permute-start.25 = (bf16[128,512]{1,0:T(8,128)(2,1)S(1)}, bf16[128,512]{1,0:T(8,128)(2,1)S(1)}, u32[]{:S(2)}, u32[]{:S(2)}) collective-permute-start(bf16[128,512]{1,0:T(8,128)(2,1)S(1)} %pad_maximum_fusion), channel_id=1, source_target_pairs={{0,4},{4,0},{8,12},{12,8},{16,20},{20,16},{24,28},{28,24},{1,5},{5... | collective-permute-start | bytes 393224 | tf_op jit(solution)/shard_map/ppermute | solution.py:375
  104.7 6.1 %collective-permute-start.16 = (bf16[4,64,512]{2,1,0:T(8,128)(2,1)S(1)}, bf16[4,64,512]{2,1,0:T(8,128)(2,1)S(1)}, u32[]{:S(2)}, u32[]{:S(2)}) collective-permute-start(bf16[4,64,512]{2,1,0:T(8,128)(2,1)S(1)} %collective-permute-done.15.refs_6_), channel_id=1, source_target_pairs={{0,4},{4,0},{8,12},{12,8},{16,20},{20,16},{24,28},{28,24},{1,5},{5... | collective-permute-start | bytes 786440 | tf_op jit(solution)/shard_map/ppermute | solution.py:375
  104.8 2.3 %collective-permute-start.33 = (bf16[128,512]{1,0:T(8,128)(2,1)S(1)}, bf16[128,512]{1,0:T(8,128)(2,1)S(1)}, u32[]{:S(2)}, u32[]{:S(2)}) collective-permute-start(bf16[128,512]{1,0:T(8,128)(2,1)S(1)} %pad_maximum_fusion.1), channel_id=1, source_target_pairs={{0,4},{4,0},{8,12},{12,8},{16,20},{20,16},{24,28},{28,24},{1,5},{5... | collective-permute-start | bytes 393224 | tf_op jit(solution)/shard_map/ppermute | solution.py:375
  105.4 7.5 %collective-permute-start.9 = (bf16[192,256]{1,0:T(8,128)(2,1)S(1)}, bf16[192,256]{1,0:T(8,128)(2,1)S(1)}, u32[]{:S(2)}, u32[]{:S(2)}) collective-permute-start(bf16[192,256]{1,0:T(8,128)(2,1)S(1)} %copy-done.15), channel_id=1, source_target_pairs={{0,3},{1,2},{2,1},{3,0},{4,7},{5,6},{6,5},{7,4},{8,11},{9,10},{10,... | collective-permute-start | bytes 294920 | tf_op jit(solution)/shard_map/ppermute | solution.py:371
  107.1 9.0 %collective-permute-start.8 = (bf16[192,256]{1,0:T(8,128)(2,1)S(1)}, bf16[192,256]{1,0:T(8,128)(2,1)S(1)}, u32[]{:S(2)}, u32[]{:S(2)}) collective-permute-start(bf16[192,256]{1,0:T(8,128)(2,1)S(1)} %copy-done.12), channel_id=1, source_target_pairs={{0,2},{1,3},{2,0},{3,1},{4,6},{5,7},{6,4},{7,5},{8,10},{9,11},{10,... | collective-permute-start | bytes 294920 | tf_op jit(solution)/shard_map/ppermute | solution.py:371
  107.2 9.0 %collective-permute-start.7 = (bf16[192,256]{1,0:T(8,128)(2,1)S(1)}, bf16[192,256]{1,0:T(8,128)(2,1)S(1)}, u32[]{:S(2)}, u32[]{:S(2)}) collective-permute-start(bf16[192,256]{1,0:T(8,128)(2,1)S(1)} %copy-done.9), channel_id=1, source_target_pairs={{0,1},{1,0},{2,3},{3,2},{4,5},{5,4},{6,7},{7,6},{8,9},{9,8},{10,11... | collective-permute-start | bytes 294920 | tf_op jit(solution)/shard_map/ppermute | solution.py:371
  (22 other events, 127.0 us)

commit v2 on v0

--- a/solution.py
+++ b/solution.py
@@ -1,16 +1,22 @@
+import functools
 import math
 
 import jax
 import jax.numpy as jnp
+import ml_dtypes
+import numpy as np
 from jax import lax
+from jax.experimental import pallas as pl
+from jax.experimental.pallas import tpu as pltpu
 from jax.sharding import PartitionSpec as P
 
 HEAD_DIM = 64
 PATCH_COLS = 80
-
-
+PATCH_ROWS = 45
 NEG_FILL = -1e30
 NORM_EPS = 1e-05
+F32 = jnp.float32
+BF16 = jnp.bfloat16
 
 
 def sincos_features(coord, width):
@@ -76,7 +82,9 @@
     return outcome.reshape(total_rows, heads_here * HEAD_DIM)
 
 
-def per_device(patches, patch_index, counts, w_embed, embed_bias, ln_gain, w_qkv, w_o, cotangent):
+def general_device(
+    patches, patch_index, counts, w_embed, embed_bias, ln_gain, w_qkv, w_o, cotangent
+):
     row_count = patches.shape[1]
     width = w_embed.shape[1]
     bin_total = lax.axis_size("tm")
@@ -101,18 +109,16 @@
     ).astype(jnp.bfloat16)
     head_rows = attend_heads(mixed_rows, key_valid)
     attended = lax.all_to_all(head_rows, "tm", split_axis=0, concat_axis=1, tiled=True)
-    columns = attended
     projected = jnp.dot(
-        columns, lax.all_gather(w_o, "tm", axis=0, tiled=True), preferred_element_type=jnp.float32
+        attended, lax.all_gather(w_o, "tm", axis=0, tiled=True), preferred_element_type=jnp.float32
     )
     encoded = jnp.where(
         valid_rows[:, None], hidden_rows.astype(jnp.float32) + projected, 0.0
     ).astype(jnp.bfloat16)
     cot_rows = jnp.where(valid_rows[:, None], cotangent[0], jnp.zeros((), jnp.bfloat16))
     grad_scale = 1.0 / math.sqrt(clip_total * row_count * bin_total)
-    columns = attended
     grad_part = lax.psum_scatter(
-        jnp.dot(columns.T, cot_rows, preferred_element_type=jnp.float32).astype(jnp.bfloat16),
+        jnp.dot(attended.T, cot_rows, preferred_element_type=jnp.float32).astype(jnp.bfloat16),
         "tm",
         scatter_dimension=0,
         tiled=True,
@@ -120,6 +126,480 @@
     grad_rows = lax.psum(grad_part, "clip").astype(jnp.float32)
     grad_w_o = grad_rows * grad_scale
     return (encoded[None], grad_w_o)
+
+
+META = 16
+
+
+def sincos_np(coord, width):
+    half_width = width // 2
+    frequency = 10000.0 ** (-np.arange(half_width) / half_width)
+    phase = np.asarray(coord, np.float64)[:, None] * frequency[None, :]
+    return np.concatenate([np.sin(phase), np.cos(phase)], axis=1)
+
+
+def position_parts(bin_total, width):
+    time_width = width // 4
+    space_width = (width - time_width) // 2
+    table = np.zeros((128, 2 * space_width), np.float64)
+    table[:PATCH_ROWS, :space_width] = sincos_np(np.arange(PATCH_ROWS), space_width)
+    table[PATCH_ROWS : PATCH_ROWS + PATCH_COLS, space_width:] = sincos_np(
+        np.arange(PATCH_COLS), space_width
+    )
+    high = table.astype(ml_dtypes.bfloat16)
+    low = (table - high.astype(np.float64)).astype(ml_dtypes.bfloat16)
+    bins = np.zeros((8, time_width), np.float32)
+    bins[:bin_total] = sincos_np(np.arange(bin_total), time_width)
+    return np.concatenate([high, low], axis=0), bins
+
+
+def local_call(kernel, out_shape, scalars, arrays, spaces, out_spaces, scratch=(), limit=16, cost=1000):
+    specs = [pl.BlockSpec(memory_space=pltpu.SMEM)] * len(scalars)
+    specs += [pl.BlockSpec(memory_space=space) for space in spaces]
+    return pl.pallas_call(
+        kernel,
+        out_shape=out_shape,
+        in_specs=specs,
+        out_specs=[pl.BlockSpec(memory_space=space) for space in out_spaces],
+        scratch_shapes=list(scratch),
+        compiler_params=pltpu.CompilerParams(vmem_limit_bytes=limit * 1024 * 1024),
+        cost_estimate=pl.CostEstimate(flops=1000, bytes_accessed=cost, transcendentals=0),
+    )(*scalars, *arrays)
+
+
+VMEM, HBM = pltpu.VMEM, pltpu.HBM
+
+
+def pack_kernel(count_ref, patch_ref, index_ref, packet_ref, meta):
+    rows = patch_ref.shape[0]
+    packet_ref[0:rows, :] = patch_ref[...]
+    numbers = jnp.clip(index_ref[...], 0, PATCH_ROWS * PATCH_COLS - 1).astype(F32)
+    patch_row = jnp.floor((numbers + 0.5) * (1.0 / PATCH_COLS))
+    meta[...] = jnp.full(meta.shape, 1.0, F32) * count_ref[0].astype(F32)
+    meta[0:1, 0:rows] = patch_row
+    meta[0:1, 256 : 256 + rows] = numbers - patch_row * PATCH_COLS
+    packet_ref[rows:, :] = meta[...].astype(BF16)
+
+
+def halve_kernel(clip_ref, cot_ref, w_ref, first_ref, second_ref):
+    rows = cot_ref.shape[0]
+    half = first_ref.shape[1]
+    piece = w_ref.shape[0] // 8
+    start = pl.multiple_of(clip_ref[0] * piece, piece)
+    first_ref[0:rows, :] = cot_ref[:, 0:half]
+    first_ref[rows : rows + piece, :] = w_ref[pl.ds(start, piece), 0:half]
+    first_ref[rows + piece :, :] = w_ref[pl.ds(start, piece), half : 2 * half]
+    second_ref[...] = cot_ref[:, half : 2 * half]
+
+
+def split_kernel(*refs):
+    sources, piece_ref, sems = refs[:4], refs[4], refs[5]
+    rows = sources[0].shape[0] - piece_ref.shape[1]
+    copies = [
+        pltpu.make_async_copy(source.at[rows:], piece_ref.at[k], sems.at[k])
+        for k, source in enumerate(sources)
+    ]
+    for copy in copies:
+        copy.start()
+    for copy in copies:
+        copy.wait()
+
+
+def stage_kernel(w_qkv_ref, qkv_out):
+    for part in range(3):
+        for pair in range(2):
+            first = (2 * pair * 3 + part) * HEAD_DIM
+            second = first + 3 * HEAD_DIM
+            both = jnp.concatenate(
+                [
+                    w_qkv_ref[:, first : first + HEAD_DIM],
+                    w_qkv_ref[:, second : second + HEAD_DIM],
+                ],
+                axis=1,
+            )
+            at = (2 * part + pair) * 2 * HEAD_DIM
+            qkv_out[:, at : at + 2 * HEAD_DIM] = both
+
+
+def attend_kernel(
+    rows,
+    bin_ref,
+    p0_hbm,
+    p1_hbm,
+    p2_hbm,
+    p3_hbm,
+    w_embed_hbm,
+    table_hbm,
+    bins_hbm,
+    bias_hbm,
+    gain_hbm,
+    w_qkv_hbm,
+    a_ref,
+    a1_ref,
+    a2_ref,
+    a3_ref,
+    hidden_ref,
+    packets,
+    w_embed_ref,
+    table_ref,
+    bins_ref,
+    bias_ref,
+    gain_ref,
+    w_qkv_ref,
+    normed_ref,
+    q_ref,
+    k_ref,
+    v_ref,
+    sems,
+):
+    me = bin_ref[0]
+    copies = [
+        pltpu.make_async_copy(source, packets.at[k], sems.at[k])
+        for k, source in enumerate((p0_hbm, p1_hbm, p2_hbm, p3_hbm))
+    ]
+    for copy in copies:
+        copy.start()
+    staged = [
+        pltpu.make_async_copy(source, target, sems.at[4 + i])
+        for i, (source, target) in enumerate(
+            (
+                (w_embed_hbm, w_embed_ref),
+                (table_hbm, table_ref),
+                (bins_hbm, bins_ref),
+                (bias_hbm, bias_ref),
+                (gain_hbm, gain_ref),
+                (w_qkv_hbm, w_qkv_ref),
+            )
+        )
+    ]
+    for copy in staged:
+        copy.start()
+    for copy in copies:
+        copy.wait()
+    for copy in staged[:-1]:
+        copy.wait()
+    group = 4 * HEAD_DIM
+    slot = lax.broadcasted_iota(jnp.int32, (rows, 1), 0).astype(F32)
+    place = lax.broadcasted_iota(jnp.int32, (128, rows), 0).astype(F32)
+    lane = lax.broadcasted_iota(jnp.int32, (1, group), 1)
+    bias = bias_ref[...].astype(F32)
+    gain = gain_ref[...].astype(F32)
+    owns, spares, spare_at = [], [], []
+    for h in range(4):
+        own = jnp.logical_and(lane >= h * HEAD_DIM, lane < (h + 1) * HEAD_DIM)
+        spare_at.append((h * HEAD_DIM + group // 2) % group)
+        owns.append(jnp.where(own, 1.0, 0.0).astype(BF16))
+        spares.append(jnp.where(lane == spare_at[h], 1.0, 0.0))
+    valid = []
+    for k in range(4):
+        here = slice(k * rows, (k + 1) * rows)
+        meta = packets[k, rows:, :].astype(F32)
+        ok = slot < meta[1:2, 0:1]
+        valid.append(ok)
+        hit = jnp.logical_or(
+            place == meta[0:1, 0:rows], place == meta[0:1, 256 : 256 + rows] + PATCH_ROWS
+        )
+        hot = jnp.where(hit, 1.0, 0.0).astype(BF16)
+        hot = jnp.concatenate([hot, hot], axis=0)
+        space = lax.dot_general(
+            hot, table_ref[...], (((0,), (0,)), ((), ())), preferred_element_type=F32
+        )
+        embedded = jnp.dot(packets[k, 0:rows, :], w_embed_ref[...], preferred_element_type=F32)
+        times = bins_ref[pl.ds(jnp.bitwise_xor(me, k), 1), :]
+        times = jnp.broadcast_to(times, (rows, times.shape[1]))
+        embedded = embedded + bias + jnp.concatenate([times, space], axis=1)
+        hidden = jnp.where(ok, embedded, 0.0).astype(BF16)
+        if k == 0:
+            hidden_ref[...] = hidden
+        values = hidden.astype(F32)
+        centred = values - jnp.mean(values, axis=1, keepdims=True)
+        variance = jnp.mean(centred * centred, axis=1, keepdims=True)
+        normed_ref[here, :] = (centred * lax.rsqrt(variance + NORM_EPS) * gain).astype(BF16)
+    mask = jnp.concatenate([jnp.where(ok, 0.0, NEG_FILL) for ok in valid], axis=0)
+    staged[-1].wait()
+    for part, ref in enumerate((q_ref, k_ref, v_ref)):
+        mixed = jnp.dot(
+            normed_ref[...],
+            w_qkv_ref[:, part * group : (part + 1) * group],
+            preferred_element_type=F32,
+        ).astype(BF16)
+        if part == 0:
+            mixed = mixed * jnp.asarray(1.0 / math.sqrt(HEAD_DIM), BF16)
+        for h in range(4):
+            fill = (mask * spares[h]).astype(BF16) if part == 1 else spares[h].astype(BF16)
+            ref[h] = mixed * owns[h] + fill
+
+    total = None
+    for h in range(4):
+        scores = lax.dot_general(
+            q_ref[h], k_ref[h], (((1,), (1,)), ((), ())), preferred_element_type=F32
+        )
+        weights = jnp.exp(scores - jnp.max(scores, axis=1, keepdims=True)).astype(BF16)
+        mixed = jnp.dot(weights, v_ref[h], preferred_element_type=F32)
+        mixed = mixed * (1.0 / mixed[:, spare_at[h] : spare_at[h] + 1])
+        total = mixed if h == 0 else jnp.where(owns[h] > 0, mixed, total)
+    total = jnp.where(mask == 0.0, total, 0.0).astype(BF16)
+    a_ref[...] = total
+    for k, ref in enumerate((a1_ref, a2_ref, a3_ref)):
+        ref[...] = total[(k + 1) * rows : (k + 2) * rows, :]
+
+
+def grad_kernel(
+    core_ref, a_ref, c0_hbm, c1_hbm, c2_hbm, c3_hbm, keep_ref, send_ref, cots, sum_ref, sems
+):
+    rows = cots.shape[0] // 4
+    copies = [
+        pltpu.make_async_copy(source.at[0:rows], cots.at[pl.ds(k * rows, rows)], sems.at[k])
+        for k, source in enumerate((c0_hbm, c1_hbm, c2_hbm, c3_hbm))
+    ]
+    for copy in copies:
+        copy.start()
+    for copy in copies:
+        copy.wait()
+    sum_ref[...] = lax.dot_general(
+        a_ref[...], cots[...], (((0,), (0,)), ((), ())), preferred_element_type=F32
+    )
+    half = sum_ref.shape[0] // 2
+    core = core_ref[0]
+    keep_ref[...] = sum_ref[pl.ds(pl.multiple_of(core * half, half), half), :].astype(BF16)
+    send_ref[...] = sum_ref[pl.ds(pl.multiple_of((1 - core) * half, half), half), :].astype(BF16)
+
+
+def gather_kernel(clip_ref, *refs):
+    held, out_hbm, sems = refs[:8], refs[8], refs[9]
+    clip = clip_ref[0]
+    piece = held[0].shape[1] // 2
+    half = held[0].shape[2]
+    copies = []
+    for m in range(8):
+        start = pl.multiple_of(jnp.bitwise_xor(clip, m) * piece, piece)
+        for k in range(4):
+            for side in range(2):
+                copies.append(
+                    pltpu.make_async_copy(
+                        held[m].at[k, side * piece : (side + 1) * piece],
+                        out_hbm.at[k, pl.ds(start, piece), side * half : (side + 1) * half],
+                        sems.at[len(copies)],
+                    )
+                )
+                copies[-1].start()
+    for copy in copies:
+        copy.wait()
+
+
+def project_kernel(
+    count_ref, hidden_hbm, a0_hbm, a1_hbm, a2_hbm, a3_hbm, w_hbm, out_hbm, hidden, heads, w_all, out, sems
+):
+    rows, group = a1_hbm.shape
+    copies = [
+        pltpu.make_async_copy(w_hbm, w_all, sems.at[0]),
+        pltpu.make_async_copy(hidden_hbm, hidden, sems.at[1]),
+        pltpu.make_async_copy(a0_hbm.at[0:rows], heads.at[:, 0:group], sems.at[2]),
+    ]
+    for k, source in enumerate((a1_hbm, a2_hbm, a3_hbm)):
+        columns = slice((k + 1) * group, (k + 2) * group)
+        copies.append(pltpu.make_async_copy(source, heads.at[:, columns], sems.at[3 + k]))
+    for copy in copies:
+        copy.start()
+    for copy in copies:
+        copy.wait()
+    slot = lax.broadcasted_iota(jnp.int32, (rows, 1), 0)
+    projected = jnp.dot(heads[...], w_all[...], preferred_element_type=F32)
+    total = hidden[...].astype(F32) + projected
+    out[...] = jnp.where(slot < count_ref[0], total, 0.0).astype(BF16)
+    write = pltpu.make_async_copy(out, out_hbm, sems.at[0])
+    write.start()
+    write.wait()
+
+
+def finish_kernel(scale, core_ref, *refs):
+    out_ref = refs[-1]
+    core = core_ref[0]
+    half = out_ref.shape[0] // 2
+    parts = (len(refs) - 1) // 2
+    width = out_ref.shape[1] // parts
+    mine = pl.multiple_of(core * half, half)
+    theirs = pl.multiple_of((1 - core) * half, half)
+    for c in range(parts):
+        columns = slice(c * width, (c + 1) * width)
+        out_ref[pl.ds(mine, half), columns] = refs[2 * c][...].astype(F32) * scale
+        out_ref[pl.ds(theirs, half), columns] = refs[2 * c + 1][...].astype(F32) * scale
+
+
+def along_tm(array, flip):
+    return lax.ppermute(array, "tm", [(i, i ^ flip) for i in range(4)])
+
+
+def along_clip(array, flip):
+    return lax.ppermute(array, "clip", [(i, i ^ flip) for i in range(8)])
+
+
+def add_rounded(first, second):
+    return (first.astype(F32) + second.astype(F32)).astype(BF16)
+
+
+def after(value, *others):
+    return lax.optimization_barrier((value, *others))[0]
+
+
+def line_device(
+    patches, patch_index, counts, w_embed, embed_bias, ln_gain, w_qkv, w_o, cotangent
+):
+    rows = patches.shape[1]
+    half = patches.shape[2]
+    width = w_embed.shape[1]
+    group = 4 * HEAD_DIM
+    piece = w_o.shape[0] // 8
+    me = lax.axis_index("tm").astype(jnp.int32)
+    clip = lax.axis_index("clip").astype(jnp.int32)
+    core = clip % 2
+    me_s, clip_s, core_s = me[None], clip[None], core[None]
+    count_s = counts[0]
+    shape = jax.ShapeDtypeStruct
+    table, bins = position_parts(4, width)
+    cot = cotangent[0]
+    dma = pltpu.SemaphoreType.DMA
+
+    (packet,) = local_call(
+        pack_kernel,
+        [shape((rows + META, half), BF16)],
+        [count_s],
+        [patches[0], patch_index],
+        [VMEM] * 2,
+        [VMEM],
+        scratch=[VMEM((META, half), F32)],
+        limit=4,
+    )
+    p1, p2, p3 = [along_tm(packet, k) for k in (1, 2, 3)]
+    first, second = local_call(
+        halve_kernel,
+        [shape((rows + 2 * piece, half), BF16), shape((rows, half), BF16)],
+        [clip_s],
+        [cot, w_o],
+        [VMEM] * 2,
+        [VMEM] * 2,
+        limit=4,
+    )
+    (w_ordered,) = local_call(
+        stage_kernel, [shape((width, 3 * group), BF16)], [], [w_qkv], [VMEM], [VMEM], limit=8
+    )
+    bias_row, gain_row = embed_bias[None], ln_gain[None]
+    c1 = along_tm(after(first, p1, w_ordered, bias_row, gain_row), 1)
+    late = after(first, p1, p2, p3)
+    c2, c3 = along_tm(late, 2), along_tm(late, 3)
+    weights = [w_embed, jnp.asarray(table), jnp.asarray(bins), bias_row, gain_row]
+    heads, *blocks, hidden = attend_call(
+        me_s, [packet, p1, p2, after(p3, w_ordered, first)], [*weights, w_ordered], rows, width
+    )
+    d1 = along_tm(after(second, c1), 1)
+    late = after(second, heads)
+    d2, d3 = along_tm(late, 2), along_tm(late, 3)
+
+    (pieces,) = local_call(
+        split_kernel,
+        [shape((4, 2 * piece, half), BF16)],
+        [],
+        [first, c1, c2, c3],
+        [HBM] * 4,
+        [VMEM],
+        scratch=[dma((4,))],
+        limit=4,
+    )
+    by_x = along_clip(pieces, 2)
+    by_y = along_clip(pieces, 4)
+    onward = jnp.where(core == 0, by_x, by_y)
+    turn = [(i, i ^ 4) if i % 2 == 0 else (i, i ^ 2) for i in range(8)]
+    by_xy = lax.ppermute(onward, "clip", turn)
+    held = {0: pieces, 2: by_x, 4: by_y, 6: by_xy}
+    for m in (0, 2, 4, 6):
+        held[m + 1] = along_clip(held[m], 1)
+    (w_all,) = local_call(
+        gather_kernel,
+        [shape((4, 8 * piece, width), BF16)],
+        [clip_s],
+        [held[m] for m in range(8)],
+        [HBM] * 8,
+        [HBM],
+        scratch=[dma((64,))],
+        limit=4,
+    )
+    w_all = w_all.reshape(width, width)
+
+    moved = [heads]
+    for k in (1, 2, 3):
+        moved.append(along_tm(after(blocks[k - 1], d1, d2, d3), k))
+
+    finals = []
+    for i, arrays in enumerate(((first, c1, c2, c3), (second, d1, d2, d3))):
+        keep, give = local_call(
+            grad_kernel,
+            [shape((group // 2, half), BF16)] * 2,
+            [core_s],
+            [heads, *arrays],
+            [VMEM] + [HBM] * 4,
+            [VMEM] * 2,
+            scratch=[VMEM((4 * rows, half), BF16), VMEM((group, half), F32), dma((4,))],
+            limit=8,
+        )
+        mine = add_rounded(keep, along_clip(give, 1))
+        total = mine.astype(F32)
+        for flip in (2, 4, 6):
+            total = total + along_clip(mine, flip).astype(F32)
+        mine = total.astype(BF16)
+        finals += [mine, along_clip(after(mine, *moved[1:]) if i else mine, 1)]
+
+    (encoded,) = local_call(
+        project_kernel,
+        [shape((rows, width), BF16)],
+        [count_s],
+        [hidden, *moved, w_all],
+        [HBM] * 6,
+        [HBM],
+        scratch=[
+            VMEM((rows, width), BF16),
+            VMEM((rows, width), BF16),
+            VMEM((width, width), BF16),
+            VMEM((rows, width), BF16),
+            dma((6,)),
+        ],
+        limit=10,
+    )
+    (grad_w_o,) = local_call(
+        functools.partial(finish_kernel, 1.0 / math.sqrt(8 * rows * 4)),
+        [shape((group, width), F32)],
+        [after(core_s, encoded)],
+        finals,
+        [VMEM] * 4,
+        [VMEM],
+        limit=8,
+    )
+    return (encoded[None], grad_w_o)
+
+
+def attend_call(me_s, packets, weights, rows, width):
+    group = 4 * HEAD_DIM
+    shape = jax.ShapeDtypeStruct
+    scratch = [VMEM((4, *packets[0].shape), BF16)]
+    scratch += [VMEM(w.shape, w.dtype) for w in weights]
+    scratch += [VMEM((4 * rows, width), BF16)]
+    scratch += [VMEM((4, 4 * rows, group), BF16)] * 3
+    scratch += [pltpu.SemaphoreType.DMA((10,))]
+    arrays = [*packets, *weights]
+    return local_call(
+        functools.partial(attend_kernel, rows),
+        [
+            shape((4 * rows, group), BF16),
+            *[shape((rows, group), BF16)] * 3,
+            shape((rows, width), BF16),
+        ],
+        [me_s],
+        arrays,
+        [HBM] * len(arrays),
+        [VMEM] * 5,
+        scratch=scratch,
+        limit=63,
+        cost=30000000,
+    )
 
 
 def solution(mesh):
@@ -135,6 +615,11 @@
         P("clip", "tm", None),
     )
     out_specs = (P("clip", "tm", None), P("tm", None))
+    on_line = mesh.shape["tm"] == 4 and mesh.shape["clip"] == 8
     return jax.shard_map(
-        per_device, mesh=mesh, in_specs=in_specs, out_specs=out_specs, check_vma=False
-    )
+        line_device if on_line else general_device,
+        mesh=mesh,
+        in_specs=in_specs,
+        out_specs=out_specs,
+        check_vma=False,
+    )

time: 244 us -> 101 us (0.41)
  waiting for transfers between devices: 172 us -> 42.4 us
  starting transfers between devices: 0.16 us -> 30.9 us
  blocking collectives: 24.2 us -> 0 us
  Pallas kernels: 0 us -> 18.3 us
  matrix products: 17.5 us -> 0 us
  between operations: 14.6 us -> 1.59 us
  other arithmetic: 9.57 us -> 0.23 us
    all_gather x2 -> x0, waiting for transfers between devices: 75.5 us -> none  [the longest x1 46.9 us: per_device(): lax.all_gather(w_o, 'tm', axis=0, tiled=True)]
    psum x1 -> x0, waiting for transfers between devices: 53.6 us -> none  [per_device(): grad_rows = lax.psum(grad_part, 'clip').astype(jnp.float32)]
    ppermute x0 -> x29, waiting for transfers between devices: none -> 42.4 us  [the longest x12 39 us: along_tm(): return lax.ppermute(array, 'tm', [(i, i ^ flip) for i in range(4)])]
    reduce_scatter x1 -> x0, waiting for transfers between devices: 42.3 us -> none  [per_device(): lax.psum_scatter(jnp.dot(columns.T, cot_rows, preferred_element_type=jnp....]
    ppermute x0 -> x29, starting transfers between devices: none -> 30.9 us  [the longest x12 18.9 us: along_tm(): return lax.ppermute(array, 'tm', [(i, i ^ flip) for i in range(4)])]
    pallas_call x0 -> x10, Pallas kernels: none -> 18.3 us  [local_call(): pl.pallas_call(kernel, out_shape=out_shape, in_specs=specs, out_specs=[pl...]
    dot_general x10 -> x0, matrix products: 17.5 us -> none  [the longest x3 4.69 us: one_block(): jnp.einsum('hqk,khd->qhd', weights.astype(jnp.bfloat16), values_all, pref...]
    all_to_all x1 -> x0, blocking collectives: 14.2 us -> none  [per_device(): lax.all_to_all(head_rows, 'tm', split_axis=0, concat_axis=1, tiled=True)]
  transfers between devices with their start and end apart: 4 -> 29, of which waited for: 4 -> 9; matrix products, arithmetic and copies ran while one was open for 2% -> 1% of each run, Pallas kernels for 0% -> 16%
where the time goes in v2:
time: 101 us; the launch traced here: 100 us
  waiting for transfers between devices  42.4 us (42%)
  starting transfers between devices  30.9 us (31%)
  Pallas kernels  18.3 us (18%)
  local copies, waits for them, and re-layouts  7.11 us (7%)
  between operations  1.59 us (2%)
    ppermute x12, waiting for transfers between devices, along_tm(): return lax.ppermute(array, 'tm', [(i, i ^ flip) for i in range(4)])  39 us
    ppermute x12, starting transfers between devices, along_tm(): return lax.ppermute(array, 'tm', [(i, i ^ flip) for i in range(4)])  18.9 us
    pallas_call x10, Pallas kernels, local_call(): pl.pallas_call(kernel, out_shape=out_shape, in_specs=specs, out_specs=[pl...  18.3 us
    ppermute x16, starting transfers between devices, along_clip(): return lax.ppermute(array, 'clip', [(i, i ^ flip) for i in range(8)])  10.4 us
    unnamed x36, local copies, waits for them, and re-layouts  5.92 us
    ppermute x16, waiting for transfers between devices, along_clip(): return lax.ppermute(array, 'clip', [(i, i ^ flip) for i in range(8)])  3.3 us
  transfers between devices with their start and end apart: 29, of which 9 were waited for; matrix products, arithmetic and copies ran while one was open for 1% of the time, Pallas kernels for 16%

profile of v2, /device:TPU:0, one launch (start us, length us, event | category | flops | bytes accessed | tf_op | source)
XLA Modules:
  0.0 100.5 jit_solution(13696354624067510918)
XLA Ops:
  2.9 5.1 %collective-permute-start.2 = (bf16[208,512]{1,0:T(8,128)(2,1)S(1)}, bf16[208,512]{1,0:T(8,128)(2,1)S(1)}, u32[]{:S(2)}, u32[]{:S(2)}) collective-permute-start(bf16[208,512]{1,0:T(8,128)(2,1)S(1)} %shard_map.122.p0_hbm), channel_id=1, source_target_pairs={{0,3},{1,2},{2,1},{3,0},{4,7},{5,6},{6,5},{7,4},{8,11},{9,10},{10,... | collective-permute-start | bytes 638984 | tf_op jit(solution)/shard_map/ppermute | solution.py:430
  8.7 1.4 %copy-done.3 = bf16[1024,768]{1,0:T(8,128)(2,1)S(1)} copy-done((bf16[1024,768]{1,0:T(8,128)(2,1)S(1)}, bf16[1024,768]{1,0:T(8,128)(2,1)}, u32[]{:S(2)}) %copy-start.3) | copy-done | bytes 1572888
  10.6 1.2 %copy-done = bf16[1024,768]{1,0:T(8,128)(2,1)} copy-done((bf16[1024,768]{1,0:T(8,128)(2,1)}, bf16[1024,768]{1,0:T(8,128)(2,1)S(1)}, u32[]{:S(2)}) %copy-start) | copy-done | bytes 1572888
  13.1 1.2 %collective-permute-done.2.p3_hbm = bf16[208,512]{1,0:T(8,128)(2,1)S(1)} collective-permute-done((bf16[208,512]{1,0:T(8,128)(2,1)S(1)}, bf16[208,512]{1,0:T(8,128)(2,1)S(1)}, u32[]{:S(2)}, u32[]{:S(2)}) %collective-permute-start.2) | collective-permute-done | bytes 213024 | tf_op jit(solution)/shard_map/ppermute | solution.py:430
  14.3 11.9 %collective-permute-done.1.p2_hbm = bf16[208,512]{1,0:T(8,128)(2,1)S(1)} collective-permute-done((bf16[208,512]{1,0:T(8,128)(2,1)S(1)}, bf16[208,512]{1,0:T(8,128)(2,1)S(1)}, u32[]{:S(2)}, u32[]{:S(2)}) %collective-permute-start.1) | collective-permute-done | bytes 213024 | tf_op jit(solution)/shard_map/ppermute | solution.py:430
  26.8 2.5 %collective-permute-start.11 = (bf16[256,512]{1,0:T(8,128)(2,1)S(1)}, bf16[256,512]{1,0:T(8,128)(2,1)S(1)}, u32[]{:S(2)}, u32[]{:S(2)}) collective-permute-start(bf16[256,512]{1,0:T(8,128)(2,1)S(1)} %get-tuple-element.37.refs_0_.c0_hbm), channel_id=1, source_target_pairs={{0,3},{1,2},{2,1},{3,0},{4,7},{5,6},{6,5},{7,4},{8,11},{9,10},{10,... | collective-permute-start | bytes 786440 | tf_op jit(solution)/shard_map/ppermute | solution.py:430
  29.3 1.9 %collective-permute-start.3 = (bf16[256,512]{1,0:T(8,128)(2,1)S(1)}, bf16[256,512]{1,0:T(8,128)(2,1)}, u32[]{:S(2)}, u32[]{:S(2)}) collective-permute-start(bf16[256,512]{1,0:T(8,128)(2,1)S(1)} %get-tuple-element.37.refs_0_.c0_hbm), channel_id=1, source_target_pairs={{0,1},{1,0},{2,3},{3,2},{4,5},{5,4},{6,7},{7,6},{8,9},{9,8},{10,11... | collective-permute-start | bytes 786440 | tf_op jit(solution)/shard_map/ppermute | solution.py:430
  31.2 9.5 %shard_map.125 = (bf16[768,256]{1,0:T(8,128)(2,1)}, bf16[192,256]{1,0:T(8,128)(2,1)}, bf16[192,256]{1,0:T(8,128)(2,1)}, bf16[192,256]{1,0:T(8,128)(2,1)}, bf16[192,1024]{1,0:T(8,128)(2,1)}) custom-call(s32[1]{0:T(128)} %bitcast.1.bin_ref, bf16[208,512]{1,0:T(8,128)(2,1)} %copy-done.4, bf16[208,512]{1,0:T(8,128)(2,1)} %copy-done.12, ...), custom_call_target="tpu_custom_call" | custom-call | flops 1000 | bytes 30000000 | tf_op jit(solution)/shard_map/pallas_call | solution.py:159
  40.7 9.2 %collective-permute-done.10.refs_2_.c2_hbm = bf16[256,512]{1,0:T(8,128)(2,1)S(1)} collective-permute-done((bf16[256,512]{1,0:T(8,128)(2,1)S(1)}, bf16[256,512]{1,0:T(8,128)(2,1)S(1)}, u32[]{:S(2)}, u32[]{:S(2)}) %collective-permute-start.10) | collective-permute-done | bytes 262176 | tf_op jit(solution)/shard_map/ppermute | solution.py:430
  50.0 1.0 copy-done.1
  51.0 1.6 %shard_map.129 = (bf16[128,512]{1,0:T(8,128)(2,1)S(1)}, bf16[128,512]{1,0:T(8,128)(2,1)S(1)}) custom-call(s32[1]{0:T(128)} %bitcast.7.core_ref, bf16[768,256]{1,0:T(8,128)(2,1)S(1)} %copy-done.1, bf16[256,512]{1,0:T(8,128)(2,1)S(1)} %get-tuple-element.37.refs_0_.c0_hbm, bf16[256,512]{1,0:T(8,128)(2,1)} %collective-permute-done.3.refs_1_.c1_hbm, ...), custom_call_target="tpu_custom_call" | custom-call | flops 1000 | bytes 1000 | tf_op jit(solution)/shard_map/pallas_call | solution.py:159
  52.7 1.0 shard_map.126.refs_0_
  53.7 1.6 %collective-permute-start.15 = (bf16[4,64,512]{2,1,0:T(8,128)(2,1)S(1)}, bf16[4,64,512]{2,1,0:T(8,128)(2,1)S(1)}, u32[]{:S(2)}, u32[]{:S(2)}) collective-permute-start(bf16[4,64,512]{2,1,0:T(8,128)(2,1)S(1)} %shard_map.126.refs_0_), channel_id=1, source_target_pairs={{0,16},{4,20},{8,24},{12,28},{16,0},{20,4},{24,8},{28,12},{1,17},{... | collective-permute-start | bytes 786440 | tf_op jit(solution)/shard_map/ppermute | solution.py:434
  55.2 1.5 %collective-permute-start.13 = (bf16[4,64,512]{2,1,0:T(8,128)(2,1)S(1)}, bf16[4,64,512]{2,1,0:T(8,128)(2,1)S(1)}, u32[]{:S(2)}, u32[]{:S(2)}) collective-permute-start(bf16[4,64,512]{2,1,0:T(8,128)(2,1)S(1)} %shard_map.126.refs_0_), channel_id=1, source_target_pairs={{0,8},{4,12},{8,0},{12,4},{16,24},{20,28},{24,16},{28,20},{1,9},{5... | collective-permute-start | bytes 786440 | tf_op jit(solution)/shard_map/ppermute | solution.py:434
  56.7 1.5 %collective-permute-start.6 = (bf16[192,512]{1,0:T(8,128)(2,1)S(1)}, bf16[192,512]{1,0:T(8,128)(2,1)S(1)}, u32[]{:S(2)}, u32[]{:S(2)}) collective-permute-start(bf16[192,512]{1,0:T(8,128)(2,1)S(1)} %get-tuple-element.31.c0_hbm), channel_id=1, source_target_pairs={{0,3},{1,2},{2,1},{3,0},{4,7},{5,6},{6,5},{7,4},{8,11},{9,10},{10,... | collective-permute-start | bytes 589832 | tf_op jit(solution)/shard_map/ppermute | solution.py:430
  58.3 2.8 %collective-permute-start.4 = (bf16[192,512]{1,0:T(8,128)(2,1)S(1)}, bf16[192,512]{1,0:T(8,128)(2,1)S(1)}, u32[]{:S(2)}, u32[]{:S(2)}) collective-permute-start(bf16[192,512]{1,0:T(8,128)(2,1)S(1)} %get-tuple-element.31.c0_hbm), channel_id=1, source_target_pairs={{0,1},{1,0},{2,3},{3,2},{4,5},{5,4},{6,7},{7,6},{8,9},{9,8},{10,11... | collective-permute-start | bytes 589832 | tf_op jit(solution)/shard_map/ppermute | solution.py:430
  61.2 5.2 %collective-permute-done.6.c3_hbm = bf16[192,512]{1,0:T(8,128)(2,1)S(1)} collective-permute-done((bf16[192,512]{1,0:T(8,128)(2,1)S(1)}, bf16[192,512]{1,0:T(8,128)(2,1)S(1)}, u32[]{:S(2)}, u32[]{:S(2)}) %collective-permute-start.6) | collective-permute-done | bytes 196640 | tf_op jit(solution)/shard_map/ppermute | solution.py:430
  66.9 7.3 %collective-permute-done.5.c2_hbm = bf16[192,512]{1,0:T(8,128)(2,1)S(1)} collective-permute-done((bf16[192,512]{1,0:T(8,128)(2,1)S(1)}, bf16[192,512]{1,0:T(8,128)(2,1)S(1)}, u32[]{:S(2)}, u32[]{:S(2)}) %collective-permute-start.5) | collective-permute-done | bytes 196640 | tf_op jit(solution)/shard_map/ppermute | solution.py:430
  75.3 1.5 %shard_map.130 = (bf16[128,512]{1,0:T(8,128)(2,1)S(1)}, bf16[128,512]{1,0:T(8,128)(2,1)S(1)}) custom-call(s32[1]{0:T(128)} %bitcast.7.core_ref, bf16[768,256]{1,0:T(8,128)(2,1)S(1)} %copy-done.2, bf16[192,512]{1,0:T(8,128)(2,1)S(1)} %get-tuple-element.31.c0_hbm, bf16[192,512]{1,0:T(8,128)(2,1)S(1)} %collective-permute-done.4.c1_hbm, ...), custom_call_target="tpu_custom_call" | custom-call | flops 1000 | bytes 1000 | tf_op jit(solution)/shard_map/pallas_call | solution.py:159
  77.0 2.8 %collective-permute-start.8 = (bf16[192,256]{1,0:T(8,128)(2,1)S(1)}, bf16[192,256]{1,0:T(8,128)(2,1)S(1)}, u32[]{:S(2)}, u32[]{:S(2)}) collective-permute-start(bf16[192,256]{1,0:T(8,128)(2,1)S(1)} %copy-done.16), channel_id=1, source_target_pairs={{0,2},{1,3},{2,0},{3,1},{4,6},{5,7},{6,4},{7,5},{8,10},{9,11},{10,... | collective-permute-start | bytes 294920 | tf_op jit(solution)/shard_map/ppermute | solution.py:430
  79.8 1.5 %collective-permute-start.17 = (bf16[4,64,512]{2,1,0:T(8,128)(2,1)S(1)}, bf16[4,64,512]{2,1,0:T(8,128)(2,1)S(1)}, u32[]{:S(2)}, u32[]{:S(2)}) collective-permute-start(bf16[4,64,512]{2,1,0:T(8,128)(2,1)S(1)} %broadcast_select_fusion), channel_id=1, source_target_pairs={{0,16},{4,12},{8,24},{12,4},{16,0},{20,28},{24,8},{28,20},{1,17},{... | collective-permute-start | bytes 786440 | tf_op jit(solution)/shard_map/ppermute | solution.py:512
  81.5 1.5 %collective-permute-start.27 = (bf16[128,512]{1,0:T(8,128)(2,1)S(1)}, bf16[128,512]{1,0:T(8,128)(2,1)S(1)}, u32[]{:S(2)}, u32[]{:S(2)}) collective-permute-start(bf16[128,512]{1,0:T(8,128)(2,1)S(1)} %add_convert_fusion.1), channel_id=1, source_target_pairs={{0,24},{4,28},{8,16},{12,20},{16,8},{20,12},{24,0},{28,4},{1,25},{... | collective-permute-start | bytes 393224 | tf_op jit(solution)/shard_map/ppermute | solution.py:434
  83.0 1.5 %collective-permute-start.26 = (bf16[128,512]{1,0:T(8,128)(2,1)S(1)}, bf16[128,512]{1,0:T(8,128)(2,1)S(1)}, u32[]{:S(2)}, u32[]{:S(2)}) collective-permute-start(bf16[128,512]{1,0:T(8,128)(2,1)S(1)} %add_convert_fusion.1), channel_id=1, source_target_pairs={{0,16},{4,20},{8,24},{12,28},{16,0},{20,4},{24,8},{28,12},{1,17},{... | collective-permute-start | bytes 393224 | tf_op jit(solution)/shard_map/ppermute | solution.py:434
  84.5 0.9 collective-permute-done.8.a2_hbm
  85.4 1.5 %collective-permute-start.25 = (bf16[128,512]{1,0:T(8,128)(2,1)S(1)}, bf16[128,512]{1,0:T(8,128)(2,1)S(1)}, u32[]{:S(2)}, u32[]{:S(2)}) collective-permute-start(bf16[128,512]{1,0:T(8,128)(2,1)S(1)} %add_convert_fusion.1), channel_id=1, source_target_pairs={{0,8},{4,12},{8,0},{12,4},{16,24},{20,28},{24,16},{28,20},{1,9},{5... | collective-permute-start | bytes 393224 | tf_op jit(solution)/shard_map/ppermute | solution.py:434
  87.0 2.0 %collective-permute-done.27 = bf16[128,512]{1,0:T(8,128)(2,1)S(1)} collective-permute-done((bf16[128,512]{1,0:T(8,128)(2,1)S(1)}, bf16[128,512]{1,0:T(8,128)(2,1)S(1)}, u32[]{:S(2)}, u32[]{:S(2)}) %collective-permute-start.27) | collective-permute-done | bytes 131104 | tf_op jit(solution)/shard_map/ppermute | solution.py:434
  89.0 1.5 %collective-permute-start.9 = (bf16[192,256]{1,0:T(8,128)(2,1)S(1)}, bf16[192,256]{1,0:T(8,128)(2,1)S(1)}, u32[]{:S(2)}, u32[]{:S(2)}) collective-permute-start(bf16[192,256]{1,0:T(8,128)(2,1)S(1)} %copy-done.15), channel_id=1, source_target_pairs={{0,3},{1,2},{2,1},{3,0},{4,7},{5,6},{6,5},{7,4},{8,11},{9,10},{10,... | collective-permute-start | bytes 294920 | tf_op jit(solution)/shard_map/ppermute | solution.py:430
  90.5 1.3 %collective-permute-done.26 = bf16[128,512]{1,0:T(8,128)(2,1)S(1)} collective-permute-done((bf16[128,512]{1,0:T(8,128)(2,1)S(1)}, bf16[128,512]{1,0:T(8,128)(2,1)S(1)}, u32[]{:S(2)}, u32[]{:S(2)}) %collective-permute-start.26) | collective-permute-done | bytes 131104 | tf_op jit(solution)/shard_map/ppermute | solution.py:434
  92.5 3.2 %collective-permute-done.9.a3_hbm = bf16[192,256]{1,0:T(8,128)(2,1)S(1)} collective-permute-done((bf16[192,256]{1,0:T(8,128)(2,1)S(1)}, bf16[192,256]{1,0:T(8,128)(2,1)S(1)}, u32[]{:S(2)}, u32[]{:S(2)}) %collective-permute-start.9) | collective-permute-done | bytes 98336 | tf_op jit(solution)/shard_map/ppermute | solution.py:430
  96.2 1.4 %shard_map.127 = bf16[4,256,1024]{2,1,0:T(8,128)(2,1)S(1)} custom-call(s32[1]{0:T(128)} %bitcast.3.clip_ref, bf16[4,64,512]{2,1,0:T(8,128)(2,1)S(1)} %shard_map.126.refs_0_, bf16[4,64,512]{2,1,0:T(8,128)(2,1)S(1)} %collective-permute-done.12.refs_1_, bf16[4,64,512]{2,1,0:T(8,128)(2,1)S(1)} %collective-permute-done.13.refs_2_, ...), custom_call_target="tpu_custom_call" | custom-call | flops 1000 | bytes 1000 | tf_op jit(solution)/shard_map/pallas_call | solution.py:159
  97.6 1.8 %shard_map.128 = bf16[192,1024]{1,0:T(8,128)(2,1)} custom-call(s32[1]{0:T(128)} %bitcast.9.count_ref, bf16[192,1024]{1,0:T(8,128)(2,1)S(1)} %copy-done.7, bf16[768,256]{1,0:T(8,128)(2,1)S(1)} %copy-done.2, bf16[192,256]{1,0:T(8,128)(2,1)S(1)} %collective-permute-done.7.a1_hbm, bf16[192,256]{1,0:T(8,128)(2,1)S(1)} %collective-permute-done.8.a2_hbm, ...), custom_call_target="tpu_custom_call" | custom-call | flops 1000 | bytes 1000 | tf_op jit(solution)/shard_map/pallas_call | solution.py:159
  99.4 1.1 %shard_map.131 = f32[256,1024]{1,0:T(8,128)} custom-call(s32[1]{0:T(128)} %bitcast.7.core_ref, bf16[128,512]{1,0:T(8,128)(2,1)S(1)} %add_convert_fusion.2.refs_0_, bf16[128,512]{1,0:T(8,128)(2,1)S(1)} %collective-permute-done.23.refs_1_, bf16[128,512]{1,0:T(8,128)(2,1)S(1)} %add_convert_fusion.refs_2_, bf16[128,512]{1,0:T(8,128)(2,1)S(1)} %collective-permute-done.28.refs_3_), custom_call_target="tpu_custom_call" | custom-call | flops 1000 | bytes 1000 | tf_op jit(solution)/shard_map/pallas_call | solution.py:159
  (79 shorter events, 7.9 us)
Async XLA Ops:
  2.9 11.3 %collective-permute-start.2 = (bf16[208,512]{1,0:T(8,128)(2,1)S(1)}, bf16[208,512]{1,0:T(8,128)(2,1)S(1)}, u32[]{:S(2)}, u32[]{:S(2)}) collective-permute-start(bf16[208,512]{1,0:T(8,128)(2,1)S(1)} %shard_map.122.p0_hbm), channel_id=1, source_target_pairs={{0,3},{1,2},{2,1},{3,0},{4,7},{5,6},{6,5},{7,4},{8,11},{9,10},{10,... | collective-permute-start | bytes 638984 | tf_op jit(solution)/shard_map/ppermute | solution.py:430
  8.0 18.1 %collective-permute-start.1 = (bf16[208,512]{1,0:T(8,128)(2,1)S(1)}, bf16[208,512]{1,0:T(8,128)(2,1)S(1)}, u32[]{:S(2)}, u32[]{:S(2)}) collective-permute-start(bf16[208,512]{1,0:T(8,128)(2,1)S(1)} %shard_map.122.p0_hbm), channel_id=1, source_target_pairs={{0,2},{1,3},{2,0},{3,1},{4,6},{5,7},{6,4},{7,5},{8,10},{9,11},{10,... | collective-permute-start | bytes 638984 | tf_op jit(solution)/shard_map/ppermute | solution.py:430
  8.0 18.1 %collective-permute-start = (bf16[208,512]{1,0:T(8,128)(2,1)S(1)}, bf16[208,512]{1,0:T(8,128)(2,1)S(1)}, u32[]{:S(2)}, u32[]{:S(2)}) collective-permute-start(bf16[208,512]{1,0:T(8,128)(2,1)S(1)} %shard_map.122.p0_hbm), channel_id=1, source_target_pairs={{0,1},{1,0},{2,3},{3,2},{4,5},{5,4},{6,7},{7,6},{8,9},{9,8},{10,11... | collective-permute-start | bytes 638984 | tf_op jit(solution)/shard_map/ppermute | solution.py:430
  26.8 13.9 %collective-permute-start.11 = (bf16[256,512]{1,0:T(8,128)(2,1)S(1)}, bf16[256,512]{1,0:T(8,128)(2,1)S(1)}, u32[]{:S(2)}, u32[]{:S(2)}) collective-permute-start(bf16[256,512]{1,0:T(8,128)(2,1)S(1)} %get-tuple-element.37.refs_0_.c0_hbm), channel_id=1, source_target_pairs={{0,3},{1,2},{2,1},{3,0},{4,7},{5,6},{6,5},{7,4},{8,11},{9,10},{10,... | collective-permute-start | bytes 786440 | tf_op jit(solution)/shard_map/ppermute | solution.py:430
  29.3 20.6 %collective-permute-start.10 = (bf16[256,512]{1,0:T(8,128)(2,1)S(1)}, bf16[256,512]{1,0:T(8,128)(2,1)S(1)}, u32[]{:S(2)}, u32[]{:S(2)}) collective-permute-start(bf16[256,512]{1,0:T(8,128)(2,1)S(1)} %get-tuple-element.37.refs_0_.c0_hbm), channel_id=1, source_target_pairs={{0,2},{1,3},{2,0},{3,1},{4,6},{5,7},{6,4},{7,5},{8,10},{9,11},{10,... | collective-permute-start | bytes 786440 | tf_op jit(solution)/shard_map/ppermute | solution.py:430
  29.3 20.6 %collective-permute-start.3 = (bf16[256,512]{1,0:T(8,128)(2,1)S(1)}, bf16[256,512]{1,0:T(8,128)(2,1)}, u32[]{:S(2)}, u32[]{:S(2)}) collective-permute-start(bf16[256,512]{1,0:T(8,128)(2,1)S(1)} %get-tuple-element.37.refs_0_.c0_hbm), channel_id=1, source_target_pairs={{0,1},{1,0},{2,3},{3,2},{4,5},{5,4},{6,7},{7,6},{8,9},{9,8},{10,11... | collective-permute-start | bytes 786440 | tf_op jit(solution)/shard_map/ppermute | solution.py:430
  51.0 24.3 %copy-start.2 = (bf16[768,256]{1,0:T(8,128)(2,1)S(1)}, bf16[768,256]{1,0:T(8,128)(2,1)}, u32[]{:S(2)}) copy-start(bf16[768,256]{1,0:T(8,128)(2,1)} %get-tuple-element.26.a0_hbm.a_ref) | copy-start | bytes 1179652
  52.6 24.4 %copy-start.16 = (bf16[192,256]{1,0:T(8,128)(2,1)S(1)}, bf16[192,256]{1,0:T(8,128)(2,1)}, u32[]{:S(2)}) copy-start(bf16[192,256]{1,0:T(8,128)(2,1)} %get-tuple-element.34) | copy-start | bytes 294916
  52.6 5.7 %collective-permute-start.19 = (bf16[128,512]{1,0:T(8,128)(2,1)S(1)}, bf16[128,512]{1,0:T(8,128)(2,1)S(1)}, u32[]{:S(2)}, u32[]{:S(2)}) collective-permute-start(bf16[128,512]{1,0:T(8,128)(2,1)S(1)} %get-tuple-element.40), channel_id=1, source_target_pairs={{0,4},{4,0},{8,12},{12,8},{16,20},{20,16},{24,28},{28,24},{1,5},{5... | collective-permute-start | bytes 393224 | tf_op jit(solution)/shard_map/ppermute | solution.py:434
  53.7 23.1 %collective-permute-start.15 = (bf16[4,64,512]{2,1,0:T(8,128)(2,1)S(1)}, bf16[4,64,512]{2,1,0:T(8,128)(2,1)S(1)}, u32[]{:S(2)}, u32[]{:S(2)}) collective-permute-start(bf16[4,64,512]{2,1,0:T(8,128)(2,1)S(1)} %shard_map.126.refs_0_), channel_id=1, source_target_pairs={{0,16},{4,20},{8,24},{12,28},{16,0},{20,4},{24,8},{28,12},{1,17},{... | collective-permute-start | bytes 786440 | tf_op jit(solution)/shard_map/ppermute | solution.py:434
  55.2 21.6 %collective-permute-start.13 = (bf16[4,64,512]{2,1,0:T(8,128)(2,1)S(1)}, bf16[4,64,512]{2,1,0:T(8,128)(2,1)S(1)}, u32[]{:S(2)}, u32[]{:S(2)}) collective-permute-start(bf16[4,64,512]{2,1,0:T(8,128)(2,1)S(1)} %shard_map.126.refs_0_), channel_id=1, source_target_pairs={{0,8},{4,12},{8,0},{12,4},{16,24},{20,28},{24,16},{28,20},{1,9},{5... | collective-permute-start | bytes 786440 | tf_op jit(solution)/shard_map/ppermute | solution.py:434
  56.7 9.7 %collective-permute-start.6 = (bf16[192,512]{1,0:T(8,128)(2,1)S(1)}, bf16[192,512]{1,0:T(8,128)(2,1)S(1)}, u32[]{:S(2)}, u32[]{:S(2)}) collective-permute-start(bf16[192,512]{1,0:T(8,128)(2,1)S(1)} %get-tuple-element.31.c0_hbm), channel_id=1, source_target_pairs={{0,3},{1,2},{2,1},{3,0},{4,7},{5,6},{6,5},{7,4},{8,11},{9,10},{10,... | collective-permute-start | bytes 589832 | tf_op jit(solution)/shard_map/ppermute | solution.py:430
  58.3 16.0 %collective-permute-start.5 = (bf16[192,512]{1,0:T(8,128)(2,1)S(1)}, bf16[192,512]{1,0:T(8,128)(2,1)S(1)}, u32[]{:S(2)}, u32[]{:S(2)}) collective-permute-start(bf16[192,512]{1,0:T(8,128)(2,1)S(1)} %get-tuple-element.31.c0_hbm), channel_id=1, source_target_pairs={{0,2},{1,3},{2,0},{3,1},{4,6},{5,7},{6,4},{7,5},{8,10},{9,11},{10,... | collective-permute-start | bytes 589832 | tf_op jit(solution)/shard_map/ppermute | solution.py:430
  58.3 16.5 %collective-permute-start.4 = (bf16[192,512]{1,0:T(8,128)(2,1)S(1)}, bf16[192,512]{1,0:T(8,128)(2,1)S(1)}, u32[]{:S(2)}, u32[]{:S(2)}) collective-permute-start(bf16[192,512]{1,0:T(8,128)(2,1)S(1)} %get-tuple-element.31.c0_hbm), channel_id=1, source_target_pairs={{0,1},{1,0},{2,3},{3,2},{4,5},{5,4},{6,7},{7,6},{8,9},{9,8},{10,11... | collective-permute-start | bytes 589832 | tf_op jit(solution)/shard_map/ppermute | solution.py:430
  61.2 27.8 %copy-start.15 = (bf16[192,256]{1,0:T(8,128)(2,1)S(1)}, bf16[192,256]{1,0:T(8,128)(2,1)}, u32[]{:S(2)}) copy-start(bf16[192,256]{1,0:T(8,128)(2,1)} %get-tuple-element.36) | copy-start | bytes 294916
  66.4 10.6 %collective-permute-start.22 = (bf16[128,512]{1,0:T(8,128)(2,1)S(1)}, bf16[128,512]{1,0:T(8,128)(2,1)S(1)}, u32[]{:S(2)}, u32[]{:S(2)}) collective-permute-start(bf16[128,512]{1,0:T(8,128)(2,1)S(1)} %add_convert_fusion.3), channel_id=1, source_target_pairs={{0,24},{4,28},{8,16},{12,20},{16,8},{20,12},{24,0},{28,4},{1,25},{... | collective-permute-start | bytes 393224 | tf_op jit(solution)/shard_map/ppermute | solution.py:434
  74.2 7.1 %collective-permute-start.21 = (bf16[128,512]{1,0:T(8,128)(2,1)S(1)}, bf16[128,512]{1,0:T(8,128)(2,1)S(1)}, u32[]{:S(2)}, u32[]{:S(2)}) collective-permute-start(bf16[128,512]{1,0:T(8,128)(2,1)S(1)} %add_convert_fusion.3), channel_id=1, source_target_pairs={{0,16},{4,20},{8,24},{12,28},{16,0},{20,4},{24,8},{28,12},{1,17},{... | collective-permute-start | bytes 393224 | tf_op jit(solution)/shard_map/ppermute | solution.py:434
  74.7 6.7 %collective-permute-start.20 = (bf16[128,512]{1,0:T(8,128)(2,1)S(1)}, bf16[128,512]{1,0:T(8,128)(2,1)S(1)}, u32[]{:S(2)}, u32[]{:S(2)}) collective-permute-start(bf16[128,512]{1,0:T(8,128)(2,1)S(1)} %add_convert_fusion.3), channel_id=1, source_target_pairs={{0,8},{4,12},{8,0},{12,4},{16,24},{20,28},{24,16},{28,20},{1,9},{5... | collective-permute-start | bytes 393224 | tf_op jit(solution)/shard_map/ppermute | solution.py:434
  76.8 6.2 %collective-permute-start.7 = (bf16[192,256]{1,0:T(8,128)(2,1)S(1)}, bf16[192,256]{1,0:T(8,128)(2,1)S(1)}, u32[]{:S(2)}, u32[]{:S(2)}) collective-permute-start(bf16[192,256]{1,0:T(8,128)(2,1)S(1)} %copy-done.17), channel_id=1, source_target_pairs={{0,1},{1,0},{2,3},{3,2},{4,5},{5,4},{6,7},{7,6},{8,9},{9,8},{10,11... | collective-permute-start | bytes 294920 | tf_op jit(solution)/shard_map/ppermute | solution.py:430
  76.9 3.0 %collective-permute-start.24 = (bf16[128,512]{1,0:T(8,128)(2,1)S(1)}, bf16[128,512]{1,0:T(8,128)(2,1)S(1)}, u32[]{:S(2)}, u32[]{:S(2)}) collective-permute-start(bf16[128,512]{1,0:T(8,128)(2,1)S(1)} %get-tuple-element.42), channel_id=1, source_target_pairs={{0,4},{4,0},{8,12},{12,8},{16,20},{20,16},{24,28},{28,24},{1,5},{5... | collective-permute-start | bytes 393224 | tf_op jit(solution)/shard_map/ppermute | solution.py:434
  77.0 8.4 %collective-permute-start.8 = (bf16[192,256]{1,0:T(8,128)(2,1)S(1)}, bf16[192,256]{1,0:T(8,128)(2,1)S(1)}, u32[]{:S(2)}, u32[]{:S(2)}) collective-permute-start(bf16[192,256]{1,0:T(8,128)(2,1)S(1)} %copy-done.16), channel_id=1, source_target_pairs={{0,2},{1,3},{2,0},{3,1},{4,6},{5,7},{6,4},{7,5},{8,10},{9,11},{10,... | collective-permute-start | bytes 294920 | tf_op jit(solution)/shard_map/ppermute | solution.py:430
  79.8 12.5 %collective-permute-start.17 = (bf16[4,64,512]{2,1,0:T(8,128)(2,1)S(1)}, bf16[4,64,512]{2,1,0:T(8,128)(2,1)S(1)}, u32[]{:S(2)}, u32[]{:S(2)}) collective-permute-start(bf16[4,64,512]{2,1,0:T(8,128)(2,1)S(1)} %broadcast_select_fusion), channel_id=1, source_target_pairs={{0,16},{4,12},{8,24},{12,4},{16,0},{20,28},{24,8},{28,20},{1,17},{... | collective-permute-start | bytes 786440 | tf_op jit(solution)/shard_map/ppermute | solution.py:512
  81.4 14.3 %collective-permute-start.12 = (bf16[4,64,512]{2,1,0:T(8,128)(2,1)S(1)}, bf16[4,64,512]{2,1,0:T(8,128)(2,1)S(1)}, u32[]{:S(2)}, u32[]{:S(2)}) collective-permute-start(bf16[4,64,512]{2,1,0:T(8,128)(2,1)S(1)} %shard_map.126.refs_0_), channel_id=1, source_target_pairs={{0,4},{4,0},{8,12},{12,8},{16,20},{20,16},{24,28},{28,24},{1,5},{5... | collective-permute-start | bytes 786440 | tf_op jit(solution)/shard_map/ppermute | solution.py:434
  81.5 7.5 %collective-permute-start.27 = (bf16[128,512]{1,0:T(8,128)(2,1)S(1)}, bf16[128,512]{1,0:T(8,128)(2,1)S(1)}, u32[]{:S(2)}, u32[]{:S(2)}) collective-permute-start(bf16[128,512]{1,0:T(8,128)(2,1)S(1)} %add_convert_fusion.1), channel_id=1, source_target_pairs={{0,24},{4,28},{8,16},{12,20},{16,8},{20,12},{24,0},{28,4},{1,25},{... | collective-permute-start | bytes 393224 | tf_op jit(solution)/shard_map/ppermute | solution.py:434
  83.0 8.8 %collective-permute-start.26 = (bf16[128,512]{1,0:T(8,128)(2,1)S(1)}, bf16[128,512]{1,0:T(8,128)(2,1)S(1)}, u32[]{:S(2)}, u32[]{:S(2)}) collective-permute-start(bf16[128,512]{1,0:T(8,128)(2,1)S(1)} %add_convert_fusion.1), channel_id=1, source_target_pairs={{0,16},{4,20},{8,24},{12,28},{16,0},{20,4},{24,8},{28,12},{1,17},{... | collective-permute-start | bytes 393224 | tf_op jit(solution)/shard_map/ppermute | solution.py:434
  85.4 6.4 %collective-permute-start.25 = (bf16[128,512]{1,0:T(8,128)(2,1)S(1)}, bf16[128,512]{1,0:T(8,128)(2,1)S(1)}, u32[]{:S(2)}, u32[]{:S(2)}) collective-permute-start(bf16[128,512]{1,0:T(8,128)(2,1)S(1)} %add_convert_fusion.1), channel_id=1, source_target_pairs={{0,8},{4,12},{8,0},{12,4},{16,24},{20,28},{24,16},{28,20},{1,9},{5... | collective-permute-start | bytes 393224 | tf_op jit(solution)/shard_map/ppermute | solution.py:434
  89.0 6.7 %collective-permute-start.9 = (bf16[192,256]{1,0:T(8,128)(2,1)S(1)}, bf16[192,256]{1,0:T(8,128)(2,1)S(1)}, u32[]{:S(2)}, u32[]{:S(2)}) collective-permute-start(bf16[192,256]{1,0:T(8,128)(2,1)S(1)} %copy-done.15), channel_id=1, source_target_pairs={{0,3},{1,2},{2,1},{3,0},{4,7},{5,6},{6,5},{7,4},{8,11},{9,10},{10,... | collective-permute-start | bytes 294920 | tf_op jit(solution)/shard_map/ppermute | solution.py:430
  91.8 4.4 %collective-permute-start.16 = (bf16[4,64,512]{2,1,0:T(8,128)(2,1)S(1)}, bf16[4,64,512]{2,1,0:T(8,128)(2,1)S(1)}, u32[]{:S(2)}, u32[]{:S(2)}) collective-permute-start(bf16[4,64,512]{2,1,0:T(8,128)(2,1)S(1)} %collective-permute-done.15.refs_4_), channel_id=1, source_target_pairs={{0,4},{4,0},{8,12},{12,8},{16,20},{20,16},{24,28},{28,24},{1,5},{5... | collective-permute-start | bytes 786440 | tf_op jit(solution)/shard_map/ppermute | solution.py:434
  91.8 4.4 %collective-permute-start.14 = (bf16[4,64,512]{2,1,0:T(8,128)(2,1)S(1)}, bf16[4,64,512]{2,1,0:T(8,128)(2,1)S(1)}, u32[]{:S(2)}, u32[]{:S(2)}) collective-permute-start(bf16[4,64,512]{2,1,0:T(8,128)(2,1)S(1)} %collective-permute-done.13.refs_2_), channel_id=1, source_target_pairs={{0,4},{4,0},{8,12},{12,8},{16,20},{20,16},{24,28},{28,24},{1,5},{5... | collective-permute-start | bytes 786440 | tf_op jit(solution)/shard_map/ppermute | solution.py:434
  92.3 3.9 %collective-permute-start.18 = (bf16[4,64,512]{2,1,0:T(8,128)(2,1)S(1)}, bf16[4,64,512]{2,1,0:T(8,128)(2,1)S(1)}, u32[]{:S(2)}, u32[]{:S(2)}) collective-permute-start(bf16[4,64,512]{2,1,0:T(8,128)(2,1)S(1)} %collective-permute-done.17.refs_6_), channel_id=1, source_target_pairs={{0,4},{4,0},{8,12},{12,8},{16,20},{20,16},{24,28},{28,24},{1,5},{5... | collective-permute-start | bytes 786440 | tf_op jit(solution)/shard_map/ppermute | solution.py:434
  95.7 3.7 %collective-permute-start.23 = (bf16[128,512]{1,0:T(8,128)(2,1)S(1)}, bf16[128,512]{1,0:T(8,128)(2,1)S(1)}, u32[]{:S(2)}, u32[]{:S(2)}) collective-permute-start(bf16[128,512]{1,0:T(8,128)(2,1)S(1)} %add_convert_fusion.2.refs_0_), channel_id=1, source_target_pairs={{0,4},{4,0},{8,12},{12,8},{16,20},{20,16},{24,28},{28,24},{1,5},{5... | collective-permute-start | bytes 393224 | tf_op jit(solution)/shard_map/ppermute | solution.py:434
  95.7 3.7 %collective-permute-start.28 = (bf16[128,512]{1,0:T(8,128)(2,1)S(1)}, bf16[128,512]{1,0:T(8,128)(2,1)S(1)}, u32[]{:S(2)}, u32[]{:S(2)}) collective-permute-start(bf16[128,512]{1,0:T(8,128)(2,1)S(1)} %add_convert_fusion.refs_2_), channel_id=1, source_target_pairs={{0,4},{4,0},{8,12},{12,8},{16,20},{20,16},{24,28},{28,24},{1,5},{5... | collective-permute-start | bytes 393224 | tf_op jit(solution)/shard_map/ppermute | solution.py:434
  (15 other events, 86.4 us)

commit v3 on v2

--- a/solution.py
+++ b/solution.py
@@ -189,7 +189,7 @@
     first_ref[0:rows, :] = cot_ref[:, 0:half]
     first_ref[rows : rows + piece, :] = w_ref[pl.ds(start, piece), 0:half]
     first_ref[rows + piece :, :] = w_ref[pl.ds(start, piece), half : 2 * half]
-    second_ref[...] = cot_ref[:, half : 2 * half]
+    second_ref[...] = cot_ref[:, half:]
 
 
 def split_kernel(*refs):
@@ -365,42 +365,31 @@
     send_ref[...] = sum_ref[pl.ds(pl.multiple_of((1 - core) * half, half), half), :].astype(BF16)
 
 
-def gather_kernel(clip_ref, *refs):
-    held, out_hbm, sems = refs[:8], refs[8], refs[9]
+def project_kernel(clip_ref, count_ref, hidden_hbm, a0_hbm, a1_hbm, a2_hbm, a3_hbm, *refs):
+    held, (out_hbm, hidden, heads, w_all, out, sems) = refs[:8], refs[8:]
+    rows = hidden.shape[0]
+    group = a0_hbm.shape[1]
     clip = clip_ref[0]
     piece = held[0].shape[1] // 2
     half = held[0].shape[2]
     copies = []
+
+    def move(source, target):
+        copies.append(pltpu.make_async_copy(source, target, sems.at[len(copies)]))
+        copies[-1].start()
+
     for m in range(8):
-        start = pl.multiple_of(jnp.bitwise_xor(clip, m) * piece, piece)
         for k in range(4):
+            start = pl.multiple_of(k * group + jnp.bitwise_xor(clip, m) * piece, piece)
             for side in range(2):
-                copies.append(
-                    pltpu.make_async_copy(
-                        held[m].at[k, side * piece : (side + 1) * piece],
-                        out_hbm.at[k, pl.ds(start, piece), side * half : (side + 1) * half],
-                        sems.at[len(copies)],
-                    )
+                move(
+                    held[m].at[k, side * piece : (side + 1) * piece],
+                    w_all.at[pl.ds(start, piece), side * half : (side + 1) * half],
                 )
-                copies[-1].start()
-    for copy in copies:
-        copy.wait()
-
-
-def project_kernel(
-    count_ref, hidden_hbm, a0_hbm, a1_hbm, a2_hbm, a3_hbm, w_hbm, out_hbm, hidden, heads, w_all, out, sems
-):
-    rows, group = a1_hbm.shape
-    copies = [
-        pltpu.make_async_copy(w_hbm, w_all, sems.at[0]),
-        pltpu.make_async_copy(hidden_hbm, hidden, sems.at[1]),
-        pltpu.make_async_copy(a0_hbm.at[0:rows], heads.at[:, 0:group], sems.at[2]),
-    ]
+    move(hidden_hbm, hidden)
+    move(a0_hbm.at[0:rows], heads.at[:, 0:group])
     for k, source in enumerate((a1_hbm, a2_hbm, a3_hbm)):
-        columns = slice((k + 1) * group, (k + 2) * group)
-        copies.append(pltpu.make_async_copy(source, heads.at[:, columns], sems.at[3 + k]))
-    for copy in copies:
-        copy.start()
+        move(source, heads.at[:, (k + 1) * group : (k + 2) * group])
     for copy in copies:
         copy.wait()
     slot = lax.broadcasted_iota(jnp.int32, (rows, 1), 0)
@@ -416,12 +405,12 @@
     out_ref = refs[-1]
     core = core_ref[0]
     half = out_ref.shape[0] // 2
-    parts = (len(refs) - 1) // 2
-    width = out_ref.shape[1] // parts
     mine = pl.multiple_of(core * half, half)
     theirs = pl.multiple_of((1 - core) * half, half)
-    for c in range(parts):
-        columns = slice(c * width, (c + 1) * width)
+    at = 0
+    for c in range((len(refs) - 1) // 2):
+        columns = slice(at, at + refs[2 * c].shape[1])
+        at = columns.stop
         out_ref[pl.ds(mine, half), columns] = refs[2 * c][...].astype(F32) * scale
         out_ref[pl.ds(theirs, half), columns] = refs[2 * c + 1][...].astype(F32) * scale
 
@@ -439,6 +428,8 @@
 
 
 def after(value, *others):
+    if not others:
+        return value
     return lax.optimization_barrier((value, *others))[0]
 
 
@@ -460,6 +451,7 @@
     cot = cotangent[0]
     dma = pltpu.SemaphoreType.DMA
 
+    extra = 2 * piece
     (packet,) = local_call(
         pack_kernel,
         [shape((rows + META, half), BF16)],
@@ -470,10 +462,12 @@
         scratch=[VMEM((META, half), F32)],
         limit=4,
     )
-    p1, p2, p3 = [along_tm(packet, k) for k in (1, 2, 3)]
     first, second = local_call(
         halve_kernel,
-        [shape((rows + 2 * piece, half), BF16), shape((rows, half), BF16)],
+        [
+            shape((rows + extra, 512), BF16),
+            shape((rows, width - 512), BF16),
+        ],
         [clip_s],
         [cot, w_o],
         [VMEM] * 2,
@@ -484,20 +478,53 @@
         stage_kernel, [shape((width, 3 * group), BF16)], [], [w_qkv], [VMEM], [VMEM], limit=8
     )
     bias_row, gain_row = embed_bias[None], ln_gain[None]
+    p1, p2 = along_tm(packet, 1), along_tm(packet, 2)
+    p3 = along_tm(after(packet), 3)
     c1 = along_tm(after(first, p1, w_ordered, bias_row, gain_row), 1)
-    late = after(first, p1, p2, p3)
-    c2, c3 = along_tm(late, 2), along_tm(late, 3)
+    c2 = along_tm(after(first, p2), 2)
+    c3 = along_tm(after(first, p1, p2, p3), 3)
     weights = [w_embed, jnp.asarray(table), jnp.asarray(bins), bias_row, gain_row]
     heads, *blocks, hidden = attend_call(
-        me_s, [packet, p1, p2, after(p3, w_ordered, first)], [*weights, w_ordered], rows, width
+        me_s, [packet, p1, p2, after(p3)], [*weights, w_ordered], rows, width
     )
     d1 = along_tm(after(second, c1), 1)
-    late = after(second, heads)
-    d2, d3 = along_tm(late, 2), along_tm(late, 3)
+    d2 = along_tm(after(second, heads), 2)
+    d3 = along_tm(after(second, heads), 3)
+
+    def reduce_clips(core, wide, arrays, two_rounds, *before):
+        keep, give = local_call(
+            grad_kernel,
+            [shape((group // 2, wide), BF16)] * 2,
+            [core],
+            [heads, after(arrays[0], *before), *arrays[1:]],
+            [VMEM] + [HBM] * 4,
+            [VMEM] * 2,
+            scratch=[VMEM((4 * rows, wide), BF16), VMEM((group, wide), F32), dma((4,))],
+            limit=8,
+        )
+        mine = add_rounded(keep, along_clip(give, 1))
+        if not two_rounds:
+            total = mine.astype(F32)
+            for flip in (2, 4, 6):
+                total = total + along_clip(mine, flip).astype(F32)
+            return total.astype(BF16)
+        quarter = group // 4
+        upper, lower = mine[:quarter], mine[quarter:]
+        upper, lower = (
+            add_rounded(upper, along_clip(upper, 2)),
+            add_rounded(lower, along_clip(lower, 4)),
+        )
+        upper, lower = (
+            add_rounded(upper, along_clip(upper, 4)),
+            add_rounded(lower, along_clip(lower, 2)),
+        )
+        return jnp.concatenate([upper, lower], axis=0)
+
+    sum_1 = reduce_clips(core_s, 512, (first, c1, c2, c3), False)
 
     (pieces,) = local_call(
         split_kernel,
-        [shape((4, 2 * piece, half), BF16)],
+        [shape((4, extra, half), BF16)],
         [],
         [first, c1, c2, c3],
         [HBM] * 4,
@@ -505,65 +532,36 @@
         scratch=[dma((4,))],
         limit=4,
     )
-    by_x = along_clip(pieces, 2)
-    by_y = along_clip(pieces, 4)
-    onward = jnp.where(core == 0, by_x, by_y)
+    pieces = after(pieces, d1)
+    held = {0: pieces}
+    held[2], held[4] = along_clip(pieces, 2), along_clip(pieces, 4)
+    onward = jnp.where(core == 0, held[2], held[4])
     turn = [(i, i ^ 4) if i % 2 == 0 else (i, i ^ 2) for i in range(8)]
-    by_xy = lax.ppermute(onward, "clip", turn)
-    held = {0: pieces, 2: by_x, 4: by_y, 6: by_xy}
+    held[6] = lax.ppermute(after(onward, heads), "clip", turn)
     for m in (0, 2, 4, 6):
         held[m + 1] = along_clip(held[m], 1)
-    (w_all,) = local_call(
-        gather_kernel,
-        [shape((4, 8 * piece, width), BF16)],
-        [clip_s],
-        [held[m] for m in range(8)],
-        [HBM] * 8,
-        [HBM],
-        scratch=[dma((64,))],
-        limit=4,
-    )
-    w_all = w_all.reshape(width, width)
-
     moved = [heads]
     for k in (1, 2, 3):
-        moved.append(along_tm(after(blocks[k - 1], d1, d2, d3), k))
-
-    finals = []
-    for i, arrays in enumerate(((first, c1, c2, c3), (second, d1, d2, d3))):
-        keep, give = local_call(
-            grad_kernel,
-            [shape((group // 2, half), BF16)] * 2,
-            [core_s],
-            [heads, *arrays],
-            [VMEM] + [HBM] * 4,
-            [VMEM] * 2,
-            scratch=[VMEM((4 * rows, half), BF16), VMEM((group, half), F32), dma((4,))],
-            limit=8,
-        )
-        mine = add_rounded(keep, along_clip(give, 1))
-        total = mine.astype(F32)
-        for flip in (2, 4, 6):
-            total = total + along_clip(mine, flip).astype(F32)
-        mine = total.astype(BF16)
-        finals += [mine, along_clip(after(mine, *moved[1:]) if i else mine, 1)]
-
+        moved.append(along_tm(after(blocks[k - 1], d2, d3), k))
+    sum_2 = reduce_clips(core_s, width - 512, (second, d1, d2, d3), False)
     (encoded,) = local_call(
         project_kernel,
         [shape((rows, width), BF16)],
-        [count_s],
-        [hidden, *moved, w_all],
-        [HBM] * 6,
+        [clip_s, count_s],
+        [hidden, *moved, *[held[m] for m in range(8)]],
+        [HBM] * 13,
         [HBM],
         scratch=[
             VMEM((rows, width), BF16),
             VMEM((rows, width), BF16),
             VMEM((width, width), BF16),
             VMEM((rows, width), BF16),
-            dma((6,)),
+            dma((69,)),
         ],
         limit=10,
     )
+    finals = [sum_1, along_clip(after(sum_1), 1)]
+    finals += [sum_2, along_clip(after(sum_2, *moved[1:]), 1)]
     (grad_w_o,) = local_call(
         functools.partial(finish_kernel, 1.0 / math.sqrt(8 * rows * 4)),
         [shape((group, width), F32)],
@@ -598,7 +596,7 @@
         [VMEM] * 5,
         scratch=scratch,
         limit=63,
-        cost=30000000,
+        cost=100000000,
     )
 
 

time: 101 us -> 97.4 us (0.964)
  waiting for transfers between devices: 42.4 us -> 28.6 us
  starting transfers between devices: 30.9 us -> 40.3 us
    ppermute x12, waiting for transfers between devices: 39 us -> 20.8 us  [along_tm(): return lax.ppermute(array, 'tm', [(i, i ^ flip) for i in range(4)])]
    ppermute x12, starting transfers between devices: 18.9 us -> 26.7 us  [along_tm(): return lax.ppermute(array, 'tm', [(i, i ^ flip) for i in range(4)])]
    ppermute x16, waiting for transfers between devices: 3.3 us -> 7.73 us  [along_clip(): return lax.ppermute(array, 'clip', [(i, i ^ flip) for i in range(8)])]
    ppermute x16, starting transfers between devices: 10.4 us -> 12 us  [along_clip(): return lax.ppermute(array, 'clip', [(i, i ^ flip) for i in range(8)])]
    pallas_call x10 -> x9, Pallas kernels: 18.3 us -> 18.7 us  [local_call(): pl.pallas_call(kernel, out_shape=out_shape, in_specs=specs, out_specs=[pl...]
  transfers between devices with their start and end apart: 29 -> 29, of which waited for: 9 -> 10; matrix products, arithmetic and copies ran while one was open for 1% -> 1% of each run, Pallas kernels for 16% -> 18%
where the time goes in v3:
time: 97.4 us; the launch traced here: 97.1 us
  starting transfers between devices  40.3 us (41%)
  waiting for transfers between devices  28.6 us (29%)
  Pallas kernels  18.7 us (19%)
  local copies, waits for them, and re-layouts  7.8 us (8%)
  between operations  1.52 us (2%)
    ppermute x12, starting transfers between devices, along_tm(): return lax.ppermute(array, 'tm', [(i, i ^ flip) for i in range(4)])  26.7 us
    ppermute x12, waiting for transfers between devices, along_tm(): return lax.ppermute(array, 'tm', [(i, i ^ flip) for i in range(4)])  20.8 us
    pallas_call x9, Pallas kernels, local_call(): pl.pallas_call(kernel, out_shape=out_shape, in_specs=specs, out_specs=[pl...  18.7 us
    ppermute x16, starting transfers between devices, along_clip(): return lax.ppermute(array, 'clip', [(i, i ^ flip) for i in range(8)])  12 us
    ppermute x16, waiting for transfers between devices, along_clip(): return lax.ppermute(array, 'clip', [(i, i ^ flip) for i in range(8)])  7.73 us
    unnamed x36, local copies, waits for them, and re-layouts  6.6 us
  transfers between devices with their start and end apart: 29, of which 10 were waited for; matrix products, arithmetic and copies ran while one was open for 1% of the time, Pallas kernels for 18%

profile of v3, /device:TPU:0, one launch (start us, length us, event | category | flops | bytes accessed | tf_op | source)
XLA Modules:
  0.0 97.1 jit_solution(9928420393890423134)
XLA Ops:
  1.3 0.9 copy-done.8
  2.9 3.1 %collective-permute-start = (bf16[208,512]{1,0:T(8,128)(2,1)S(1)}, bf16[208,512]{1,0:T(8,128)(2,1)S(1)}, u32[]{:S(2)}, u32[]{:S(2)}) collective-permute-start(bf16[208,512]{1,0:T(8,128)(2,1)S(1)} %shard_map.122.p0_hbm), channel_id=1, source_target_pairs={{0,1},{1,0},{2,3},{3,2},{4,5},{5,4},{6,7},{7,6},{8,9},{9,8},{10,11... | collective-permute-start | bytes 638984 | tf_op jit(solution)/shard_map/ppermute | solution.py:419
  6.0 2.6 %collective-permute-start.1 = (bf16[208,512]{1,0:T(8,128)(2,1)S(1)}, bf16[208,512]{1,0:T(8,128)(2,1)S(1)}, u32[]{:S(2)}, u32[]{:S(2)}) collective-permute-start(bf16[208,512]{1,0:T(8,128)(2,1)S(1)} %shard_map.122.p0_hbm), channel_id=1, source_target_pairs={{0,2},{1,3},{2,0},{3,1},{4,6},{5,7},{6,4},{7,5},{8,10},{9,11},{10,... | collective-permute-start | bytes 638984 | tf_op jit(solution)/shard_map/ppermute | solution.py:419
  8.6 1.4 %copy-done.3 = bf16[1024,768]{1,0:T(8,128)(2,1)S(1)} copy-done((bf16[1024,768]{1,0:T(8,128)(2,1)S(1)}, bf16[1024,768]{1,0:T(8,128)(2,1)}, u32[]{:S(2)}) %copy-start.3) | copy-done | bytes 1572888
  10.6 1.2 %copy-done = bf16[1024,768]{1,0:T(8,128)(2,1)} copy-done((bf16[1024,768]{1,0:T(8,128)(2,1)}, bf16[1024,768]{1,0:T(8,128)(2,1)S(1)}, u32[]{:S(2)}) %copy-start) | copy-done | bytes 1572888
  13.0 2.1 %collective-permute-done.p1_hbm = bf16[208,512]{1,0:T(8,128)(2,1)S(1)} collective-permute-done((bf16[208,512]{1,0:T(8,128)(2,1)S(1)}, bf16[208,512]{1,0:T(8,128)(2,1)S(1)}, u32[]{:S(2)}, u32[]{:S(2)}) %collective-permute-start) | collective-permute-done | bytes 213024 | tf_op jit(solution)/shard_map/ppermute | solution.py:419
  15.7 8.5 %collective-permute-done.1.p2_hbm = bf16[208,512]{1,0:T(8,128)(2,1)S(1)} collective-permute-done((bf16[208,512]{1,0:T(8,128)(2,1)S(1)}, bf16[208,512]{1,0:T(8,128)(2,1)S(1)}, u32[]{:S(2)}, u32[]{:S(2)}) %collective-permute-start.1) | collective-permute-done | bytes 213024 | tf_op jit(solution)/shard_map/ppermute | solution.py:419
  25.0 2.5 %collective-permute-start.10 = (bf16[256,512]{1,0:T(8,128)(2,1)S(1)}, bf16[256,512]{1,0:T(8,128)(2,1)S(1)}, u32[]{:S(2)}, u32[]{:S(2)}) collective-permute-start(bf16[256,512]{1,0:T(8,128)(2,1)S(1)} %get-tuple-element.38.refs_0_.c0_hbm), channel_id=1, source_target_pairs={{0,3},{1,2},{2,1},{3,0},{4,7},{5,6},{6,5},{7,4},{8,11},{9,10},{10,... | collective-permute-start | bytes 786440 | tf_op jit(solution)/shard_map/ppermute | solution.py:419
  27.4 9.9 %collective-permute-start.9 = (bf16[256,512]{1,0:T(8,128)(2,1)S(1)}, bf16[256,512]{1,0:T(8,128)(2,1)}, u32[]{:S(2)}, u32[]{:S(2)}) collective-permute-start(bf16[256,512]{1,0:T(8,128)(2,1)S(1)} %get-tuple-element.38.refs_0_.c0_hbm), channel_id=1, source_target_pairs={{0,2},{1,3},{2,0},{3,1},{4,6},{5,7},{6,4},{7,5},{8,10},{9,11},{10,... | collective-permute-start | bytes 786440 | tf_op jit(solution)/shard_map/ppermute | solution.py:419
  38.0 9.5 %shard_map.124 = (bf16[768,256]{1,0:T(8,128)(2,1)}, bf16[192,256]{1,0:T(8,128)(2,1)}, bf16[192,256]{1,0:T(8,128)(2,1)}, bf16[192,256]{1,0:T(8,128)(2,1)}, bf16[192,1024]{1,0:T(8,128)(2,1)}) custom-call(s32[1]{0:T(128)} %bitcast.2.bin_ref, bf16[208,512]{1,0:T(8,128)(2,1)} %copy-done.4, bf16[208,512]{1,0:T(8,128)(2,1)} %copy-done.10, ...), custom_call_target="tpu_custom_call" | custom-call | flops 1000 | bytes 100000000 | tf_op jit(solution)/shard_map/pallas_call | solution.py:159
  47.5 2.9 %collective-permute-start.3 = (bf16[192,512]{1,0:T(8,128)(2,1)S(1)}, bf16[192,512]{1,0:T(8,128)(2,1)S(1)}, u32[]{:S(2)}, u32[]{:S(2)}) collective-permute-start(bf16[192,512]{1,0:T(8,128)(2,1)S(1)} %get-tuple-element.39.c0_hbm), channel_id=1, source_target_pairs={{0,2},{1,3},{2,0},{3,1},{4,6},{5,7},{6,4},{7,5},{8,10},{9,11},{10,... | collective-permute-start | bytes 589832 | tf_op jit(solution)/shard_map/ppermute | solution.py:419
  50.4 0.9 collective-permute-start.4
  51.4 10.2 %collective-permute-done.9.refs_2_.c2_hbm = bf16[256,512]{1,0:T(8,128)(2,1)} collective-permute-done((bf16[256,512]{1,0:T(8,128)(2,1)S(1)}, bf16[256,512]{1,0:T(8,128)(2,1)}, u32[]{:S(2)}, u32[]{:S(2)}) %collective-permute-start.9) | collective-permute-done | bytes 262176 | tf_op jit(solution)/shard_map/ppermute | solution.py:419
  61.6 1.0 %copy-done.1 = bf16[768,256]{1,0:T(8,128)(2,1)S(1)} copy-done((bf16[768,256]{1,0:T(8,128)(2,1)S(1)}, bf16[768,256]{1,0:T(8,128)(2,1)}, u32[]{:S(2)}) %copy-start.1) | copy-done | bytes 393240
  62.6 1.9 %shard_map.128 = (bf16[128,512]{1,0:T(8,128)(2,1)S(1)}, bf16[128,512]{1,0:T(8,128)(2,1)S(1)}) custom-call(s32[1]{0:T(128)} %bitcast.6.core_ref, bf16[768,256]{1,0:T(8,128)(2,1)S(1)} %copy-done.1, bf16[256,512]{1,0:T(8,128)(2,1)S(1)} %get-tuple-element.38.refs_0_.c0_hbm, bf16[256,512]{1,0:T(8,128)(2,1)S(1)} %collective-permute-done.8.refs_1_.c1_hbm, ...), custom_call_target="tpu_custom_call" | custom-call | flops 1000 | bytes 1000 | tf_op jit(solution)/shard_map/pallas_call | solution.py:159
  64.5 1.0 %shard_map.126.refs_0_ = bf16[4,64,512]{2,1,0:T(8,128)(2,1)S(1)} custom-call(bf16[256,512]{1,0:T(8,128)(2,1)S(1)} %get-tuple-element.38.refs_0_.c0_hbm, bf16[256,512]{1,0:T(8,128)(2,1)S(1)} %collective-permute-done.8.refs_1_.c1_hbm, bf16[256,512]{1,0:T(8,128)(2,1)} %collective-permute-done.9.refs_2_.c2_hbm, ...), custom_call_target="tpu_custom_call" | custom-call | flops 1000 | bytes 1000 | tf_op jit(solution)/shard_map/pallas_call | solution.py:159
  65.6 1.6 %collective-permute-start.13 = (bf16[4,64,512]{2,1,0:T(8,128)(2,1)S(1)}, bf16[4,64,512]{2,1,0:T(8,128)(2,1)S(1)}, u32[]{:S(2)}, u32[]{:S(2)}) collective-permute-start(bf16[4,64,512]{2,1,0:T(8,128)(2,1)S(1)} %shard_map.126.refs_0_), channel_id=1, source_target_pairs={{0,8},{4,12},{8,0},{12,4},{16,24},{20,28},{24,16},{28,20},{1,9},{5... | collective-permute-start | bytes 786440 | tf_op jit(solution)/shard_map/ppermute | solution.py:423
  67.1 1.5 %collective-permute-start.15 = (bf16[4,64,512]{2,1,0:T(8,128)(2,1)S(1)}, bf16[4,64,512]{2,1,0:T(8,128)(2,1)S(1)}, u32[]{:S(2)}, u32[]{:S(2)}) collective-permute-start(bf16[4,64,512]{2,1,0:T(8,128)(2,1)S(1)} %shard_map.126.refs_0_), channel_id=1, source_target_pairs={{0,16},{4,20},{8,24},{12,28},{16,0},{20,4},{24,8},{28,12},{1,17},{... | collective-permute-start | bytes 786440 | tf_op jit(solution)/shard_map/ppermute | solution.py:423
  68.7 3.0 %collective-permute-start.7 = (bf16[192,256]{1,0:T(8,128)(2,1)S(1)}, bf16[192,256]{1,0:T(8,128)(2,1)S(1)}, u32[]{:S(2)}, u32[]{:S(2)}) collective-permute-start(bf16[192,256]{1,0:T(8,128)(2,1)S(1)} %copy-done.17), channel_id=1, source_target_pairs={{0,3},{1,2},{2,1},{3,0},{4,7},{5,6},{6,5},{7,4},{8,11},{9,10},{10,... | collective-permute-start | bytes 294920 | tf_op jit(solution)/shard_map/ppermute | solution.py:419
  72.4 1.6 %shard_map.129 = (bf16[128,512]{1,0:T(8,128)(2,1)S(1)}, bf16[128,512]{1,0:T(8,128)(2,1)S(1)}) custom-call(s32[1]{0:T(128)} %bitcast.6.core_ref, bf16[768,256]{1,0:T(8,128)(2,1)S(1)} %copy-done.2, bf16[192,512]{1,0:T(8,128)(2,1)S(1)} %get-tuple-element.39.c0_hbm, bf16[192,512]{1,0:T(8,128)(2,1)} %collective-permute-done.11.c1_hbm, ...), custom_call_target="tpu_custom_call" | custom-call | flops 1000 | bytes 1000 | tf_op jit(solution)/shard_map/pallas_call | solution.py:159
  74.6 1.7 %collective-permute-start.21 = (bf16[128,512]{1,0:T(8,128)(2,1)S(1)}, bf16[128,512]{1,0:T(8,128)(2,1)S(1)}, u32[]{:S(2)}, u32[]{:S(2)}) collective-permute-start(bf16[128,512]{1,0:T(8,128)(2,1)S(1)} %add_convert_fusion.3), channel_id=1, source_target_pairs={{0,16},{4,20},{8,24},{12,28},{16,0},{20,4},{24,8},{28,12},{1,17},{... | collective-permute-start | bytes 393224 | tf_op jit(solution)/shard_map/ppermute | solution.py:423
  76.3 1.5 %collective-permute-start.22 = (bf16[128,512]{1,0:T(8,128)(2,1)S(1)}, bf16[128,512]{1,0:T(8,128)(2,1)S(1)}, u32[]{:S(2)}, u32[]{:S(2)}) collective-permute-start(bf16[128,512]{1,0:T(8,128)(2,1)S(1)} %add_convert_fusion.3), channel_id=1, source_target_pairs={{0,24},{4,28},{8,16},{12,20},{16,8},{20,12},{24,0},{28,4},{1,25},{... | collective-permute-start | bytes 393224 | tf_op jit(solution)/shard_map/ppermute | solution.py:423
  77.8 1.5 %collective-permute-start.17 = (bf16[4,64,512]{2,1,0:T(8,128)(2,1)S(1)}, bf16[4,64,512]{2,1,0:T(8,128)(2,1)S(1)}, u32[]{:S(2)}, u32[]{:S(2)}) collective-permute-start(bf16[4,64,512]{2,1,0:T(8,128)(2,1)S(1)} %broadcast_select_fusion), channel_id=1, source_target_pairs={{0,16},{4,12},{8,24},{12,4},{16,0},{20,28},{24,8},{28,20},{1,17},{... | collective-permute-start | bytes 786440 | tf_op jit(solution)/shard_map/ppermute | solution.py:540
  80.1 1.4 %collective-permute-start.26 = (bf16[128,512]{1,0:T(8,128)(2,1)S(1)}, bf16[128,512]{1,0:T(8,128)(2,1)S(1)}, u32[]{:S(2)}, u32[]{:S(2)}) collective-permute-start(bf16[128,512]{1,0:T(8,128)(2,1)S(1)} %add_convert_fusion.1), channel_id=1, source_target_pairs={{0,16},{4,20},{8,24},{12,28},{16,0},{20,4},{24,8},{28,12},{1,17},{... | collective-permute-start | bytes 393224 | tf_op jit(solution)/shard_map/ppermute | solution.py:423
  81.5 2.1 %collective-permute-done.22 = bf16[128,512]{1,0:T(8,128)(2,1)S(1)} collective-permute-done((bf16[128,512]{1,0:T(8,128)(2,1)S(1)}, bf16[128,512]{1,0:T(8,128)(2,1)S(1)}, u32[]{:S(2)}, u32[]{:S(2)}) %collective-permute-start.22) | collective-permute-done | bytes 131104 | tf_op jit(solution)/shard_map/ppermute | solution.py:423
  83.6 1.6 %collective-permute-start.27 = (bf16[128,512]{1,0:T(8,128)(2,1)S(1)}, bf16[128,512]{1,0:T(8,128)(2,1)S(1)}, u32[]{:S(2)}, u32[]{:S(2)}) collective-permute-start(bf16[128,512]{1,0:T(8,128)(2,1)S(1)} %add_convert_fusion.1), channel_id=1, source_target_pairs={{0,24},{4,28},{8,16},{12,20},{16,8},{20,12},{24,0},{28,4},{1,25},{... | collective-permute-start | bytes 393224 | tf_op jit(solution)/shard_map/ppermute | solution.py:423
  86.0 1.2 %collective-permute-start.5 = (bf16[192,256]{1,0:T(8,128)(2,1)S(1)}, bf16[192,256]{1,0:T(8,128)(2,1)S(1)}, u32[]{:S(2)}, u32[]{:S(2)}) collective-permute-start(bf16[192,256]{1,0:T(8,128)(2,1)S(1)} %copy-done.15), channel_id=1, source_target_pairs={{0,1},{1,0},{2,3},{3,2},{4,5},{5,4},{6,7},{7,6},{8,9},{9,8},{10,11... | collective-permute-start | bytes 294920 | tf_op jit(solution)/shard_map/ppermute | solution.py:419
  87.2 2.3 %collective-permute-done.26 = bf16[128,512]{1,0:T(8,128)(2,1)S(1)} collective-permute-done((bf16[128,512]{1,0:T(8,128)(2,1)S(1)}, bf16[128,512]{1,0:T(8,128)(2,1)S(1)}, u32[]{:S(2)}, u32[]{:S(2)}) %collective-permute-start.26) | collective-permute-done | bytes 131104 | tf_op jit(solution)/shard_map/ppermute | solution.py:423
  89.5 1.4 %collective-permute-done.27 = bf16[128,512]{1,0:T(8,128)(2,1)S(1)} collective-permute-done((bf16[128,512]{1,0:T(8,128)(2,1)S(1)}, bf16[128,512]{1,0:T(8,128)(2,1)S(1)}, u32[]{:S(2)}, u32[]{:S(2)}) %collective-permute-start.27) | collective-permute-done | bytes 131104 | tf_op jit(solution)/shard_map/ppermute | solution.py:423
  91.5 0.9 collective-permute-start.23
  93.0 3.0 %shard_map.127 = bf16[192,1024]{1,0:T(8,128)(2,1)} custom-call(s32[1]{0:T(128)} %bitcast.clip_ref, s32[1]{0:T(128)} %bitcast.8.count_ref, bf16[192,1024]{1,0:T(8,128)(2,1)S(1)} %copy-done.7, bf16[768,256]{1,0:T(8,128)(2,1)S(1)} %copy-done.2, bf16[192,256]{1,0:T(8,128)(2,1)S(1)} %collective-permute-done.5.a1_hbm, ...), custom_call_target="tpu_custom_call" | custom-call | flops 1000 | bytes 1000 | tf_op jit(solution)/shard_map/pallas_call | solution.py:159
  96.0 1.1 %shard_map.130 = f32[256,1024]{1,0:T(8,128)} custom-call(s32[1]{0:T(128)} %bitcast.6.core_ref, bf16[128,512]{1,0:T(8,128)(2,1)S(1)} %add_convert_fusion.2.refs_0_, bf16[128,512]{1,0:T(8,128)(2,1)S(1)} %collective-permute-done.23.refs_1_, bf16[128,512]{1,0:T(8,128)(2,1)S(1)} %add_convert_fusion.refs_2_, bf16[128,512]{1,0:T(8,128)(2,1)S(1)} %collective-permute-done.28.refs_3_), custom_call_target="tpu_custom_call" | custom-call | flops 1000 | bytes 1000 | tf_op jit(solution)/shard_map/pallas_call | solution.py:159
  (78 shorter events, 8.5 us)
Async XLA Ops:
  2.9 12.1 %collective-permute-start = (bf16[208,512]{1,0:T(8,128)(2,1)S(1)}, bf16[208,512]{1,0:T(8,128)(2,1)S(1)}, u32[]{:S(2)}, u32[]{:S(2)}) collective-permute-start(bf16[208,512]{1,0:T(8,128)(2,1)S(1)} %shard_map.122.p0_hbm), channel_id=1, source_target_pairs={{0,1},{1,0},{2,3},{3,2},{4,5},{5,4},{6,7},{7,6},{8,9},{9,8},{10,11... | collective-permute-start | bytes 638984 | tf_op jit(solution)/shard_map/ppermute | solution.py:419
  6.0 18.2 %collective-permute-start.1 = (bf16[208,512]{1,0:T(8,128)(2,1)S(1)}, bf16[208,512]{1,0:T(8,128)(2,1)S(1)}, u32[]{:S(2)}, u32[]{:S(2)}) collective-permute-start(bf16[208,512]{1,0:T(8,128)(2,1)S(1)} %shard_map.122.p0_hbm), channel_id=1, source_target_pairs={{0,2},{1,3},{2,0},{3,1},{4,6},{5,7},{6,4},{7,5},{8,10},{9,11},{10,... | collective-permute-start | bytes 638984 | tf_op jit(solution)/shard_map/ppermute | solution.py:419
  8.6 16.4 %collective-permute-start.2 = (bf16[208,512]{1,0:T(8,128)(2,1)S(1)}, bf16[208,512]{1,0:T(8,128)(2,1)S(1)}, u32[]{:S(2)}, u32[]{:S(2)}) collective-permute-start(bf16[208,512]{1,0:T(8,128)(2,1)S(1)} %shard_map.122.p0_hbm), channel_id=1, source_target_pairs={{0,3},{1,2},{2,1},{3,0},{4,7},{5,6},{6,5},{7,4},{8,11},{9,10},{10,... | collective-permute-start | bytes 638984 | tf_op jit(solution)/shard_map/ppermute | solution.py:419
  15.7 21.6 %collective-permute-start.8 = (bf16[256,512]{1,0:T(8,128)(2,1)S(1)}, bf16[256,512]{1,0:T(8,128)(2,1)S(1)}, u32[]{:S(2)}, u32[]{:S(2)}) collective-permute-start(bf16[256,512]{1,0:T(8,128)(2,1)S(1)} %get-tuple-element.38.refs_0_.c0_hbm), channel_id=1, source_target_pairs={{0,1},{1,0},{2,3},{3,2},{4,5},{5,4},{6,7},{7,6},{8,9},{9,8},{10,11... | collective-permute-start | bytes 786440 | tf_op jit(solution)/shard_map/ppermute | solution.py:419
  25.0 12.4 %copy-start.12 = (bf16[208,512]{1,0:T(8,128)(2,1)}, bf16[208,512]{1,0:T(8,128)(2,1)S(1)}, u32[]{:S(2)}) copy-start(bf16[208,512]{1,0:T(8,128)(2,1)S(1)} %collective-permute-done.2.p3_hbm) | copy-start | bytes 638980
  25.0 26.4 %collective-permute-start.10 = (bf16[256,512]{1,0:T(8,128)(2,1)S(1)}, bf16[256,512]{1,0:T(8,128)(2,1)S(1)}, u32[]{:S(2)}, u32[]{:S(2)}) collective-permute-start(bf16[256,512]{1,0:T(8,128)(2,1)S(1)} %get-tuple-element.38.refs_0_.c0_hbm), channel_id=1, source_target_pairs={{0,3},{1,2},{2,1},{3,0},{4,7},{5,6},{6,5},{7,4},{8,11},{9,10},{10,... | collective-permute-start | bytes 786440 | tf_op jit(solution)/shard_map/ppermute | solution.py:419
  27.4 34.1 %collective-permute-start.9 = (bf16[256,512]{1,0:T(8,128)(2,1)S(1)}, bf16[256,512]{1,0:T(8,128)(2,1)}, u32[]{:S(2)}, u32[]{:S(2)}) collective-permute-start(bf16[256,512]{1,0:T(8,128)(2,1)S(1)} %get-tuple-element.38.refs_0_.c0_hbm), channel_id=1, source_target_pairs={{0,2},{1,3},{2,0},{3,1},{4,6},{5,7},{6,4},{7,5},{8,10},{9,11},{10,... | collective-permute-start | bytes 786440 | tf_op jit(solution)/shard_map/ppermute | solution.py:419
  37.4 28.2 %collective-permute-start.11 = (bf16[192,512]{1,0:T(8,128)(2,1)S(1)}, bf16[192,512]{1,0:T(8,128)(2,1)}, u32[]{:S(2)}, u32[]{:S(2)}) collective-permute-start(bf16[192,512]{1,0:T(8,128)(2,1)S(1)} %get-tuple-element.39.c0_hbm), channel_id=1, source_target_pairs={{0,1},{1,0},{2,3},{3,2},{4,5},{5,4},{6,7},{7,6},{8,9},{9,8},{10,11... | collective-permute-start | bytes 589832 | tf_op jit(solution)/shard_map/ppermute | solution.py:419
  47.5 21.1 %collective-permute-start.3 = (bf16[192,512]{1,0:T(8,128)(2,1)S(1)}, bf16[192,512]{1,0:T(8,128)(2,1)S(1)}, u32[]{:S(2)}, u32[]{:S(2)}) collective-permute-start(bf16[192,512]{1,0:T(8,128)(2,1)S(1)} %get-tuple-element.39.c0_hbm), channel_id=1, source_target_pairs={{0,2},{1,3},{2,0},{3,1},{4,6},{5,7},{6,4},{7,5},{8,10},{9,11},{10,... | collective-permute-start | bytes 589832 | tf_op jit(solution)/shard_map/ppermute | solution.py:419
  50.4 18.2 %collective-permute-start.4 = (bf16[192,512]{1,0:T(8,128)(2,1)S(1)}, bf16[192,512]{1,0:T(8,128)(2,1)S(1)}, u32[]{:S(2)}, u32[]{:S(2)}) collective-permute-start(bf16[192,512]{1,0:T(8,128)(2,1)S(1)} %get-tuple-element.39.c0_hbm), channel_id=1, source_target_pairs={{0,3},{1,2},{2,1},{3,0},{4,7},{5,6},{6,5},{7,4},{8,11},{9,10},{10,... | collective-permute-start | bytes 589832 | tf_op jit(solution)/shard_map/ppermute | solution.py:419
  64.4 7.2 %collective-permute-start.19 = (bf16[128,512]{1,0:T(8,128)(2,1)S(1)}, bf16[128,512]{1,0:T(8,128)(2,1)S(1)}, u32[]{:S(2)}, u32[]{:S(2)}) collective-permute-start(bf16[128,512]{1,0:T(8,128)(2,1)S(1)} %get-tuple-element.44), channel_id=1, source_target_pairs={{0,4},{4,0},{8,12},{12,8},{16,20},{20,16},{24,28},{28,24},{1,5},{5... | collective-permute-start | bytes 393224 | tf_op jit(solution)/shard_map/ppermute | solution.py:423
  65.6 9.0 %collective-permute-start.13 = (bf16[4,64,512]{2,1,0:T(8,128)(2,1)S(1)}, bf16[4,64,512]{2,1,0:T(8,128)(2,1)S(1)}, u32[]{:S(2)}, u32[]{:S(2)}) collective-permute-start(bf16[4,64,512]{2,1,0:T(8,128)(2,1)S(1)} %shard_map.126.refs_0_), channel_id=1, source_target_pairs={{0,8},{4,12},{8,0},{12,4},{16,24},{20,28},{24,16},{28,20},{1,9},{5... | collective-permute-start | bytes 786440 | tf_op jit(solution)/shard_map/ppermute | solution.py:423
  67.1 9.1 %collective-permute-start.15 = (bf16[4,64,512]{2,1,0:T(8,128)(2,1)S(1)}, bf16[4,64,512]{2,1,0:T(8,128)(2,1)S(1)}, u32[]{:S(2)}, u32[]{:S(2)}) collective-permute-start(bf16[4,64,512]{2,1,0:T(8,128)(2,1)S(1)} %shard_map.126.refs_0_), channel_id=1, source_target_pairs={{0,16},{4,20},{8,24},{12,28},{16,0},{20,4},{24,8},{28,12},{1,17},{... | collective-permute-start | bytes 786440 | tf_op jit(solution)/shard_map/ppermute | solution.py:423
  68.7 7.6 %collective-permute-start.7 = (bf16[192,256]{1,0:T(8,128)(2,1)S(1)}, bf16[192,256]{1,0:T(8,128)(2,1)S(1)}, u32[]{:S(2)}, u32[]{:S(2)}) collective-permute-start(bf16[192,256]{1,0:T(8,128)(2,1)S(1)} %copy-done.17), channel_id=1, source_target_pairs={{0,3},{1,2},{2,1},{3,0},{4,7},{5,6},{6,5},{7,4},{8,11},{9,10},{10,... | collective-permute-start | bytes 294920 | tf_op jit(solution)/shard_map/ppermute | solution.py:419
  71.7 7.7 %collective-permute-start.6 = (bf16[192,256]{1,0:T(8,128)(2,1)S(1)}, bf16[192,256]{1,0:T(8,128)(2,1)S(1)}, u32[]{:S(2)}, u32[]{:S(2)}) collective-permute-start(bf16[192,256]{1,0:T(8,128)(2,1)S(1)} %copy-done.16), channel_id=1, source_target_pairs={{0,2},{1,3},{2,0},{3,1},{4,6},{5,7},{6,4},{7,5},{8,10},{9,11},{10,... | collective-permute-start | bytes 294920 | tf_op jit(solution)/shard_map/ppermute | solution.py:419
  71.7 14.3 %copy-start.15 = (bf16[192,256]{1,0:T(8,128)(2,1)S(1)}, bf16[192,256]{1,0:T(8,128)(2,1)}, u32[]{:S(2)}) copy-start(bf16[192,256]{1,0:T(8,128)(2,1)} %get-tuple-element.30) | copy-start | bytes 294916
  71.7 21.3 %copy-start.7 = (bf16[192,1024]{1,0:T(8,128)(2,1)S(1)}, bf16[192,1024]{1,0:T(8,128)(2,1)}, u32[]{:S(2)}) copy-start(bf16[192,1024]{1,0:T(8,128)(2,1)} %get-tuple-element.25.hidden_hbm) | copy-start | bytes 1179652
  71.8 7.7 %collective-permute-start.20 = (bf16[128,512]{1,0:T(8,128)(2,1)S(1)}, bf16[128,512]{1,0:T(8,128)(2,1)S(1)}, u32[]{:S(2)}, u32[]{:S(2)}) collective-permute-start(bf16[128,512]{1,0:T(8,128)(2,1)S(1)} %add_convert_fusion.3), channel_id=1, source_target_pairs={{0,8},{4,12},{8,0},{12,4},{16,24},{20,28},{24,16},{28,20},{1,9},{5... | collective-permute-start | bytes 393224 | tf_op jit(solution)/shard_map/ppermute | solution.py:423
  74.6 5.5 %collective-permute-start.21 = (bf16[128,512]{1,0:T(8,128)(2,1)S(1)}, bf16[128,512]{1,0:T(8,128)(2,1)S(1)}, u32[]{:S(2)}, u32[]{:S(2)}) collective-permute-start(bf16[128,512]{1,0:T(8,128)(2,1)S(1)} %add_convert_fusion.3), channel_id=1, source_target_pairs={{0,16},{4,20},{8,24},{12,28},{16,0},{20,4},{24,8},{28,12},{1,17},{... | collective-permute-start | bytes 393224 | tf_op jit(solution)/shard_map/ppermute | solution.py:423
  76.3 1.5 %collective-permute-start.24 = (bf16[128,512]{1,0:T(8,128)(2,1)S(1)}, bf16[128,512]{1,0:T(8,128)(2,1)S(1)}, u32[]{:S(2)}, u32[]{:S(2)}) collective-permute-start(bf16[128,512]{1,0:T(8,128)(2,1)S(1)} %get-tuple-element.46), channel_id=1, source_target_pairs={{0,4},{4,0},{8,12},{12,8},{16,20},{20,16},{24,28},{28,24},{1,5},{5... | collective-permute-start | bytes 393224 | tf_op jit(solution)/shard_map/ppermute | solution.py:423
  76.3 7.3 %collective-permute-start.22 = (bf16[128,512]{1,0:T(8,128)(2,1)S(1)}, bf16[128,512]{1,0:T(8,128)(2,1)S(1)}, u32[]{:S(2)}, u32[]{:S(2)}) collective-permute-start(bf16[128,512]{1,0:T(8,128)(2,1)S(1)} %add_convert_fusion.3), channel_id=1, source_target_pairs={{0,24},{4,28},{8,16},{12,20},{16,8},{20,12},{24,0},{28,4},{1,25},{... | collective-permute-start | bytes 393224 | tf_op jit(solution)/shard_map/ppermute | solution.py:423
  77.8 13.6 %collective-permute-start.17 = (bf16[4,64,512]{2,1,0:T(8,128)(2,1)S(1)}, bf16[4,64,512]{2,1,0:T(8,128)(2,1)S(1)}, u32[]{:S(2)}, u32[]{:S(2)}) collective-permute-start(bf16[4,64,512]{2,1,0:T(8,128)(2,1)S(1)} %broadcast_select_fusion), channel_id=1, source_target_pairs={{0,16},{4,12},{8,24},{12,4},{16,0},{20,28},{24,8},{28,20},{1,17},{... | collective-permute-start | bytes 786440 | tf_op jit(solution)/shard_map/ppermute | solution.py:540
  79.4 13.0 %collective-permute-start.12 = (bf16[4,64,512]{2,1,0:T(8,128)(2,1)S(1)}, bf16[4,64,512]{2,1,0:T(8,128)(2,1)S(1)}, u32[]{:S(2)}, u32[]{:S(2)}) collective-permute-start(bf16[4,64,512]{2,1,0:T(8,128)(2,1)S(1)} %shard_map.126.refs_0_), channel_id=1, source_target_pairs={{0,4},{4,0},{8,12},{12,8},{16,20},{20,16},{24,28},{28,24},{1,5},{5... | collective-permute-start | bytes 786440 | tf_op jit(solution)/shard_map/ppermute | solution.py:423
  79.5 6.5 %collective-permute-start.25 = (bf16[128,512]{1,0:T(8,128)(2,1)S(1)}, bf16[128,512]{1,0:T(8,128)(2,1)S(1)}, u32[]{:S(2)}, u32[]{:S(2)}) collective-permute-start(bf16[128,512]{1,0:T(8,128)(2,1)S(1)} %add_convert_fusion.1), channel_id=1, source_target_pairs={{0,8},{4,12},{8,0},{12,4},{16,24},{20,28},{24,16},{28,20},{1,9},{5... | collective-permute-start | bytes 393224 | tf_op jit(solution)/shard_map/ppermute | solution.py:423
  80.1 9.4 %collective-permute-start.26 = (bf16[128,512]{1,0:T(8,128)(2,1)S(1)}, bf16[128,512]{1,0:T(8,128)(2,1)S(1)}, u32[]{:S(2)}, u32[]{:S(2)}) collective-permute-start(bf16[128,512]{1,0:T(8,128)(2,1)S(1)} %add_convert_fusion.1), channel_id=1, source_target_pairs={{0,16},{4,20},{8,24},{12,28},{16,0},{20,4},{24,8},{28,12},{1,17},{... | collective-permute-start | bytes 393224 | tf_op jit(solution)/shard_map/ppermute | solution.py:423
  83.6 7.3 %collective-permute-start.27 = (bf16[128,512]{1,0:T(8,128)(2,1)S(1)}, bf16[128,512]{1,0:T(8,128)(2,1)S(1)}, u32[]{:S(2)}, u32[]{:S(2)}) collective-permute-start(bf16[128,512]{1,0:T(8,128)(2,1)S(1)} %add_convert_fusion.1), channel_id=1, source_target_pairs={{0,24},{4,28},{8,16},{12,20},{16,8},{20,12},{24,0},{28,4},{1,25},{... | collective-permute-start | bytes 393224 | tf_op jit(solution)/shard_map/ppermute | solution.py:423
  86.0 5.5 %collective-permute-start.5 = (bf16[192,256]{1,0:T(8,128)(2,1)S(1)}, bf16[192,256]{1,0:T(8,128)(2,1)S(1)}, u32[]{:S(2)}, u32[]{:S(2)}) collective-permute-start(bf16[192,256]{1,0:T(8,128)(2,1)S(1)} %copy-done.15), channel_id=1, source_target_pairs={{0,1},{1,0},{2,3},{3,2},{4,5},{5,4},{6,7},{7,6},{8,9},{9,8},{10,11... | collective-permute-start | bytes 294920 | tf_op jit(solution)/shard_map/ppermute | solution.py:419
  89.5 2.9 %collective-permute-start.14 = (bf16[4,64,512]{2,1,0:T(8,128)(2,1)S(1)}, bf16[4,64,512]{2,1,0:T(8,128)(2,1)S(1)}, u32[]{:S(2)}, u32[]{:S(2)}) collective-permute-start(bf16[4,64,512]{2,1,0:T(8,128)(2,1)S(1)} %collective-permute-done.13.refs_2_), channel_id=1, source_target_pairs={{0,4},{4,0},{8,12},{12,8},{16,20},{20,16},{24,28},{28,24},{1,5},{5... | collective-permute-start | bytes 786440 | tf_op jit(solution)/shard_map/ppermute | solution.py:423
  90.9 1.7 %collective-permute-start.16 = (bf16[4,64,512]{2,1,0:T(8,128)(2,1)S(1)}, bf16[4,64,512]{2,1,0:T(8,128)(2,1)S(1)}, u32[]{:S(2)}, u32[]{:S(2)}) collective-permute-start(bf16[4,64,512]{2,1,0:T(8,128)(2,1)S(1)} %collective-permute-done.15.refs_4_), channel_id=1, source_target_pairs={{0,4},{4,0},{8,12},{12,8},{16,20},{20,16},{24,28},{28,24},{1,5},{5... | collective-permute-start | bytes 786440 | tf_op jit(solution)/shard_map/ppermute | solution.py:423
  91.5 1.5 %collective-permute-start.18 = (bf16[4,64,512]{2,1,0:T(8,128)(2,1)S(1)}, bf16[4,64,512]{2,1,0:T(8,128)(2,1)S(1)}, u32[]{:S(2)}, u32[]{:S(2)}) collective-permute-start(bf16[4,64,512]{2,1,0:T(8,128)(2,1)S(1)} %collective-permute-done.17.refs_6_), channel_id=1, source_target_pairs={{0,4},{4,0},{8,12},{12,8},{16,20},{20,16},{24,28},{28,24},{1,5},{5... | collective-permute-start | bytes 786440 | tf_op jit(solution)/shard_map/ppermute | solution.py:423
  91.5 4.5 %collective-permute-start.23 = (bf16[128,512]{1,0:T(8,128)(2,1)S(1)}, bf16[128,512]{1,0:T(8,128)(2,1)S(1)}, u32[]{:S(2)}, u32[]{:S(2)}) collective-permute-start(bf16[128,512]{1,0:T(8,128)(2,1)S(1)} %add_convert_fusion.2.refs_0_), channel_id=1, source_target_pairs={{0,4},{4,0},{8,12},{12,8},{16,20},{20,16},{24,28},{28,24},{1,5},{5... | collective-permute-start | bytes 393224 | tf_op jit(solution)/shard_map/ppermute | solution.py:423
  92.5 3.6 %collective-permute-start.28 = (bf16[128,512]{1,0:T(8,128)(2,1)S(1)}, bf16[128,512]{1,0:T(8,128)(2,1)S(1)}, u32[]{:S(2)}, u32[]{:S(2)}) collective-permute-start(bf16[128,512]{1,0:T(8,128)(2,1)S(1)} %add_convert_fusion.refs_2_), channel_id=1, source_target_pairs={{0,4},{4,0},{8,12},{12,8},{16,20},{20,16},{24,28},{28,24},{1,5},{5... | collective-permute-start | bytes 393224 | tf_op jit(solution)/shard_map/ppermute | solution.py:423
  (15 other events, 68.2 us)

commit v4 on v3

--- a/solution.py
+++ b/solution.py
@@ -532,7 +532,7 @@
         scratch=[dma((4,))],
         limit=4,
     )
-    pieces = after(pieces, d1)
+    pieces = after(pieces, d1, d2)
     held = {0: pieces}
     held[2], held[4] = along_clip(pieces, 2), along_clip(pieces, 4)
     onward = jnp.where(core == 0, held[2], held[4])

time: 97.4 us -> 95.8 us (0.984)
  starting transfers between devices: 40.3 us -> 37.8 us
    ppermute x12, starting transfers between devices: 26.7 us -> 22 us  [along_tm(): return lax.ppermute(array, 'tm', [(i, i ^ flip) for i in range(4)])]
    ppermute x12, waiting for transfers between devices: 20.8 us -> 25 us  [along_tm(): return lax.ppermute(array, 'tm', [(i, i ^ flip) for i in range(4)])]
    ppermute x16, waiting for transfers between devices: 7.73 us -> 3.68 us  [along_clip(): return lax.ppermute(array, 'clip', [(i, i ^ flip) for i in range(8)])]
    ppermute x16, starting transfers between devices: 12 us -> 14.4 us  [along_clip(): return lax.ppermute(array, 'clip', [(i, i ^ flip) for i in range(8)])]
where the time goes in v4:
time: 95.8 us; the launch traced here: 95.2 us
  starting transfers between devices  37.8 us (39%)
  waiting for transfers between devices  28.7 us (30%)
  Pallas kernels  18.5 us (19%)
  local copies, waits for them, and re-layouts  8.47 us (9%)
  between operations  1.5 us (2%)
    ppermute x12, waiting for transfers between devices, along_tm(): return lax.ppermute(array, 'tm', [(i, i ^ flip) for i in range(4)])  25 us
    ppermute x12, starting transfers between devices, along_tm(): return lax.ppermute(array, 'tm', [(i, i ^ flip) for i in range(4)])  22 us
    pallas_call x9, Pallas kernels, local_call(): pl.pallas_call(kernel, out_shape=out_shape, in_specs=specs, out_specs=[pl...  18.5 us
    ppermute x16, starting transfers between devices, along_clip(): return lax.ppermute(array, 'clip', [(i, i ^ flip) for i in range(8)])  14.4 us
    unnamed x36, local copies, waits for them, and re-layouts  7.28 us
    ppermute x16, waiting for transfers between devices, along_clip(): return lax.ppermute(array, 'clip', [(i, i ^ flip) for i in range(8)])  3.68 us
  transfers between devices with their start and end apart: 29, of which 10 were waited for; matrix products, arithmetic and copies ran while one was open for 1% of the time, Pallas kernels for 18%

profile of v4, /device:TPU:0, one launch (start us, length us, event | category | flops | bytes accessed | tf_op | source)
XLA Modules:
  0.0 95.2 jit_solution(18354075065551203086)
XLA Ops:
  2.9 3.1 %collective-permute-start = (bf16[208,512]{1,0:T(8,128)(2,1)S(1)}, bf16[208,512]{1,0:T(8,128)(2,1)S(1)}, u32[]{:S(2)}, u32[]{:S(2)}) collective-permute-start(bf16[208,512]{1,0:T(8,128)(2,1)S(1)} %shard_map.122.p0_hbm), channel_id=1, source_target_pairs={{0,1},{1,0},{2,3},{3,2},{4,5},{5,4},{6,7},{7,6},{8,9},{9,8},{10,11... | collective-permute-start | bytes 638984 | tf_op jit(solution)/shard_map/ppermute | solution.py:419
  6.0 2.6 %collective-permute-start.1 = (bf16[208,512]{1,0:T(8,128)(2,1)S(1)}, bf16[208,512]{1,0:T(8,128)(2,1)S(1)}, u32[]{:S(2)}, u32[]{:S(2)}) collective-permute-start(bf16[208,512]{1,0:T(8,128)(2,1)S(1)} %shard_map.122.p0_hbm), channel_id=1, source_target_pairs={{0,2},{1,3},{2,0},{3,1},{4,6},{5,7},{6,4},{7,5},{8,10},{9,11},{10,... | collective-permute-start | bytes 638984 | tf_op jit(solution)/shard_map/ppermute | solution.py:419
  8.6 1.4 %copy-done.3 = bf16[1024,768]{1,0:T(8,128)(2,1)S(1)} copy-done((bf16[1024,768]{1,0:T(8,128)(2,1)S(1)}, bf16[1024,768]{1,0:T(8,128)(2,1)}, u32[]{:S(2)}) %copy-start.3) | copy-done | bytes 1572888
  10.6 1.2 %copy-done = bf16[1024,768]{1,0:T(8,128)(2,1)} copy-done((bf16[1024,768]{1,0:T(8,128)(2,1)}, bf16[1024,768]{1,0:T(8,128)(2,1)S(1)}, u32[]{:S(2)}) %copy-start) | copy-done | bytes 1572888
  13.0 2.1 %collective-permute-done.p1_hbm = bf16[208,512]{1,0:T(8,128)(2,1)S(1)} collective-permute-done((bf16[208,512]{1,0:T(8,128)(2,1)S(1)}, bf16[208,512]{1,0:T(8,128)(2,1)S(1)}, u32[]{:S(2)}, u32[]{:S(2)}) %collective-permute-start) | collective-permute-done | bytes 213024 | tf_op jit(solution)/shard_map/ppermute | solution.py:419
  15.7 8.5 %collective-permute-done.1.p2_hbm = bf16[208,512]{1,0:T(8,128)(2,1)S(1)} collective-permute-done((bf16[208,512]{1,0:T(8,128)(2,1)S(1)}, bf16[208,512]{1,0:T(8,128)(2,1)S(1)}, u32[]{:S(2)}, u32[]{:S(2)}) %collective-permute-start.1) | collective-permute-done | bytes 213024 | tf_op jit(solution)/shard_map/ppermute | solution.py:419
  25.7 2.5 %collective-permute-start.10 = (bf16[256,512]{1,0:T(8,128)(2,1)S(1)}, bf16[256,512]{1,0:T(8,128)(2,1)S(1)}, u32[]{:S(2)}, u32[]{:S(2)}) collective-permute-start(bf16[256,512]{1,0:T(8,128)(2,1)S(1)} %get-tuple-element.38.refs_0_.c0_hbm), channel_id=1, source_target_pairs={{0,3},{1,2},{2,1},{3,0},{4,7},{5,6},{6,5},{7,4},{8,11},{9,10},{10,... | collective-permute-start | bytes 786440 | tf_op jit(solution)/shard_map/ppermute | solution.py:419
  28.1 4.4 %collective-permute-start.9 = (bf16[256,512]{1,0:T(8,128)(2,1)S(1)}, bf16[256,512]{1,0:T(8,128)(2,1)}, u32[]{:S(2)}, u32[]{:S(2)}) collective-permute-start(bf16[256,512]{1,0:T(8,128)(2,1)S(1)} %get-tuple-element.38.refs_0_.c0_hbm), channel_id=1, source_target_pairs={{0,2},{1,3},{2,0},{3,1},{4,6},{5,7},{6,4},{7,5},{8,10},{9,11},{10,... | collective-permute-start | bytes 786440 | tf_op jit(solution)/shard_map/ppermute | solution.py:419
  32.6 9.5 %shard_map.124 = (bf16[768,256]{1,0:T(8,128)(2,1)}, bf16[192,256]{1,0:T(8,128)(2,1)}, bf16[192,256]{1,0:T(8,128)(2,1)}, bf16[192,256]{1,0:T(8,128)(2,1)}, bf16[192,1024]{1,0:T(8,128)(2,1)}) custom-call(s32[1]{0:T(128)} %bitcast.2.bin_ref, bf16[208,512]{1,0:T(8,128)(2,1)} %copy-done.4, bf16[208,512]{1,0:T(8,128)(2,1)} %copy-done.10, ...), custom_call_target="tpu_custom_call" | custom-call | flops 1000 | bytes 100000000 | tf_op jit(solution)/shard_map/pallas_call | solution.py:159
  42.2 3.5 %collective-permute-start.11 = (bf16[192,512]{1,0:T(8,128)(2,1)S(1)}, bf16[192,512]{1,0:T(8,128)(2,1)S(1)}, u32[]{:S(2)}, u32[]{:S(2)}) collective-permute-start(bf16[192,512]{1,0:T(8,128)(2,1)S(1)} %get-tuple-element.39.c0_hbm), channel_id=1, source_target_pairs={{0,1},{1,0},{2,3},{3,2},{4,5},{5,4},{6,7},{7,6},{8,9},{9,8},{10,11... | collective-permute-start | bytes 589832 | tf_op jit(solution)/shard_map/ppermute | solution.py:419
  46.5 12.9 %collective-permute-done.9.refs_2_.c2_hbm = bf16[256,512]{1,0:T(8,128)(2,1)} collective-permute-done((bf16[256,512]{1,0:T(8,128)(2,1)S(1)}, bf16[256,512]{1,0:T(8,128)(2,1)}, u32[]{:S(2)}, u32[]{:S(2)}) %collective-permute-start.9) | collective-permute-done | bytes 262176 | tf_op jit(solution)/shard_map/ppermute | solution.py:419
  59.4 1.0 %copy-done.1 = bf16[768,256]{1,0:T(8,128)(2,1)S(1)} copy-done((bf16[768,256]{1,0:T(8,128)(2,1)S(1)}, bf16[768,256]{1,0:T(8,128)(2,1)}, u32[]{:S(2)}) %copy-start.1) | copy-done | bytes 393240
  60.4 1.9 %shard_map.128 = (bf16[128,512]{1,0:T(8,128)(2,1)S(1)}, bf16[128,512]{1,0:T(8,128)(2,1)S(1)}) custom-call(s32[1]{0:T(128)} %bitcast.6.core_ref, bf16[768,256]{1,0:T(8,128)(2,1)S(1)} %copy-done.1, bf16[256,512]{1,0:T(8,128)(2,1)S(1)} %get-tuple-element.38.refs_0_.c0_hbm, bf16[256,512]{1,0:T(8,128)(2,1)S(1)} %collective-permute-done.8.refs_1_.c1_hbm, ...), custom_call_target="tpu_custom_call" | custom-call | flops 1000 | bytes 1000 | tf_op jit(solution)/shard_map/pallas_call | solution.py:159
  62.4 1.0 %shard_map.126.refs_0_ = bf16[4,64,512]{2,1,0:T(8,128)(2,1)S(1)} custom-call(bf16[256,512]{1,0:T(8,128)(2,1)S(1)} %get-tuple-element.38.refs_0_.c0_hbm, bf16[256,512]{1,0:T(8,128)(2,1)S(1)} %collective-permute-done.8.refs_1_.c1_hbm, bf16[256,512]{1,0:T(8,128)(2,1)} %collective-permute-done.9.refs_2_.c2_hbm, ...), custom_call_target="tpu_custom_call" | custom-call | flops 1000 | bytes 1000 | tf_op jit(solution)/shard_map/pallas_call | solution.py:159
  63.5 1.5 %collective-permute-start.13 = (bf16[4,64,512]{2,1,0:T(8,128)(2,1)S(1)}, bf16[4,64,512]{2,1,0:T(8,128)(2,1)S(1)}, u32[]{:S(2)}, u32[]{:S(2)}) collective-permute-start(bf16[4,64,512]{2,1,0:T(8,128)(2,1)S(1)} %shard_map.126.refs_0_), channel_id=1, source_target_pairs={{0,8},{4,12},{8,0},{12,4},{16,24},{20,28},{24,16},{28,20},{1,9},{5... | collective-permute-start | bytes 786440 | tf_op jit(solution)/shard_map/ppermute | solution.py:423
  65.0 1.5 %collective-permute-start.15 = (bf16[4,64,512]{2,1,0:T(8,128)(2,1)S(1)}, bf16[4,64,512]{2,1,0:T(8,128)(2,1)S(1)}, u32[]{:S(2)}, u32[]{:S(2)}) collective-permute-start(bf16[4,64,512]{2,1,0:T(8,128)(2,1)S(1)} %shard_map.126.refs_0_), channel_id=1, source_target_pairs={{0,16},{4,20},{8,24},{12,28},{16,0},{20,4},{24,8},{28,12},{1,17},{... | collective-permute-start | bytes 786440 | tf_op jit(solution)/shard_map/ppermute | solution.py:423
  66.5 1.8 %collective-permute-start.7 = (bf16[192,256]{1,0:T(8,128)(2,1)S(1)}, bf16[192,256]{1,0:T(8,128)(2,1)S(1)}, u32[]{:S(2)}, u32[]{:S(2)}) collective-permute-start(bf16[192,256]{1,0:T(8,128)(2,1)S(1)} %copy-done.17), channel_id=1, source_target_pairs={{0,3},{1,2},{2,1},{3,0},{4,7},{5,6},{6,5},{7,4},{8,11},{9,10},{10,... | collective-permute-start | bytes 294920 | tf_op jit(solution)/shard_map/ppermute | solution.py:419
  68.3 1.3 %collective-permute-start.6 = (bf16[192,256]{1,0:T(8,128)(2,1)S(1)}, bf16[192,256]{1,0:T(8,128)(2,1)S(1)}, u32[]{:S(2)}, u32[]{:S(2)}) collective-permute-start(bf16[192,256]{1,0:T(8,128)(2,1)S(1)} %copy-done.16), channel_id=1, source_target_pairs={{0,2},{1,3},{2,0},{3,1},{4,6},{5,7},{6,4},{7,5},{8,10},{9,11},{10,... | collective-permute-start | bytes 294920 | tf_op jit(solution)/shard_map/ppermute | solution.py:419
  69.7 1.6 %collective-permute-start.20 = (bf16[128,512]{1,0:T(8,128)(2,1)S(1)}, bf16[128,512]{1,0:T(8,128)(2,1)S(1)}, u32[]{:S(2)}, u32[]{:S(2)}) collective-permute-start(bf16[128,512]{1,0:T(8,128)(2,1)S(1)} %add_convert_fusion.3), channel_id=1, source_target_pairs={{0,8},{4,12},{8,0},{12,4},{16,24},{20,28},{24,16},{28,20},{1,9},{5... | collective-permute-start | bytes 393224 | tf_op jit(solution)/shard_map/ppermute | solution.py:423
  71.2 1.5 %shard_map.129 = (bf16[128,512]{1,0:T(8,128)(2,1)S(1)}, bf16[128,512]{1,0:T(8,128)(2,1)S(1)}) custom-call(s32[1]{0:T(128)} %bitcast.6.core_ref, bf16[768,256]{1,0:T(8,128)(2,1)S(1)} %copy-done.2, bf16[192,512]{1,0:T(8,128)(2,1)S(1)} %get-tuple-element.39.c0_hbm, bf16[192,512]{1,0:T(8,128)(2,1)S(1)} %collective-permute-done.11.c1_hbm, ...), custom_call_target="tpu_custom_call" | custom-call | flops 1000 | bytes 1000 | tf_op jit(solution)/shard_map/pallas_call | solution.py:159
  72.7 1.6 %collective-permute-start.21 = (bf16[128,512]{1,0:T(8,128)(2,1)S(1)}, bf16[128,512]{1,0:T(8,128)(2,1)S(1)}, u32[]{:S(2)}, u32[]{:S(2)}) collective-permute-start(bf16[128,512]{1,0:T(8,128)(2,1)S(1)} %add_convert_fusion.3), channel_id=1, source_target_pairs={{0,16},{4,20},{8,24},{12,28},{16,0},{20,4},{24,8},{28,12},{1,17},{... | collective-permute-start | bytes 393224 | tf_op jit(solution)/shard_map/ppermute | solution.py:423
  74.3 1.3 %collective-permute-start.22 = (bf16[128,512]{1,0:T(8,128)(2,1)S(1)}, bf16[128,512]{1,0:T(8,128)(2,1)S(1)}, u32[]{:S(2)}, u32[]{:S(2)}) collective-permute-start(bf16[128,512]{1,0:T(8,128)(2,1)S(1)} %add_convert_fusion.3), channel_id=1, source_target_pairs={{0,24},{4,28},{8,16},{12,20},{16,8},{20,12},{24,0},{28,4},{1,25},{... | collective-permute-start | bytes 393224 | tf_op jit(solution)/shard_map/ppermute | solution.py:423
  75.6 1.5 %collective-permute-start.17 = (bf16[4,64,512]{2,1,0:T(8,128)(2,1)S(1)}, bf16[4,64,512]{2,1,0:T(8,128)(2,1)S(1)}, u32[]{:S(2)}, u32[]{:S(2)}) collective-permute-start(bf16[4,64,512]{2,1,0:T(8,128)(2,1)S(1)} %broadcast_select_fusion), channel_id=1, source_target_pairs={{0,16},{4,12},{8,24},{12,4},{16,0},{20,28},{24,8},{28,20},{1,17},{... | collective-permute-start | bytes 786440 | tf_op jit(solution)/shard_map/ppermute | solution.py:540
  77.2 1.4 %collective-permute-done.6.a2_hbm = bf16[192,256]{1,0:T(8,128)(2,1)S(1)} collective-permute-done((bf16[192,256]{1,0:T(8,128)(2,1)S(1)}, bf16[192,256]{1,0:T(8,128)(2,1)S(1)}, u32[]{:S(2)}, u32[]{:S(2)}) %collective-permute-start.6) | collective-permute-done | bytes 98336 | tf_op jit(solution)/shard_map/ppermute | solution.py:419
  78.6 1.2 %collective-permute-start.25 = (bf16[128,512]{1,0:T(8,128)(2,1)S(1)}, bf16[128,512]{1,0:T(8,128)(2,1)S(1)}, u32[]{:S(2)}, u32[]{:S(2)}) collective-permute-start(bf16[128,512]{1,0:T(8,128)(2,1)S(1)} %add_convert_fusion.1), channel_id=1, source_target_pairs={{0,8},{4,12},{8,0},{12,4},{16,24},{20,28},{24,16},{28,20},{1,9},{5... | collective-permute-start | bytes 393224 | tf_op jit(solution)/shard_map/ppermute | solution.py:423
  79.8 2.1 %collective-permute-start.26 = (bf16[128,512]{1,0:T(8,128)(2,1)S(1)}, bf16[128,512]{1,0:T(8,128)(2,1)S(1)}, u32[]{:S(2)}, u32[]{:S(2)}) collective-permute-start(bf16[128,512]{1,0:T(8,128)(2,1)S(1)} %add_convert_fusion.1), channel_id=1, source_target_pairs={{0,16},{4,20},{8,24},{12,28},{16,0},{20,4},{24,8},{28,12},{1,17},{... | collective-permute-start | bytes 393224 | tf_op jit(solution)/shard_map/ppermute | solution.py:423
  81.9 1.0 %collective-permute-start.27 = (bf16[128,512]{1,0:T(8,128)(2,1)S(1)}, bf16[128,512]{1,0:T(8,128)(2,1)S(1)}, u32[]{:S(2)}, u32[]{:S(2)}) collective-permute-start(bf16[128,512]{1,0:T(8,128)(2,1)S(1)} %add_convert_fusion.1), channel_id=1, source_target_pairs={{0,24},{4,28},{8,16},{12,20},{16,8},{20,12},{24,0},{28,4},{1,25},{... | collective-permute-start | bytes 393224 | tf_op jit(solution)/shard_map/ppermute | solution.py:423
  82.9 2.1 %collective-permute-done.25 = bf16[128,512]{1,0:T(8,128)(2,1)S(1)} collective-permute-done((bf16[128,512]{1,0:T(8,128)(2,1)S(1)}, bf16[128,512]{1,0:T(8,128)(2,1)S(1)}, u32[]{:S(2)}, u32[]{:S(2)}) %collective-permute-start.25) | collective-permute-done | bytes 131104 | tf_op jit(solution)/shard_map/ppermute | solution.py:423
  85.0 1.9 %collective-permute-start.5 = (bf16[192,256]{1,0:T(8,128)(2,1)S(1)}, bf16[192,256]{1,0:T(8,128)(2,1)S(1)}, u32[]{:S(2)}, u32[]{:S(2)}) collective-permute-start(bf16[192,256]{1,0:T(8,128)(2,1)S(1)} %copy-done.15), channel_id=1, source_target_pairs={{0,1},{1,0},{2,3},{3,2},{4,5},{5,4},{6,7},{7,6},{8,9},{9,8},{10,11... | collective-permute-start | bytes 294920 | tf_op jit(solution)/shard_map/ppermute | solution.py:419
  87.3 1.3 %collective-permute-start.14 = (bf16[4,64,512]{2,1,0:T(8,128)(2,1)S(1)}, bf16[4,64,512]{2,1,0:T(8,128)(2,1)S(1)}, u32[]{:S(2)}, u32[]{:S(2)}) collective-permute-start(bf16[4,64,512]{2,1,0:T(8,128)(2,1)S(1)} %collective-permute-done.13.refs_2_), channel_id=1, source_target_pairs={{0,4},{4,0},{8,12},{12,8},{16,20},{20,16},{24,28},{28,24},{1,5},{5... | collective-permute-start | bytes 786440 | tf_op jit(solution)/shard_map/ppermute | solution.py:423
  91.1 3.0 %shard_map.127 = bf16[192,1024]{1,0:T(8,128)(2,1)} custom-call(s32[1]{0:T(128)} %bitcast.clip_ref, s32[1]{0:T(128)} %bitcast.8.count_ref, bf16[192,1024]{1,0:T(8,128)(2,1)S(1)} %copy-done.7, bf16[768,256]{1,0:T(8,128)(2,1)S(1)} %copy-done.2, bf16[192,256]{1,0:T(8,128)(2,1)S(1)} %collective-permute-done.5.a1_hbm, ...), custom_call_target="tpu_custom_call" | custom-call | flops 1000 | bytes 1000 | tf_op jit(solution)/shard_map/pallas_call | solution.py:159
  94.2 1.1 %shard_map.130 = f32[256,1024]{1,0:T(8,128)} custom-call(s32[1]{0:T(128)} %bitcast.6.core_ref, bf16[128,512]{1,0:T(8,128)(2,1)S(1)} %add_convert_fusion.2.refs_0_, bf16[128,512]{1,0:T(8,128)(2,1)S(1)} %collective-permute-done.23.refs_1_, bf16[128,512]{1,0:T(8,128)(2,1)S(1)} %add_convert_fusion.refs_2_, bf16[128,512]{1,0:T(8,128)(2,1)S(1)} %collective-permute-done.28.refs_3_), custom_call_target="tpu_custom_call" | custom-call | flops 1000 | bytes 1000 | tf_op jit(solution)/shard_map/pallas_call | solution.py:159
  (78 shorter events, 9.7 us)
Async XLA Ops:
  2.9 12.1 %collective-permute-start = (bf16[208,512]{1,0:T(8,128)(2,1)S(1)}, bf16[208,512]{1,0:T(8,128)(2,1)S(1)}, u32[]{:S(2)}, u32[]{:S(2)}) collective-permute-start(bf16[208,512]{1,0:T(8,128)(2,1)S(1)} %shard_map.122.p0_hbm), channel_id=1, source_target_pairs={{0,1},{1,0},{2,3},{3,2},{4,5},{5,4},{6,7},{7,6},{8,9},{9,8},{10,11... | collective-permute-start | bytes 638984 | tf_op jit(solution)/shard_map/ppermute | solution.py:419
  6.0 18.2 %collective-permute-start.1 = (bf16[208,512]{1,0:T(8,128)(2,1)S(1)}, bf16[208,512]{1,0:T(8,128)(2,1)S(1)}, u32[]{:S(2)}, u32[]{:S(2)}) collective-permute-start(bf16[208,512]{1,0:T(8,128)(2,1)S(1)} %shard_map.122.p0_hbm), channel_id=1, source_target_pairs={{0,2},{1,3},{2,0},{3,1},{4,6},{5,7},{6,4},{7,5},{8,10},{9,11},{10,... | collective-permute-start | bytes 638984 | tf_op jit(solution)/shard_map/ppermute | solution.py:419
  8.6 16.4 %collective-permute-start.2 = (bf16[208,512]{1,0:T(8,128)(2,1)S(1)}, bf16[208,512]{1,0:T(8,128)(2,1)S(1)}, u32[]{:S(2)}, u32[]{:S(2)}) collective-permute-start(bf16[208,512]{1,0:T(8,128)(2,1)S(1)} %shard_map.122.p0_hbm), channel_id=1, source_target_pairs={{0,3},{1,2},{2,1},{3,0},{4,7},{5,6},{6,5},{7,4},{8,11},{9,10},{10,... | collective-permute-start | bytes 638984 | tf_op jit(solution)/shard_map/ppermute | solution.py:419
  15.7 26.4 %collective-permute-start.8 = (bf16[256,512]{1,0:T(8,128)(2,1)S(1)}, bf16[256,512]{1,0:T(8,128)(2,1)S(1)}, u32[]{:S(2)}, u32[]{:S(2)}) collective-permute-start(bf16[256,512]{1,0:T(8,128)(2,1)S(1)} %get-tuple-element.38.refs_0_.c0_hbm), channel_id=1, source_target_pairs={{0,1},{1,0},{2,3},{3,2},{4,5},{5,4},{6,7},{7,6},{8,9},{9,8},{10,11... | collective-permute-start | bytes 786440 | tf_op jit(solution)/shard_map/ppermute | solution.py:419
  25.7 20.9 %collective-permute-start.10 = (bf16[256,512]{1,0:T(8,128)(2,1)S(1)}, bf16[256,512]{1,0:T(8,128)(2,1)S(1)}, u32[]{:S(2)}, u32[]{:S(2)}) collective-permute-start(bf16[256,512]{1,0:T(8,128)(2,1)S(1)} %get-tuple-element.38.refs_0_.c0_hbm), channel_id=1, source_target_pairs={{0,3},{1,2},{2,1},{3,0},{4,7},{5,6},{6,5},{7,4},{8,11},{9,10},{10,... | collective-permute-start | bytes 786440 | tf_op jit(solution)/shard_map/ppermute | solution.py:419
  28.1 31.3 %collective-permute-start.9 = (bf16[256,512]{1,0:T(8,128)(2,1)S(1)}, bf16[256,512]{1,0:T(8,128)(2,1)}, u32[]{:S(2)}, u32[]{:S(2)}) collective-permute-start(bf16[256,512]{1,0:T(8,128)(2,1)S(1)} %get-tuple-element.38.refs_0_.c0_hbm), channel_id=1, source_target_pairs={{0,2},{1,3},{2,0},{3,1},{4,6},{5,7},{6,4},{7,5},{8,10},{9,11},{10,... | collective-permute-start | bytes 786440 | tf_op jit(solution)/shard_map/ppermute | solution.py:419
  42.1 21.4 %collective-permute-start.3 = (bf16[192,512]{1,0:T(8,128)(2,1)S(1)}, bf16[192,512]{1,0:T(8,128)(2,1)S(1)}, u32[]{:S(2)}, u32[]{:S(2)}) collective-permute-start(bf16[192,512]{1,0:T(8,128)(2,1)S(1)} %get-tuple-element.39.c0_hbm), channel_id=1, source_target_pairs={{0,2},{1,3},{2,0},{3,1},{4,6},{5,7},{6,4},{7,5},{8,10},{9,11},{10,... | collective-permute-start | bytes 589832 | tf_op jit(solution)/shard_map/ppermute | solution.py:419
  42.2 21.3 %collective-permute-start.11 = (bf16[192,512]{1,0:T(8,128)(2,1)S(1)}, bf16[192,512]{1,0:T(8,128)(2,1)S(1)}, u32[]{:S(2)}, u32[]{:S(2)}) collective-permute-start(bf16[192,512]{1,0:T(8,128)(2,1)S(1)} %get-tuple-element.39.c0_hbm), channel_id=1, source_target_pairs={{0,1},{1,0},{2,3},{3,2},{4,5},{5,4},{6,7},{7,6},{8,9},{9,8},{10,11... | collective-permute-start | bytes 589832 | tf_op jit(solution)/shard_map/ppermute | solution.py:419
  45.6 20.9 %collective-permute-start.4 = (bf16[192,512]{1,0:T(8,128)(2,1)S(1)}, bf16[192,512]{1,0:T(8,128)(2,1)S(1)}, u32[]{:S(2)}, u32[]{:S(2)}) collective-permute-start(bf16[192,512]{1,0:T(8,128)(2,1)S(1)} %get-tuple-element.39.c0_hbm), channel_id=1, source_target_pairs={{0,3},{1,2},{2,1},{3,0},{4,7},{5,6},{6,5},{7,4},{8,11},{9,10},{10,... | collective-permute-start | bytes 589832 | tf_op jit(solution)/shard_map/ppermute | solution.py:419
  60.4 10.8 %copy-start.2 = (bf16[768,256]{1,0:T(8,128)(2,1)S(1)}, bf16[768,256]{1,0:T(8,128)(2,1)}, u32[]{:S(2)}) copy-start(bf16[768,256]{1,0:T(8,128)(2,1)} %get-tuple-element.26.a0_hbm.a_ref) | copy-start | bytes 1179652
  62.3 7.3 %collective-permute-start.19 = (bf16[128,512]{1,0:T(8,128)(2,1)S(1)}, bf16[128,512]{1,0:T(8,128)(2,1)S(1)}, u32[]{:S(2)}, u32[]{:S(2)}) collective-permute-start(bf16[128,512]{1,0:T(8,128)(2,1)S(1)} %get-tuple-element.44), channel_id=1, source_target_pairs={{0,4},{4,0},{8,12},{12,8},{16,20},{20,16},{24,28},{28,24},{1,5},{5... | collective-permute-start | bytes 393224 | tf_op jit(solution)/shard_map/ppermute | solution.py:423
  63.5 9.2 %collective-permute-start.13 = (bf16[4,64,512]{2,1,0:T(8,128)(2,1)S(1)}, bf16[4,64,512]{2,1,0:T(8,128)(2,1)S(1)}, u32[]{:S(2)}, u32[]{:S(2)}) collective-permute-start(bf16[4,64,512]{2,1,0:T(8,128)(2,1)S(1)} %shard_map.126.refs_0_), channel_id=1, source_target_pairs={{0,8},{4,12},{8,0},{12,4},{16,24},{20,28},{24,16},{28,20},{1,9},{5... | collective-permute-start | bytes 786440 | tf_op jit(solution)/shard_map/ppermute | solution.py:423
  65.0 9.3 %collective-permute-start.15 = (bf16[4,64,512]{2,1,0:T(8,128)(2,1)S(1)}, bf16[4,64,512]{2,1,0:T(8,128)(2,1)S(1)}, u32[]{:S(2)}, u32[]{:S(2)}) collective-permute-start(bf16[4,64,512]{2,1,0:T(8,128)(2,1)S(1)} %shard_map.126.refs_0_), channel_id=1, source_target_pairs={{0,16},{4,20},{8,24},{12,28},{16,0},{20,4},{24,8},{28,12},{1,17},{... | collective-permute-start | bytes 786440 | tf_op jit(solution)/shard_map/ppermute | solution.py:423
  66.5 7.8 %collective-permute-start.7 = (bf16[192,256]{1,0:T(8,128)(2,1)S(1)}, bf16[192,256]{1,0:T(8,128)(2,1)S(1)}, u32[]{:S(2)}, u32[]{:S(2)}) collective-permute-start(bf16[192,256]{1,0:T(8,128)(2,1)S(1)} %copy-done.17), channel_id=1, source_target_pairs={{0,3},{1,2},{2,1},{3,0},{4,7},{5,6},{6,5},{7,4},{8,11},{9,10},{10,... | collective-permute-start | bytes 294920 | tf_op jit(solution)/shard_map/ppermute | solution.py:419
  68.3 10.3 %collective-permute-start.6 = (bf16[192,256]{1,0:T(8,128)(2,1)S(1)}, bf16[192,256]{1,0:T(8,128)(2,1)S(1)}, u32[]{:S(2)}, u32[]{:S(2)}) collective-permute-start(bf16[192,256]{1,0:T(8,128)(2,1)S(1)} %copy-done.16), channel_id=1, source_target_pairs={{0,2},{1,3},{2,0},{3,1},{4,6},{5,7},{6,4},{7,5},{8,10},{9,11},{10,... | collective-permute-start | bytes 294920 | tf_op jit(solution)/shard_map/ppermute | solution.py:419
  69.7 15.4 %copy-start.15 = (bf16[192,256]{1,0:T(8,128)(2,1)S(1)}, bf16[192,256]{1,0:T(8,128)(2,1)}, u32[]{:S(2)}) copy-start(bf16[192,256]{1,0:T(8,128)(2,1)} %get-tuple-element.30) | copy-start | bytes 294916
  69.7 21.5 %copy-start.7 = (bf16[192,1024]{1,0:T(8,128)(2,1)S(1)}, bf16[192,1024]{1,0:T(8,128)(2,1)}, u32[]{:S(2)}) copy-start(bf16[192,1024]{1,0:T(8,128)(2,1)} %get-tuple-element.25.hidden_hbm) | copy-start | bytes 1179652
  69.7 8.9 %collective-permute-start.20 = (bf16[128,512]{1,0:T(8,128)(2,1)S(1)}, bf16[128,512]{1,0:T(8,128)(2,1)S(1)}, u32[]{:S(2)}, u32[]{:S(2)}) collective-permute-start(bf16[128,512]{1,0:T(8,128)(2,1)S(1)} %add_convert_fusion.3), channel_id=1, source_target_pairs={{0,8},{4,12},{8,0},{12,4},{16,24},{20,28},{24,16},{28,20},{1,9},{5... | collective-permute-start | bytes 393224 | tf_op jit(solution)/shard_map/ppermute | solution.py:423
  72.7 7.1 %collective-permute-start.21 = (bf16[128,512]{1,0:T(8,128)(2,1)S(1)}, bf16[128,512]{1,0:T(8,128)(2,1)S(1)}, u32[]{:S(2)}, u32[]{:S(2)}) collective-permute-start(bf16[128,512]{1,0:T(8,128)(2,1)S(1)} %add_convert_fusion.3), channel_id=1, source_target_pairs={{0,16},{4,20},{8,24},{12,28},{16,0},{20,4},{24,8},{28,12},{1,17},{... | collective-permute-start | bytes 393224 | tf_op jit(solution)/shard_map/ppermute | solution.py:423
  74.3 1.3 %collective-permute-start.24 = (bf16[128,512]{1,0:T(8,128)(2,1)S(1)}, bf16[128,512]{1,0:T(8,128)(2,1)S(1)}, u32[]{:S(2)}, u32[]{:S(2)}) collective-permute-start(bf16[128,512]{1,0:T(8,128)(2,1)S(1)} %get-tuple-element.46), channel_id=1, source_target_pairs={{0,4},{4,0},{8,12},{12,8},{16,20},{20,16},{24,28},{28,24},{1,5},{5... | collective-permute-start | bytes 393224 | tf_op jit(solution)/shard_map/ppermute | solution.py:423
  74.3 7.5 %collective-permute-start.22 = (bf16[128,512]{1,0:T(8,128)(2,1)S(1)}, bf16[128,512]{1,0:T(8,128)(2,1)S(1)}, u32[]{:S(2)}, u32[]{:S(2)}) collective-permute-start(bf16[128,512]{1,0:T(8,128)(2,1)S(1)} %add_convert_fusion.3), channel_id=1, source_target_pairs={{0,24},{4,28},{8,16},{12,20},{16,8},{20,12},{24,0},{28,4},{1,25},{... | collective-permute-start | bytes 393224 | tf_op jit(solution)/shard_map/ppermute | solution.py:423
  75.6 13.8 %collective-permute-start.17 = (bf16[4,64,512]{2,1,0:T(8,128)(2,1)S(1)}, bf16[4,64,512]{2,1,0:T(8,128)(2,1)S(1)}, u32[]{:S(2)}, u32[]{:S(2)}) collective-permute-start(bf16[4,64,512]{2,1,0:T(8,128)(2,1)S(1)} %broadcast_select_fusion), channel_id=1, source_target_pairs={{0,16},{4,12},{8,24},{12,4},{16,0},{20,28},{24,8},{28,20},{1,17},{... | collective-permute-start | bytes 786440 | tf_op jit(solution)/shard_map/ppermute | solution.py:540
  78.6 12.0 %collective-permute-start.12 = (bf16[4,64,512]{2,1,0:T(8,128)(2,1)S(1)}, bf16[4,64,512]{2,1,0:T(8,128)(2,1)S(1)}, u32[]{:S(2)}, u32[]{:S(2)}) collective-permute-start(bf16[4,64,512]{2,1,0:T(8,128)(2,1)S(1)} %shard_map.126.refs_0_), channel_id=1, source_target_pairs={{0,4},{4,0},{8,12},{12,8},{16,20},{20,16},{24,28},{28,24},{1,5},{5... | collective-permute-start | bytes 786440 | tf_op jit(solution)/shard_map/ppermute | solution.py:423
  78.6 6.4 %collective-permute-start.25 = (bf16[128,512]{1,0:T(8,128)(2,1)S(1)}, bf16[128,512]{1,0:T(8,128)(2,1)S(1)}, u32[]{:S(2)}, u32[]{:S(2)}) collective-permute-start(bf16[128,512]{1,0:T(8,128)(2,1)S(1)} %add_convert_fusion.1), channel_id=1, source_target_pairs={{0,8},{4,12},{8,0},{12,4},{16,24},{20,28},{24,16},{28,20},{1,9},{5... | collective-permute-start | bytes 393224 | tf_op jit(solution)/shard_map/ppermute | solution.py:423
  79.8 7.5 %collective-permute-start.26 = (bf16[128,512]{1,0:T(8,128)(2,1)S(1)}, bf16[128,512]{1,0:T(8,128)(2,1)S(1)}, u32[]{:S(2)}, u32[]{:S(2)}) collective-permute-start(bf16[128,512]{1,0:T(8,128)(2,1)S(1)} %add_convert_fusion.1), channel_id=1, source_target_pairs={{0,16},{4,20},{8,24},{12,28},{16,0},{20,4},{24,8},{28,12},{1,17},{... | collective-permute-start | bytes 393224 | tf_op jit(solution)/shard_map/ppermute | solution.py:423
  81.9 7.3 %collective-permute-start.27 = (bf16[128,512]{1,0:T(8,128)(2,1)S(1)}, bf16[128,512]{1,0:T(8,128)(2,1)S(1)}, u32[]{:S(2)}, u32[]{:S(2)}) collective-permute-start(bf16[128,512]{1,0:T(8,128)(2,1)S(1)} %add_convert_fusion.1), channel_id=1, source_target_pairs={{0,24},{4,28},{8,16},{12,20},{16,8},{20,12},{24,0},{28,4},{1,25},{... | collective-permute-start | bytes 393224 | tf_op jit(solution)/shard_map/ppermute | solution.py:423
  85.0 4.8 %collective-permute-start.5 = (bf16[192,256]{1,0:T(8,128)(2,1)S(1)}, bf16[192,256]{1,0:T(8,128)(2,1)S(1)}, u32[]{:S(2)}, u32[]{:S(2)}) collective-permute-start(bf16[192,256]{1,0:T(8,128)(2,1)S(1)} %copy-done.15), channel_id=1, source_target_pairs={{0,1},{1,0},{2,3},{3,2},{4,5},{5,4},{6,7},{7,6},{8,9},{9,8},{10,11... | collective-permute-start | bytes 294920 | tf_op jit(solution)/shard_map/ppermute | solution.py:419
  87.3 3.3 %collective-permute-start.14 = (bf16[4,64,512]{2,1,0:T(8,128)(2,1)S(1)}, bf16[4,64,512]{2,1,0:T(8,128)(2,1)S(1)}, u32[]{:S(2)}, u32[]{:S(2)}) collective-permute-start(bf16[4,64,512]{2,1,0:T(8,128)(2,1)S(1)} %collective-permute-done.13.refs_2_), channel_id=1, source_target_pairs={{0,4},{4,0},{8,12},{12,8},{16,20},{20,16},{24,28},{28,24},{1,5},{5... | collective-permute-start | bytes 786440 | tf_op jit(solution)/shard_map/ppermute | solution.py:423
  89.2 1.5 %collective-permute-start.16 = (bf16[4,64,512]{2,1,0:T(8,128)(2,1)S(1)}, bf16[4,64,512]{2,1,0:T(8,128)(2,1)S(1)}, u32[]{:S(2)}, u32[]{:S(2)}) collective-permute-start(bf16[4,64,512]{2,1,0:T(8,128)(2,1)S(1)} %collective-permute-done.15.refs_4_), channel_id=1, source_target_pairs={{0,4},{4,0},{8,12},{12,8},{16,20},{20,16},{24,28},{28,24},{1,5},{5... | collective-permute-start | bytes 786440 | tf_op jit(solution)/shard_map/ppermute | solution.py:423
  89.5 1.6 %collective-permute-start.18 = (bf16[4,64,512]{2,1,0:T(8,128)(2,1)S(1)}, bf16[4,64,512]{2,1,0:T(8,128)(2,1)S(1)}, u32[]{:S(2)}, u32[]{:S(2)}) collective-permute-start(bf16[4,64,512]{2,1,0:T(8,128)(2,1)S(1)} %collective-permute-done.17.refs_6_), channel_id=1, source_target_pairs={{0,4},{4,0},{8,12},{12,8},{16,20},{20,16},{24,28},{28,24},{1,5},{5... | collective-permute-start | bytes 786440 | tf_op jit(solution)/shard_map/ppermute | solution.py:423
  89.8 4.3 %collective-permute-start.23 = (bf16[128,512]{1,0:T(8,128)(2,1)S(1)}, bf16[128,512]{1,0:T(8,128)(2,1)S(1)}, u32[]{:S(2)}, u32[]{:S(2)}) collective-permute-start(bf16[128,512]{1,0:T(8,128)(2,1)S(1)} %add_convert_fusion.2.refs_0_), channel_id=1, source_target_pairs={{0,4},{4,0},{8,12},{12,8},{16,20},{20,16},{24,28},{28,24},{1,5},{5... | collective-permute-start | bytes 393224 | tf_op jit(solution)/shard_map/ppermute | solution.py:423
  90.6 3.6 %collective-permute-start.28 = (bf16[128,512]{1,0:T(8,128)(2,1)S(1)}, bf16[128,512]{1,0:T(8,128)(2,1)S(1)}, u32[]{:S(2)}, u32[]{:S(2)}) collective-permute-start(bf16[128,512]{1,0:T(8,128)(2,1)S(1)} %add_convert_fusion.refs_2_), channel_id=1, source_target_pairs={{0,4},{4,0},{8,12},{12,8},{16,20},{20,16},{24,28},{28,24},{1,5},{5... | collective-permute-start | bytes 393224 | tf_op jit(solution)/shard_map/ppermute | solution.py:423
  (15 other events, 57.9 us)

commit v5 on v4

--- a/solution.py
+++ b/solution.py
@@ -379,13 +379,7 @@
         copies[-1].start()
 
     for m in range(8):
-        for k in range(4):
-            start = pl.multiple_of(k * group + jnp.bitwise_xor(clip, m) * piece, piece)
-            for side in range(2):
-                move(
-                    held[m].at[k, side * piece : (side + 1) * piece],
-                    w_all.at[pl.ds(start, piece), side * half : (side + 1) * half],
-                )
+        move(held[m], w_all.at[:, jnp.bitwise_xor(clip, m)])
     move(hidden_hbm, hidden)
     move(a0_hbm.at[0:rows], heads.at[:, 0:group])
     for k, source in enumerate((a1_hbm, a2_hbm, a3_hbm)):
@@ -393,7 +387,16 @@
     for copy in copies:
         copy.wait()
     slot = lax.broadcasted_iota(jnp.int32, (rows, 1), 0)
-    projected = jnp.dot(heads[...], w_all[...], preferred_element_type=F32)
+    depth = 32 * piece
+    sides = [
+        jnp.dot(
+            heads[...],
+            w_all[:, :, side * piece : (side + 1) * piece, :].reshape(depth, half),
+            preferred_element_type=F32,
+        )
+        for side in range(2)
+    ]
+    projected = jnp.concatenate(sides, axis=1)
     total = hidden[...].astype(F32) + projected
     out[...] = jnp.where(slot < count_ref[0], total, 0.0).astype(BF16)
     write = pltpu.make_async_copy(out, out_hbm, sems.at[0])
@@ -554,9 +557,9 @@
         scratch=[
             VMEM((rows, width), BF16),
             VMEM((rows, width), BF16),
-            VMEM((width, width), BF16),
+            VMEM((4, 8, extra, half), BF16),
             VMEM((rows, width), BF16),
-            dma((69,)),
+            dma((13,)),
         ],
         limit=10,
     )

time: 95.8 us -> 94.6 us (0.987)
  Pallas kernels: 18.5 us -> 17.4 us
    pallas_call x9, Pallas kernels: 18.5 us -> 17.4 us  [local_call(): pl.pallas_call(kernel, out_shape=out_shape, in_specs=specs, out_specs=[pl...]
  transfers between devices with their start and end apart: 29 -> 29, of which waited for: 10 -> 10; matrix products, arithmetic and copies ran while one was open for 1% -> 2% of each run, Pallas kernels for 18% -> 17%
where the time goes in v5:
time: 94.6 us; the launch traced here: 94.1 us
  starting transfers between devices  37.8 us (40%)
  waiting for transfers between devices  28.7 us (30%)
  Pallas kernels  17.4 us (18%)
  local copies, waits for them, and re-layouts  8.47 us (9%)
  between operations  1.5 us (2%)
    ppermute x12, waiting for transfers between devices, along_tm(): return lax.ppermute(array, 'tm', [(i, i ^ flip) for i in range(4)])  25 us
    ppermute x12, starting transfers between devices, along_tm(): return lax.ppermute(array, 'tm', [(i, i ^ flip) for i in range(4)])  22 us
    pallas_call x9, Pallas kernels, local_call(): pl.pallas_call(kernel, out_shape=out_shape, in_specs=specs, out_specs=[pl...  17.4 us
    ppermute x16, starting transfers between devices, along_clip(): return lax.ppermute(array, 'clip', [(i, i ^ flip) for i in range(8)])  14.4 us
    unnamed x36, local copies, waits for them, and re-layouts  7.28 us
    ppermute x16, waiting for transfers between devices, along_clip(): return lax.ppermute(array, 'clip', [(i, i ^ flip) for i in range(8)])  3.68 us
  transfers between devices with their start and end apart: 29, of which 10 were waited for; matrix products, arithmetic and copies ran while one was open for 2% of the time, Pallas kernels for 17%

profile of v5, /device:TPU:0, one launch (start us, length us, event | category | flops | bytes accessed | tf_op | source)
XLA Modules:
  0.0 94.1 jit_solution(14587207749738357068)
XLA Ops:
  2.9 3.1 %collective-permute-start = (bf16[208,512]{1,0:T(8,128)(2,1)S(1)}, bf16[208,512]{1,0:T(8,128)(2,1)S(1)}, u32[]{:S(2)}, u32[]{:S(2)}) collective-permute-start(bf16[208,512]{1,0:T(8,128)(2,1)S(1)} %shard_map.122.p0_hbm), channel_id=1, source_target_pairs={{0,1},{1,0},{2,3},{3,2},{4,5},{5,4},{6,7},{7,6},{8,9},{9,8},{10,11... | collective-permute-start | bytes 638984 | tf_op jit(solution)/shard_map/ppermute | solution.py:422
  6.0 2.6 %collective-permute-start.1 = (bf16[208,512]{1,0:T(8,128)(2,1)S(1)}, bf16[208,512]{1,0:T(8,128)(2,1)S(1)}, u32[]{:S(2)}, u32[]{:S(2)}) collective-permute-start(bf16[208,512]{1,0:T(8,128)(2,1)S(1)} %shard_map.122.p0_hbm), channel_id=1, source_target_pairs={{0,2},{1,3},{2,0},{3,1},{4,6},{5,7},{6,4},{7,5},{8,10},{9,11},{10,... | collective-permute-start | bytes 638984 | tf_op jit(solution)/shard_map/ppermute | solution.py:422
  8.6 1.4 %copy-done.3 = bf16[1024,768]{1,0:T(8,128)(2,1)S(1)} copy-done((bf16[1024,768]{1,0:T(8,128)(2,1)S(1)}, bf16[1024,768]{1,0:T(8,128)(2,1)}, u32[]{:S(2)}) %copy-start.3) | copy-done | bytes 1572888
  10.6 1.2 %copy-done = bf16[1024,768]{1,0:T(8,128)(2,1)} copy-done((bf16[1024,768]{1,0:T(8,128)(2,1)}, bf16[1024,768]{1,0:T(8,128)(2,1)S(1)}, u32[]{:S(2)}) %copy-start) | copy-done | bytes 1572888
  13.0 2.1 %collective-permute-done.p1_hbm = bf16[208,512]{1,0:T(8,128)(2,1)S(1)} collective-permute-done((bf16[208,512]{1,0:T(8,128)(2,1)S(1)}, bf16[208,512]{1,0:T(8,128)(2,1)S(1)}, u32[]{:S(2)}, u32[]{:S(2)}) %collective-permute-start) | collective-permute-done | bytes 213024 | tf_op jit(solution)/shard_map/ppermute | solution.py:422
  15.7 8.5 %collective-permute-done.1.p2_hbm = bf16[208,512]{1,0:T(8,128)(2,1)S(1)} collective-permute-done((bf16[208,512]{1,0:T(8,128)(2,1)S(1)}, bf16[208,512]{1,0:T(8,128)(2,1)S(1)}, u32[]{:S(2)}, u32[]{:S(2)}) %collective-permute-start.1) | collective-permute-done | bytes 213024 | tf_op jit(solution)/shard_map/ppermute | solution.py:422
  25.7 2.5 %collective-permute-start.10 = (bf16[256,512]{1,0:T(8,128)(2,1)S(1)}, bf16[256,512]{1,0:T(8,128)(2,1)S(1)}, u32[]{:S(2)}, u32[]{:S(2)}) collective-permute-start(bf16[256,512]{1,0:T(8,128)(2,1)S(1)} %get-tuple-element.38.refs_0_.c0_hbm), channel_id=1, source_target_pairs={{0,3},{1,2},{2,1},{3,0},{4,7},{5,6},{6,5},{7,4},{8,11},{9,10},{10,... | collective-permute-start | bytes 786440 | tf_op jit(solution)/shard_map/ppermute | solution.py:422
  28.1 4.4 %collective-permute-start.9 = (bf16[256,512]{1,0:T(8,128)(2,1)S(1)}, bf16[256,512]{1,0:T(8,128)(2,1)}, u32[]{:S(2)}, u32[]{:S(2)}) collective-permute-start(bf16[256,512]{1,0:T(8,128)(2,1)S(1)} %get-tuple-element.38.refs_0_.c0_hbm), channel_id=1, source_target_pairs={{0,2},{1,3},{2,0},{3,1},{4,6},{5,7},{6,4},{7,5},{8,10},{9,11},{10,... | collective-permute-start | bytes 786440 | tf_op jit(solution)/shard_map/ppermute | solution.py:422
  32.6 9.5 %shard_map.124 = (bf16[768,256]{1,0:T(8,128)(2,1)}, bf16[192,256]{1,0:T(8,128)(2,1)}, bf16[192,256]{1,0:T(8,128)(2,1)}, bf16[192,256]{1,0:T(8,128)(2,1)}, bf16[192,1024]{1,0:T(8,128)(2,1)}) custom-call(s32[1]{0:T(128)} %bitcast.2.bin_ref, bf16[208,512]{1,0:T(8,128)(2,1)} %copy-done.4, bf16[208,512]{1,0:T(8,128)(2,1)} %copy-done.10, ...), custom_call_target="tpu_custom_call" | custom-call | flops 1000 | bytes 100000000 | tf_op jit(solution)/shard_map/pallas_call | solution.py:159
  42.2 3.5 %collective-permute-start.11 = (bf16[192,512]{1,0:T(8,128)(2,1)S(1)}, bf16[192,512]{1,0:T(8,128)(2,1)S(1)}, u32[]{:S(2)}, u32[]{:S(2)}) collective-permute-start(bf16[192,512]{1,0:T(8,128)(2,1)S(1)} %get-tuple-element.39.c0_hbm), channel_id=1, source_target_pairs={{0,1},{1,0},{2,3},{3,2},{4,5},{5,4},{6,7},{7,6},{8,9},{9,8},{10,11... | collective-permute-start | bytes 589832 | tf_op jit(solution)/shard_map/ppermute | solution.py:422
  46.5 12.9 %collective-permute-done.9.refs_2_.c2_hbm = bf16[256,512]{1,0:T(8,128)(2,1)} collective-permute-done((bf16[256,512]{1,0:T(8,128)(2,1)S(1)}, bf16[256,512]{1,0:T(8,128)(2,1)}, u32[]{:S(2)}, u32[]{:S(2)}) %collective-permute-start.9) | collective-permute-done | bytes 262176 | tf_op jit(solution)/shard_map/ppermute | solution.py:422
  59.4 1.0 %copy-done.1 = bf16[768,256]{1,0:T(8,128)(2,1)S(1)} copy-done((bf16[768,256]{1,0:T(8,128)(2,1)S(1)}, bf16[768,256]{1,0:T(8,128)(2,1)}, u32[]{:S(2)}) %copy-start.1) | copy-done | bytes 393240
  60.4 1.9 %shard_map.128 = (bf16[128,512]{1,0:T(8,128)(2,1)S(1)}, bf16[128,512]{1,0:T(8,128)(2,1)S(1)}) custom-call(s32[1]{0:T(128)} %bitcast.6.core_ref, bf16[768,256]{1,0:T(8,128)(2,1)S(1)} %copy-done.1, bf16[256,512]{1,0:T(8,128)(2,1)S(1)} %get-tuple-element.38.refs_0_.c0_hbm, bf16[256,512]{1,0:T(8,128)(2,1)S(1)} %collective-permute-done.8.refs_1_.c1_hbm, ...), custom_call_target="tpu_custom_call" | custom-call | flops 1000 | bytes 1000 | tf_op jit(solution)/shard_map/pallas_call | solution.py:159
  62.4 1.0 %shard_map.126.refs_0_ = bf16[4,64,512]{2,1,0:T(8,128)(2,1)S(1)} custom-call(bf16[256,512]{1,0:T(8,128)(2,1)S(1)} %get-tuple-element.38.refs_0_.c0_hbm, bf16[256,512]{1,0:T(8,128)(2,1)S(1)} %collective-permute-done.8.refs_1_.c1_hbm, bf16[256,512]{1,0:T(8,128)(2,1)} %collective-permute-done.9.refs_2_.c2_hbm, ...), custom_call_target="tpu_custom_call" | custom-call | flops 1000 | bytes 1000 | tf_op jit(solution)/shard_map/pallas_call | solution.py:159
  63.5 1.5 %collective-permute-start.13 = (bf16[4,64,512]{2,1,0:T(8,128)(2,1)S(1)}, bf16[4,64,512]{2,1,0:T(8,128)(2,1)S(1)}, u32[]{:S(2)}, u32[]{:S(2)}) collective-permute-start(bf16[4,64,512]{2,1,0:T(8,128)(2,1)S(1)} %shard_map.126.refs_0_), channel_id=1, source_target_pairs={{0,8},{4,12},{8,0},{12,4},{16,24},{20,28},{24,16},{28,20},{1,9},{5... | collective-permute-start | bytes 786440 | tf_op jit(solution)/shard_map/ppermute | solution.py:426
  65.0 1.5 %collective-permute-start.15 = (bf16[4,64,512]{2,1,0:T(8,128)(2,1)S(1)}, bf16[4,64,512]{2,1,0:T(8,128)(2,1)S(1)}, u32[]{:S(2)}, u32[]{:S(2)}) collective-permute-start(bf16[4,64,512]{2,1,0:T(8,128)(2,1)S(1)} %shard_map.126.refs_0_), channel_id=1, source_target_pairs={{0,16},{4,20},{8,24},{12,28},{16,0},{20,4},{24,8},{28,12},{1,17},{... | collective-permute-start | bytes 786440 | tf_op jit(solution)/shard_map/ppermute | solution.py:426
  66.5 1.8 %collective-permute-start.7 = (bf16[192,256]{1,0:T(8,128)(2,1)S(1)}, bf16[192,256]{1,0:T(8,128)(2,1)S(1)}, u32[]{:S(2)}, u32[]{:S(2)}) collective-permute-start(bf16[192,256]{1,0:T(8,128)(2,1)S(1)} %copy-done.17), channel_id=1, source_target_pairs={{0,3},{1,2},{2,1},{3,0},{4,7},{5,6},{6,5},{7,4},{8,11},{9,10},{10,... | collective-permute-start | bytes 294920 | tf_op jit(solution)/shard_map/ppermute | solution.py:422
  68.3 1.3 %collective-permute-start.6 = (bf16[192,256]{1,0:T(8,128)(2,1)S(1)}, bf16[192,256]{1,0:T(8,128)(2,1)S(1)}, u32[]{:S(2)}, u32[]{:S(2)}) collective-permute-start(bf16[192,256]{1,0:T(8,128)(2,1)S(1)} %copy-done.16), channel_id=1, source_target_pairs={{0,2},{1,3},{2,0},{3,1},{4,6},{5,7},{6,4},{7,5},{8,10},{9,11},{10,... | collective-permute-start | bytes 294920 | tf_op jit(solution)/shard_map/ppermute | solution.py:422
  69.7 1.6 %collective-permute-start.20 = (bf16[128,512]{1,0:T(8,128)(2,1)S(1)}, bf16[128,512]{1,0:T(8,128)(2,1)S(1)}, u32[]{:S(2)}, u32[]{:S(2)}) collective-permute-start(bf16[128,512]{1,0:T(8,128)(2,1)S(1)} %add_convert_fusion.3), channel_id=1, source_target_pairs={{0,8},{4,12},{8,0},{12,4},{16,24},{20,28},{24,16},{28,20},{1,9},{5... | collective-permute-start | bytes 393224 | tf_op jit(solution)/shard_map/ppermute | solution.py:426
  71.2 1.5 %shard_map.129 = (bf16[128,512]{1,0:T(8,128)(2,1)S(1)}, bf16[128,512]{1,0:T(8,128)(2,1)S(1)}) custom-call(s32[1]{0:T(128)} %bitcast.6.core_ref, bf16[768,256]{1,0:T(8,128)(2,1)S(1)} %copy-done.2, bf16[192,512]{1,0:T(8,128)(2,1)S(1)} %get-tuple-element.39.c0_hbm, bf16[192,512]{1,0:T(8,128)(2,1)S(1)} %collective-permute-done.11.c1_hbm, ...), custom_call_target="tpu_custom_call" | custom-call | flops 1000 | bytes 1000 | tf_op jit(solution)/shard_map/pallas_call | solution.py:159
  72.7 1.6 %collective-permute-start.21 = (bf16[128,512]{1,0:T(8,128)(2,1)S(1)}, bf16[128,512]{1,0:T(8,128)(2,1)S(1)}, u32[]{:S(2)}, u32[]{:S(2)}) collective-permute-start(bf16[128,512]{1,0:T(8,128)(2,1)S(1)} %add_convert_fusion.3), channel_id=1, source_target_pairs={{0,16},{4,20},{8,24},{12,28},{16,0},{20,4},{24,8},{28,12},{1,17},{... | collective-permute-start | bytes 393224 | tf_op jit(solution)/shard_map/ppermute | solution.py:426
  74.3 1.3 %collective-permute-start.22 = (bf16[128,512]{1,0:T(8,128)(2,1)S(1)}, bf16[128,512]{1,0:T(8,128)(2,1)S(1)}, u32[]{:S(2)}, u32[]{:S(2)}) collective-permute-start(bf16[128,512]{1,0:T(8,128)(2,1)S(1)} %add_convert_fusion.3), channel_id=1, source_target_pairs={{0,24},{4,28},{8,16},{12,20},{16,8},{20,12},{24,0},{28,4},{1,25},{... | collective-permute-start | bytes 393224 | tf_op jit(solution)/shard_map/ppermute | solution.py:426
  75.6 1.5 %collective-permute-start.17 = (bf16[4,64,512]{2,1,0:T(8,128)(2,1)S(1)}, bf16[4,64,512]{2,1,0:T(8,128)(2,1)S(1)}, u32[]{:S(2)}, u32[]{:S(2)}) collective-permute-start(bf16[4,64,512]{2,1,0:T(8,128)(2,1)S(1)} %broadcast_select_fusion), channel_id=1, source_target_pairs={{0,16},{4,12},{8,24},{12,4},{16,0},{20,28},{24,8},{28,20},{1,17},{... | collective-permute-start | bytes 786440 | tf_op jit(solution)/shard_map/ppermute | solution.py:543
  77.2 1.4 %collective-permute-done.6.a2_hbm = bf16[192,256]{1,0:T(8,128)(2,1)S(1)} collective-permute-done((bf16[192,256]{1,0:T(8,128)(2,1)S(1)}, bf16[192,256]{1,0:T(8,128)(2,1)S(1)}, u32[]{:S(2)}, u32[]{:S(2)}) %collective-permute-start.6) | collective-permute-done | bytes 98336 | tf_op jit(solution)/shard_map/ppermute | solution.py:422
  78.6 1.2 %collective-permute-start.25 = (bf16[128,512]{1,0:T(8,128)(2,1)S(1)}, bf16[128,512]{1,0:T(8,128)(2,1)S(1)}, u32[]{:S(2)}, u32[]{:S(2)}) collective-permute-start(bf16[128,512]{1,0:T(8,128)(2,1)S(1)} %add_convert_fusion.1), channel_id=1, source_target_pairs={{0,8},{4,12},{8,0},{12,4},{16,24},{20,28},{24,16},{28,20},{1,9},{5... | collective-permute-start | bytes 393224 | tf_op jit(solution)/shard_map/ppermute | solution.py:426
  79.8 2.1 %collective-permute-start.26 = (bf16[128,512]{1,0:T(8,128)(2,1)S(1)}, bf16[128,512]{1,0:T(8,128)(2,1)S(1)}, u32[]{:S(2)}, u32[]{:S(2)}) collective-permute-start(bf16[128,512]{1,0:T(8,128)(2,1)S(1)} %add_convert_fusion.1), channel_id=1, source_target_pairs={{0,16},{4,20},{8,24},{12,28},{16,0},{20,4},{24,8},{28,12},{1,17},{... | collective-permute-start | bytes 393224 | tf_op jit(solution)/shard_map/ppermute | solution.py:426
  81.9 1.0 %collective-permute-start.27 = (bf16[128,512]{1,0:T(8,128)(2,1)S(1)}, bf16[128,512]{1,0:T(8,128)(2,1)S(1)}, u32[]{:S(2)}, u32[]{:S(2)}) collective-permute-start(bf16[128,512]{1,0:T(8,128)(2,1)S(1)} %add_convert_fusion.1), channel_id=1, source_target_pairs={{0,24},{4,28},{8,16},{12,20},{16,8},{20,12},{24,0},{28,4},{1,25},{... | collective-permute-start | bytes 393224 | tf_op jit(solution)/shard_map/ppermute | solution.py:426
  82.9 2.1 %collective-permute-done.25 = bf16[128,512]{1,0:T(8,128)(2,1)S(1)} collective-permute-done((bf16[128,512]{1,0:T(8,128)(2,1)S(1)}, bf16[128,512]{1,0:T(8,128)(2,1)S(1)}, u32[]{:S(2)}, u32[]{:S(2)}) %collective-permute-start.25) | collective-permute-done | bytes 131104 | tf_op jit(solution)/shard_map/ppermute | solution.py:426
  85.0 1.9 %collective-permute-start.5 = (bf16[192,256]{1,0:T(8,128)(2,1)S(1)}, bf16[192,256]{1,0:T(8,128)(2,1)S(1)}, u32[]{:S(2)}, u32[]{:S(2)}) collective-permute-start(bf16[192,256]{1,0:T(8,128)(2,1)S(1)} %copy-done.15), channel_id=1, source_target_pairs={{0,1},{1,0},{2,3},{3,2},{4,5},{5,4},{6,7},{7,6},{8,9},{9,8},{10,11... | collective-permute-start | bytes 294920 | tf_op jit(solution)/shard_map/ppermute | solution.py:422
  87.3 1.3 %collective-permute-start.14 = (bf16[4,64,512]{2,1,0:T(8,128)(2,1)S(1)}, bf16[4,64,512]{2,1,0:T(8,128)(2,1)S(1)}, u32[]{:S(2)}, u32[]{:S(2)}) collective-permute-start(bf16[4,64,512]{2,1,0:T(8,128)(2,1)S(1)} %collective-permute-done.13.refs_2_), channel_id=1, source_target_pairs={{0,4},{4,0},{8,12},{12,8},{16,20},{20,16},{24,28},{28,24},{1,5},{5... | collective-permute-start | bytes 786440 | tf_op jit(solution)/shard_map/ppermute | solution.py:426
  91.1 1.9 %shard_map.127 = bf16[192,1024]{1,0:T(8,128)(2,1)} custom-call(s32[1]{0:T(128)} %bitcast.clip_ref, s32[1]{0:T(128)} %bitcast.8.count_ref, bf16[192,1024]{1,0:T(8,128)(2,1)S(1)} %copy-done.7, bf16[768,256]{1,0:T(8,128)(2,1)S(1)} %copy-done.2, bf16[192,256]{1,0:T(8,128)(2,1)S(1)} %collective-permute-done.5.a1_hbm, ...), custom_call_target="tpu_custom_call" | custom-call | flops 1000 | bytes 1000 | tf_op jit(solution)/shard_map/pallas_call | solution.py:159
  93.0 1.1 %shard_map.130 = f32[256,1024]{1,0:T(8,128)} custom-call(s32[1]{0:T(128)} %bitcast.6.core_ref, bf16[128,512]{1,0:T(8,128)(2,1)S(1)} %add_convert_fusion.2.refs_0_, bf16[128,512]{1,0:T(8,128)(2,1)S(1)} %collective-permute-done.23.refs_1_, bf16[128,512]{1,0:T(8,128)(2,1)S(1)} %add_convert_fusion.refs_2_, bf16[128,512]{1,0:T(8,128)(2,1)S(1)} %collective-permute-done.28.refs_3_), custom_call_target="tpu_custom_call" | custom-call | flops 1000 | bytes 1000 | tf_op jit(solution)/shard_map/pallas_call | solution.py:159
  (78 shorter events, 9.7 us)
Async XLA Ops:
  2.9 12.1 %collective-permute-start = (bf16[208,512]{1,0:T(8,128)(2,1)S(1)}, bf16[208,512]{1,0:T(8,128)(2,1)S(1)}, u32[]{:S(2)}, u32[]{:S(2)}) collective-permute-start(bf16[208,512]{1,0:T(8,128)(2,1)S(1)} %shard_map.122.p0_hbm), channel_id=1, source_target_pairs={{0,1},{1,0},{2,3},{3,2},{4,5},{5,4},{6,7},{7,6},{8,9},{9,8},{10,11... | collective-permute-start | bytes 638984 | tf_op jit(solution)/shard_map/ppermute | solution.py:422
  6.0 18.2 %collective-permute-start.1 = (bf16[208,512]{1,0:T(8,128)(2,1)S(1)}, bf16[208,512]{1,0:T(8,128)(2,1)S(1)}, u32[]{:S(2)}, u32[]{:S(2)}) collective-permute-start(bf16[208,512]{1,0:T(8,128)(2,1)S(1)} %shard_map.122.p0_hbm), channel_id=1, source_target_pairs={{0,2},{1,3},{2,0},{3,1},{4,6},{5,7},{6,4},{7,5},{8,10},{9,11},{10,... | collective-permute-start | bytes 638984 | tf_op jit(solution)/shard_map/ppermute | solution.py:422
  8.6 16.4 %collective-permute-start.2 = (bf16[208,512]{1,0:T(8,128)(2,1)S(1)}, bf16[208,512]{1,0:T(8,128)(2,1)S(1)}, u32[]{:S(2)}, u32[]{:S(2)}) collective-permute-start(bf16[208,512]{1,0:T(8,128)(2,1)S(1)} %shard_map.122.p0_hbm), channel_id=1, source_target_pairs={{0,3},{1,2},{2,1},{3,0},{4,7},{5,6},{6,5},{7,4},{8,11},{9,10},{10,... | collective-permute-start | bytes 638984 | tf_op jit(solution)/shard_map/ppermute | solution.py:422
  15.7 26.4 %collective-permute-start.8 = (bf16[256,512]{1,0:T(8,128)(2,1)S(1)}, bf16[256,512]{1,0:T(8,128)(2,1)S(1)}, u32[]{:S(2)}, u32[]{:S(2)}) collective-permute-start(bf16[256,512]{1,0:T(8,128)(2,1)S(1)} %get-tuple-element.38.refs_0_.c0_hbm), channel_id=1, source_target_pairs={{0,1},{1,0},{2,3},{3,2},{4,5},{5,4},{6,7},{7,6},{8,9},{9,8},{10,11... | collective-permute-start | bytes 786440 | tf_op jit(solution)/shard_map/ppermute | solution.py:422
  25.7 20.9 %collective-permute-start.10 = (bf16[256,512]{1,0:T(8,128)(2,1)S(1)}, bf16[256,512]{1,0:T(8,128)(2,1)S(1)}, u32[]{:S(2)}, u32[]{:S(2)}) collective-permute-start(bf16[256,512]{1,0:T(8,128)(2,1)S(1)} %get-tuple-element.38.refs_0_.c0_hbm), channel_id=1, source_target_pairs={{0,3},{1,2},{2,1},{3,0},{4,7},{5,6},{6,5},{7,4},{8,11},{9,10},{10,... | collective-permute-start | bytes 786440 | tf_op jit(solution)/shard_map/ppermute | solution.py:422
  28.1 31.3 %collective-permute-start.9 = (bf16[256,512]{1,0:T(8,128)(2,1)S(1)}, bf16[256,512]{1,0:T(8,128)(2,1)}, u32[]{:S(2)}, u32[]{:S(2)}) collective-permute-start(bf16[256,512]{1,0:T(8,128)(2,1)S(1)} %get-tuple-element.38.refs_0_.c0_hbm), channel_id=1, source_target_pairs={{0,2},{1,3},{2,0},{3,1},{4,6},{5,7},{6,4},{7,5},{8,10},{9,11},{10,... | collective-permute-start | bytes 786440 | tf_op jit(solution)/shard_map/ppermute | solution.py:422
  42.1 21.4 %collective-permute-start.3 = (bf16[192,512]{1,0:T(8,128)(2,1)S(1)}, bf16[192,512]{1,0:T(8,128)(2,1)S(1)}, u32[]{:S(2)}, u32[]{:S(2)}) collective-permute-start(bf16[192,512]{1,0:T(8,128)(2,1)S(1)} %get-tuple-element.39.c0_hbm), channel_id=1, source_target_pairs={{0,2},{1,3},{2,0},{3,1},{4,6},{5,7},{6,4},{7,5},{8,10},{9,11},{10,... | collective-permute-start | bytes 589832 | tf_op jit(solution)/shard_map/ppermute | solution.py:422
  42.2 21.3 %collective-permute-start.11 = (bf16[192,512]{1,0:T(8,128)(2,1)S(1)}, bf16[192,512]{1,0:T(8,128)(2,1)S(1)}, u32[]{:S(2)}, u32[]{:S(2)}) collective-permute-start(bf16[192,512]{1,0:T(8,128)(2,1)S(1)} %get-tuple-element.39.c0_hbm), channel_id=1, source_target_pairs={{0,1},{1,0},{2,3},{3,2},{4,5},{5,4},{6,7},{7,6},{8,9},{9,8},{10,11... | collective-permute-start | bytes 589832 | tf_op jit(solution)/shard_map/ppermute | solution.py:422
  45.6 20.9 %collective-permute-start.4 = (bf16[192,512]{1,0:T(8,128)(2,1)S(1)}, bf16[192,512]{1,0:T(8,128)(2,1)S(1)}, u32[]{:S(2)}, u32[]{:S(2)}) collective-permute-start(bf16[192,512]{1,0:T(8,128)(2,1)S(1)} %get-tuple-element.39.c0_hbm), channel_id=1, source_target_pairs={{0,3},{1,2},{2,1},{3,0},{4,7},{5,6},{6,5},{7,4},{8,11},{9,10},{10,... | collective-permute-start | bytes 589832 | tf_op jit(solution)/shard_map/ppermute | solution.py:422
  60.4 10.8 %copy-start.2 = (bf16[768,256]{1,0:T(8,128)(2,1)S(1)}, bf16[768,256]{1,0:T(8,128)(2,1)}, u32[]{:S(2)}) copy-start(bf16[768,256]{1,0:T(8,128)(2,1)} %get-tuple-element.26.a0_hbm.a_ref) | copy-start | bytes 1179652
  62.3 7.3 %collective-permute-start.19 = (bf16[128,512]{1,0:T(8,128)(2,1)S(1)}, bf16[128,512]{1,0:T(8,128)(2,1)S(1)}, u32[]{:S(2)}, u32[]{:S(2)}) collective-permute-start(bf16[128,512]{1,0:T(8,128)(2,1)S(1)} %get-tuple-element.44), channel_id=1, source_target_pairs={{0,4},{4,0},{8,12},{12,8},{16,20},{20,16},{24,28},{28,24},{1,5},{5... | collective-permute-start | bytes 393224 | tf_op jit(solution)/shard_map/ppermute | solution.py:426
  63.5 9.2 %collective-permute-start.13 = (bf16[4,64,512]{2,1,0:T(8,128)(2,1)S(1)}, bf16[4,64,512]{2,1,0:T(8,128)(2,1)S(1)}, u32[]{:S(2)}, u32[]{:S(2)}) collective-permute-start(bf16[4,64,512]{2,1,0:T(8,128)(2,1)S(1)} %shard_map.126.refs_0_), channel_id=1, source_target_pairs={{0,8},{4,12},{8,0},{12,4},{16,24},{20,28},{24,16},{28,20},{1,9},{5... | collective-permute-start | bytes 786440 | tf_op jit(solution)/shard_map/ppermute | solution.py:426
  65.0 9.3 %collective-permute-start.15 = (bf16[4,64,512]{2,1,0:T(8,128)(2,1)S(1)}, bf16[4,64,512]{2,1,0:T(8,128)(2,1)S(1)}, u32[]{:S(2)}, u32[]{:S(2)}) collective-permute-start(bf16[4,64,512]{2,1,0:T(8,128)(2,1)S(1)} %shard_map.126.refs_0_), channel_id=1, source_target_pairs={{0,16},{4,20},{8,24},{12,28},{16,0},{20,4},{24,8},{28,12},{1,17},{... | collective-permute-start | bytes 786440 | tf_op jit(solution)/shard_map/ppermute | solution.py:426
  66.5 7.8 %collective-permute-start.7 = (bf16[192,256]{1,0:T(8,128)(2,1)S(1)}, bf16[192,256]{1,0:T(8,128)(2,1)S(1)}, u32[]{:S(2)}, u32[]{:S(2)}) collective-permute-start(bf16[192,256]{1,0:T(8,128)(2,1)S(1)} %copy-done.17), channel_id=1, source_target_pairs={{0,3},{1,2},{2,1},{3,0},{4,7},{5,6},{6,5},{7,4},{8,11},{9,10},{10,... | collective-permute-start | bytes 294920 | tf_op jit(solution)/shard_map/ppermute | solution.py:422
  68.3 10.3 %collective-permute-start.6 = (bf16[192,256]{1,0:T(8,128)(2,1)S(1)}, bf16[192,256]{1,0:T(8,128)(2,1)S(1)}, u32[]{:S(2)}, u32[]{:S(2)}) collective-permute-start(bf16[192,256]{1,0:T(8,128)(2,1)S(1)} %copy-done.16), channel_id=1, source_target_pairs={{0,2},{1,3},{2,0},{3,1},{4,6},{5,7},{6,4},{7,5},{8,10},{9,11},{10,... | collective-permute-start | bytes 294920 | tf_op jit(solution)/shard_map/ppermute | solution.py:422
  69.7 15.4 %copy-start.15 = (bf16[192,256]{1,0:T(8,128)(2,1)S(1)}, bf16[192,256]{1,0:T(8,128)(2,1)}, u32[]{:S(2)}) copy-start(bf16[192,256]{1,0:T(8,128)(2,1)} %get-tuple-element.30) | copy-start | bytes 294916
  69.7 21.5 %copy-start.7 = (bf16[192,1024]{1,0:T(8,128)(2,1)S(1)}, bf16[192,1024]{1,0:T(8,128)(2,1)}, u32[]{:S(2)}) copy-start(bf16[192,1024]{1,0:T(8,128)(2,1)} %get-tuple-element.25.hidden_hbm) | copy-start | bytes 1179652
  69.7 8.9 %collective-permute-start.20 = (bf16[128,512]{1,0:T(8,128)(2,1)S(1)}, bf16[128,512]{1,0:T(8,128)(2,1)S(1)}, u32[]{:S(2)}, u32[]{:S(2)}) collective-permute-start(bf16[128,512]{1,0:T(8,128)(2,1)S(1)} %add_convert_fusion.3), channel_id=1, source_target_pairs={{0,8},{4,12},{8,0},{12,4},{16,24},{20,28},{24,16},{28,20},{1,9},{5... | collective-permute-start | bytes 393224 | tf_op jit(solution)/shard_map/ppermute | solution.py:426
  72.7 7.1 %collective-permute-start.21 = (bf16[128,512]{1,0:T(8,128)(2,1)S(1)}, bf16[128,512]{1,0:T(8,128)(2,1)S(1)}, u32[]{:S(2)}, u32[]{:S(2)}) collective-permute-start(bf16[128,512]{1,0:T(8,128)(2,1)S(1)} %add_convert_fusion.3), channel_id=1, source_target_pairs={{0,16},{4,20},{8,24},{12,28},{16,0},{20,4},{24,8},{28,12},{1,17},{... | collective-permute-start | bytes 393224 | tf_op jit(solution)/shard_map/ppermute | solution.py:426
  74.3 1.3 %collective-permute-start.24 = (bf16[128,512]{1,0:T(8,128)(2,1)S(1)}, bf16[128,512]{1,0:T(8,128)(2,1)S(1)}, u32[]{:S(2)}, u32[]{:S(2)}) collective-permute-start(bf16[128,512]{1,0:T(8,128)(2,1)S(1)} %get-tuple-element.46), channel_id=1, source_target_pairs={{0,4},{4,0},{8,12},{12,8},{16,20},{20,16},{24,28},{28,24},{1,5},{5... | collective-permute-start | bytes 393224 | tf_op jit(solution)/shard_map/ppermute | solution.py:426
  74.3 7.5 %collective-permute-start.22 = (bf16[128,512]{1,0:T(8,128)(2,1)S(1)}, bf16[128,512]{1,0:T(8,128)(2,1)S(1)}, u32[]{:S(2)}, u32[]{:S(2)}) collective-permute-start(bf16[128,512]{1,0:T(8,128)(2,1)S(1)} %add_convert_fusion.3), channel_id=1, source_target_pairs={{0,24},{4,28},{8,16},{12,20},{16,8},{20,12},{24,0},{28,4},{1,25},{... | collective-permute-start | bytes 393224 | tf_op jit(solution)/shard_map/ppermute | solution.py:426
  75.6 13.8 %collective-permute-start.17 = (bf16[4,64,512]{2,1,0:T(8,128)(2,1)S(1)}, bf16[4,64,512]{2,1,0:T(8,128)(2,1)S(1)}, u32[]{:S(2)}, u32[]{:S(2)}) collective-permute-start(bf16[4,64,512]{2,1,0:T(8,128)(2,1)S(1)} %broadcast_select_fusion), channel_id=1, source_target_pairs={{0,16},{4,12},{8,24},{12,4},{16,0},{20,28},{24,8},{28,20},{1,17},{... | collective-permute-start | bytes 786440 | tf_op jit(solution)/shard_map/ppermute | solution.py:543
  78.6 12.0 %collective-permute-start.12 = (bf16[4,64,512]{2,1,0:T(8,128)(2,1)S(1)}, bf16[4,64,512]{2,1,0:T(8,128)(2,1)S(1)}, u32[]{:S(2)}, u32[]{:S(2)}) collective-permute-start(bf16[4,64,512]{2,1,0:T(8,128)(2,1)S(1)} %shard_map.126.refs_0_), channel_id=1, source_target_pairs={{0,4},{4,0},{8,12},{12,8},{16,20},{20,16},{24,28},{28,24},{1,5},{5... | collective-permute-start | bytes 786440 | tf_op jit(solution)/shard_map/ppermute | solution.py:426
  78.6 6.4 %collective-permute-start.25 = (bf16[128,512]{1,0:T(8,128)(2,1)S(1)}, bf16[128,512]{1,0:T(8,128)(2,1)S(1)}, u32[]{:S(2)}, u32[]{:S(2)}) collective-permute-start(bf16[128,512]{1,0:T(8,128)(2,1)S(1)} %add_convert_fusion.1), channel_id=1, source_target_pairs={{0,8},{4,12},{8,0},{12,4},{16,24},{20,28},{24,16},{28,20},{1,9},{5... | collective-permute-start | bytes 393224 | tf_op jit(solution)/shard_map/ppermute | solution.py:426
  79.8 7.5 %collective-permute-start.26 = (bf16[128,512]{1,0:T(8,128)(2,1)S(1)}, bf16[128,512]{1,0:T(8,128)(2,1)S(1)}, u32[]{:S(2)}, u32[]{:S(2)}) collective-permute-start(bf16[128,512]{1,0:T(8,128)(2,1)S(1)} %add_convert_fusion.1), channel_id=1, source_target_pairs={{0,16},{4,20},{8,24},{12,28},{16,0},{20,4},{24,8},{28,12},{1,17},{... | collective-permute-start | bytes 393224 | tf_op jit(solution)/shard_map/ppermute | solution.py:426
  81.9 7.3 %collective-permute-start.27 = (bf16[128,512]{1,0:T(8,128)(2,1)S(1)}, bf16[128,512]{1,0:T(8,128)(2,1)S(1)}, u32[]{:S(2)}, u32[]{:S(2)}) collective-permute-start(bf16[128,512]{1,0:T(8,128)(2,1)S(1)} %add_convert_fusion.1), channel_id=1, source_target_pairs={{0,24},{4,28},{8,16},{12,20},{16,8},{20,12},{24,0},{28,4},{1,25},{... | collective-permute-start | bytes 393224 | tf_op jit(solution)/shard_map/ppermute | solution.py:426
  85.0 4.8 %collective-permute-start.5 = (bf16[192,256]{1,0:T(8,128)(2,1)S(1)}, bf16[192,256]{1,0:T(8,128)(2,1)S(1)}, u32[]{:S(2)}, u32[]{:S(2)}) collective-permute-start(bf16[192,256]{1,0:T(8,128)(2,1)S(1)} %copy-done.15), channel_id=1, source_target_pairs={{0,1},{1,0},{2,3},{3,2},{4,5},{5,4},{6,7},{7,6},{8,9},{9,8},{10,11... | collective-permute-start | bytes 294920 | tf_op jit(solution)/shard_map/ppermute | solution.py:422
  87.3 3.3 %collective-permute-start.14 = (bf16[4,64,512]{2,1,0:T(8,128)(2,1)S(1)}, bf16[4,64,512]{2,1,0:T(8,128)(2,1)S(1)}, u32[]{:S(2)}, u32[]{:S(2)}) collective-permute-start(bf16[4,64,512]{2,1,0:T(8,128)(2,1)S(1)} %collective-permute-done.13.refs_2_), channel_id=1, source_target_pairs={{0,4},{4,0},{8,12},{12,8},{16,20},{20,16},{24,28},{28,24},{1,5},{5... | collective-permute-start | bytes 786440 | tf_op jit(solution)/shard_map/ppermute | solution.py:426
  89.2 1.5 %collective-permute-start.16 = (bf16[4,64,512]{2,1,0:T(8,128)(2,1)S(1)}, bf16[4,64,512]{2,1,0:T(8,128)(2,1)S(1)}, u32[]{:S(2)}, u32[]{:S(2)}) collective-permute-start(bf16[4,64,512]{2,1,0:T(8,128)(2,1)S(1)} %collective-permute-done.15.refs_4_), channel_id=1, source_target_pairs={{0,4},{4,0},{8,12},{12,8},{16,20},{20,16},{24,28},{28,24},{1,5},{5... | collective-permute-start | bytes 786440 | tf_op jit(solution)/shard_map/ppermute | solution.py:426
  89.5 1.6 %collective-permute-start.18 = (bf16[4,64,512]{2,1,0:T(8,128)(2,1)S(1)}, bf16[4,64,512]{2,1,0:T(8,128)(2,1)S(1)}, u32[]{:S(2)}, u32[]{:S(2)}) collective-permute-start(bf16[4,64,512]{2,1,0:T(8,128)(2,1)S(1)} %collective-permute-done.17.refs_6_), channel_id=1, source_target_pairs={{0,4},{4,0},{8,12},{12,8},{16,20},{20,16},{24,28},{28,24},{1,5},{5... | collective-permute-start | bytes 786440 | tf_op jit(solution)/shard_map/ppermute | solution.py:426
  89.8 3.2 %collective-permute-start.23 = (bf16[128,512]{1,0:T(8,128)(2,1)S(1)}, bf16[128,512]{1,0:T(8,128)(2,1)S(1)}, u32[]{:S(2)}, u32[]{:S(2)}) collective-permute-start(bf16[128,512]{1,0:T(8,128)(2,1)S(1)} %add_convert_fusion.2.refs_0_), channel_id=1, source_target_pairs={{0,4},{4,0},{8,12},{12,8},{16,20},{20,16},{24,28},{28,24},{1,5},{5... | collective-permute-start | bytes 393224 | tf_op jit(solution)/shard_map/ppermute | solution.py:426
  90.6 2.4 %collective-permute-start.28 = (bf16[128,512]{1,0:T(8,128)(2,1)S(1)}, bf16[128,512]{1,0:T(8,128)(2,1)S(1)}, u32[]{:S(2)}, u32[]{:S(2)}) collective-permute-start(bf16[128,512]{1,0:T(8,128)(2,1)S(1)} %add_convert_fusion.refs_2_), channel_id=1, source_target_pairs={{0,4},{4,0},{8,12},{12,8},{16,20},{20,16},{24,28},{28,24},{1,5},{5... | collective-permute-start | bytes 393224 | tf_op jit(solution)/shard_map/ppermute | solution.py:426
  (15 other events, 57.9 us)
